TPU v7x, 128 devices: a whole 4x4x4 slice. The times are simulated.
128 devices in a mesh: ctx: 16 (over x, z), head: 8 (over y, core).
Axes of the slice: x: 4, y: 4, z: 4, core: 2. Of those that a mesh axis runs over, the one named last changes fastest.
Arguments:
- activations: bfloat16 [32768, 2304], P('ctx'), may hold values from -6 to 6
- norm_gain: float32 [2304], replicated, may hold values from 0.1 to 1.9
- qkv_weight: bfloat16 [3, 2304, 2048], P(None, None, 'head'), may hold values from -0.125 to 0.125
- conv_weight: bfloat16 [3, 4, 2048], P(None, None, 'head'), may hold values from -3 to 3
- gate_down_matrix: bfloat16 [2304, 128], replicated, may hold values from -0.125 to 0.125
- gate_up: bfloat16 [128, 2048], P(None, 'head'), may hold values from -0.5 to 0.5
- log_forget_gates: float32 [16, 32768, 128], P('head', 'ctx'), may hold values from -0.8 to 0
- step_size: float32 [16, 32768], P('head', 'ctx'), may hold values from 0.02 to 0.1
- out_gain: float32 [2048], P('head'), may hold values from 0.1 to 1.9
- out_weight: bfloat16 [2048, 2304], P('head'), may hold values from -0.1875 to 0.1875
Outputs:
- mixed: bfloat16 [32768, 2304], P('ctx', 'head')
All inputs are finite; a program needn't handle non-finite values.
Results may differ from a plain program's by a relative error of at most 0.014.
Values may be sent and summed in bfloat16 or wider, within the bound.
No kernel may reach another device: no remote copies, remote signals or barrier semaphores. Data moves between devices by JAX's collectives and lax.ppermute only.
A program may use at most 128 MiB of HBM per device.

v0:
```python
import math

import jax
import jax.numpy as jnp
from jax import lax
from jax.sharding import PartitionSpec as P


def passed_along(shard, axis, by):
    size = lax.axis_size(axis)
    pairs = [(i, i + by) for i in range(size) if 0 <= i + by < size]
    return lax.ppermute(shard, axis, pairs)


def unit_rows(field, eps):
    return field * lax.rsqrt(jnp.sum(field * field, axis=-1, keepdims=True) + eps)


def lower_inverse(lower, ident_block, rounds):
    highest = lax.Precision.HIGHEST
    power = -lower
    inverse = jnp.broadcast_to(ident_block, lower.shape)
    for level in range(rounds):
        inverse = inverse + jnp.einsum("hts,hsr->htr", inverse, power, precision=highest)
        if level + 1 < rounds:
            power = jnp.einsum("hts,hsr->htr", power, power, precision=highest)
    return inverse


def body(
    activations,
    norm_gain,
    qkv_weight,
    conv_weight,
    gate_down_matrix,
    gate_up,
    log_forget_gates,
    step_size,
    out_gain,
    out_weight,
):
    highest = lax.Precision.HIGHEST
    tokens = activations.shape[0]
    heads = log_forget_gates.shape[0]
    width = log_forget_gates.shape[2]
    taps = conv_weight.shape[1]
    wide = activations.astype(jnp.float32)
    normed = (
        wide * lax.rsqrt(jnp.mean(wide * wide, axis=-1, keepdims=True) + 1e-06) * norm_gain
    ).astype(jnp.bfloat16)
    projected = jnp.einsum(
        "td,ide->ite", normed, qkv_weight, preferred_element_type=jnp.float32
    ).astype(jnp.bfloat16)
    earlier = passed_along(projected[:, tokens - (taps - 1) :, :], "ctx", 1)
    padded = jnp.concatenate([earlier, projected], axis=1).astype(jnp.float32)
    summed = jnp.zeros(projected.shape, jnp.float32)
    for j in range(taps):
        summed = (
            summed + conv_weight[:, j][:, None, :].astype(jnp.float32) * padded[:, j : j + tokens]
        )
    convolved = jax.nn.silu(summed)
    query = unit_rows(convolved[0].reshape(tokens, heads, width), 1e-06) / jnp.sqrt(
        jnp.float32(width)
    )
    key = unit_rows(convolved[1].reshape(tokens, heads, width), 1e-06)
    value = convolved[2].reshape(tokens, heads, width)
    block = math.gcd(tokens, 128)
    blocks = tokens // block
    rounds = max((block - 1).bit_length(), 1)

    def by_block(field):
        return jnp.transpose(
            jnp.transpose(field, (1, 0, 2)).reshape(heads, blocks, block, width), (1, 0, 2, 3)
        )

    steps_in = (
        by_block(query),
        by_block(key),
        by_block(value),
        jnp.transpose(log_forget_gates.reshape(heads, blocks, block, width), (1, 0, 2, 3)),
        jnp.transpose(step_size.reshape(heads, blocks, block), (1, 0, 2)),
    )
    row_ids = lax.broadcasted_iota(jnp.int32, (block, block), 0)
    col_ids = lax.broadcasted_iota(jnp.int32, (block, block), 1)
    strict = col_ids < row_ids
    inclusive = col_ids <= row_ids
    ident = jnp.eye(width, dtype=jnp.float32)
    ident_block = jnp.eye(block, dtype=jnp.float32)

    def advance(state, inputs):
        q_blk, k_blk, v_blk, g_blk, b_blk = inputs
        cum = jnp.cumsum(g_blk, axis=1)
        rising = jnp.exp(cum)
        descending = jnp.exp(-cum)
        to_end = jnp.exp(cum[:, -1:, :] - cum)
        k_pos = k_blk * rising
        k_neg = k_blk * descending * b_blk[:, :, None]
        q_pos = q_blk * rising
        pairs = jnp.einsum("htc,hsc->hts", k_pos, k_neg, precision=highest)
        lower = jnp.where(strict, pairs, 0.0)
        targets = jnp.concatenate([v_blk, jnp.zeros_like(v_blk)], axis=-1)
        targets = targets - jnp.einsum("htc,hcj->htj", k_pos, state, precision=highest)
        inverse = lower_inverse(lower, ident_block, rounds)
        updates = jnp.einsum("hts,hsj->htj", inverse, targets, precision=highest)
        mixing = jnp.where(
            inclusive, jnp.einsum("htc,hsc->hts", q_pos, k_neg, precision=highest), 0.0
        )
        outs = jnp.einsum("htc,hcj->htj", q_pos, state, precision=highest)
        outs = outs + jnp.einsum("hts,hsj->htj", mixing, updates, precision=highest)
        carried = k_blk * to_end * b_blk[:, :, None]
        state = jnp.exp(cum[:, -1, :])[:, :, None] * state
        state = state + jnp.einsum("hsc,hsj->hcj", carried, updates, precision=highest)
        return (state, outs)

    start = jnp.concatenate(
        [
            jnp.zeros((heads, width, width), jnp.float32),
            jnp.broadcast_to(ident, (heads, width, width)),
        ],
        axis=-1,
    )
    final, outs = lax.scan(advance, start, steps_in)
    outs = jnp.transpose(outs, (1, 0, 2, 3)).reshape(heads, tokens, 2 * width)
    local_out = outs[:, :, :width]
    reading = outs[:, :, width:]
    increment = final[:, :, :width]
    transit = final[:, :, width:]

    def relay(turn, incoming):
        leaving = jnp.einsum("hab,hbc->hac", transit, incoming, precision=highest) + increment
        return passed_along(leaving, "ctx", 1)

    incoming = lax.fori_loop(
        0, lax.axis_size("ctx") - 1, relay, jnp.zeros((heads, width, width), jnp.float32)
    )
    attended = local_out + jnp.einsum("htc,hcj->htj", reading, incoming, precision=highest)
    normalized = attended * lax.rsqrt(jnp.mean(attended * attended, axis=-1, keepdims=True) + 1e-05)
    normalized = normalized * out_gain.reshape(heads, 1, width)
    lowered = jnp.dot(normed, gate_down_matrix, preferred_element_type=jnp.float32).astype(
        jnp.bfloat16
    )
    gate = jnp.dot(lowered, gate_up, preferred_element_type=jnp.float32).reshape(
        tokens, heads, width
    )
    gated = (
        (jnp.transpose(normalized, (1, 0, 2)) * jax.nn.sigmoid(gate))
        .reshape(tokens, heads * width)
        .astype(jnp.bfloat16)
    )
    columns = lax.all_to_all(out_weight, "head", split_axis=1, concat_axis=0, tiled=True)
    mixed = jnp.dot(
        lax.all_gather(gated, "head", axis=1, tiled=True),
        columns,
        preferred_element_type=jnp.float32,
    )
    return mixed.astype(jnp.bfloat16)


def solution(mesh):
    in_specs = (
        P("ctx", None),
        P(),
        P(None, None, "head"),
        P(None, None, "head"),
        P(),
        P(None, "head"),
        P("head", "ctx", None),
        P("head", "ctx"),
        P("head"),
        P("head", None),
    )
    out_specs = P("ctx", "head")
    return jax.shard_map(body, mesh=mesh, in_specs=in_specs, out_specs=out_specs, check_vma=False)
```

profile of v0, /device:TPU:5, one launch (start us, length us, event | category | flops | bytes accessed | tf_op | source)
XLA Modules:
  0.0 528.7 jit_solution(3445733335431108917)
XLA Ops:
  6.5 5.7 %fusion.29 = f32[2048]{0:T(1024)S(1)} fusion(bf16[2048,2304]{1,0:T(8,128)(2,1)} %param.14), kind=kLoop, calls=%fused_computation.48 | loop fusion | flops 14153728 | bytes 9445376 | tf_op jit(solution)/shard_map/reduce_sum | solution.py:49
  12.3 1.7 copy-done.2
  14.0 7.9 %fusion.40 = bf16[3,2048,256]{2,1,0:T(8,128)(2,1)S(1)} fusion(bf16[3,2304,256]{2,1,0:T(8,128)(2,1)S(1)} %copy-done, bf16[2048,2304]{1,0:T(8,128)(2,1)S(1)} %copy-done.2, f32[2304]{0:T(1024)S(1)} %copy-done.10, f32[2048]{0:T(1024)S(1)} %add_rsqrt_fusion.3), kind=kOutput, calls=%fused_computation.63 | convolution fusion | flops 7268204544 | bytes 16139264 | tf_op jit(solution)/shard_map/td,ide->ite/dot_general | solution.py:51
  21.9 1.6 copy-done.4
  24.1 3.5 collective-permute-start.1
  27.7 8.5 %fusion.45 = f32[2048,256]{0,1:T(8,128)} fusion(bf16[128,256]{1,0:T(8,128)(2,1)} %param.19, bf16[2304,128]{1,0:T(8,128)(2,1)} %param.18, bf16[2048,2304]{1,0:T(8,128)(2,1)} %param.14, f32[2304]{0:T(1024)} %param.15, f32[2048]{0:T(1024)} %copy-done.8), kind=kOutput, calls=%fused_computation.68 | convolution fusion | flops 1362886656 | bytes 12207104 | tf_op jit(solution)/shard_map/dot_general | solution.py:142
  36.3 3.3 copy.116
  40.9 3.7 divide_multiply_fusion
  44.7 2.8 fusion.58
  47.5 2.3 reshape_squeeze.11
  49.8 3.5 multiply_reduce_fusion.1
  53.6 1.7 fusion.54
  55.3 2.3 reshape_squeeze.9
  57.6 3.5 multiply_reduce_fusion.2
  61.4 1.7 copy_multiply_fusion.1
  63.2 2.3 reshape_squeeze.10
  65.5 1.5 copy.106
  67.0 236.8 %while.25 = (s32[]{:T(128)}, f32[2,128,256]{2,1,0:T(8,128)S(1)}, f32[16,2,128,256]{3,2,1,0:T(8,128)}, f32[16,2,128,128]{3,2,0,1:T(8,128)}, f32[16,2,128,128]{3,2...) while((s32[]{:T(128)}, f32[2,128,256]{2,1,0:T(8,128)S(1)}, ...), condition=%wide.region_5.6_spmd.clone.clone, body=%wide.region_3.5_spmd.clone.clone.sunk | while | flops 1263534080 | bytes 10828913 | solution.py:122
  68.8 1.4 fusion.197
  83.6 1.4 fusion.197
  98.5 1.4 fusion.197
  113.3 1.4 fusion.197
  128.1 1.4 fusion.197
  142.9 1.4 fusion.197
  157.7 1.4 fusion.197
  187.3 1.4 fusion.197
  276.1 1.4 fusion.197
  290.9 1.4 fusion.197
  303.8 4.6 copy.113
  308.5 124.1 %while.24 = (s32[]{:T(128)}, f32[2,128,128]{2,1,0:T(8,128)S(1)}, f32[2,128,128]{2,1,0:T(8,128)S(1)}, f32[2,128,128]{2,1,0:T(8,128)S(1)}, s32[]{:T(128)}) while((s32[]{:T(128)}, f32[2,128,128]{2,1,0:T(8,128)S(1)}, f32[2,128,128]{2,1,0:T(8,128)S(1)}, f32[2,128,128]{2,1,0:T(8,128)S(1)}, s32[]{:T(128)}) %tuple.55), condition=%wide.region_7.8_spmd, body=%wide.region_6.7_spmd.sunk | while | flops 50364416 | bytes 1048677 | solution.py:133
  308.7 3.7 collective-permute-start
  312.4 4.3 collective-permute-done
  317.0 1.9 collective-permute-start
  318.9 5.9 %collective-permute-done = f32[2,128,128]{2,1,0:T(8,128)S(1)} collective-permute-done((f32[2,128,128]{2,1,0:T(8,128)S(1)}, f32[2,128,128]{2,1,0:T(8,128)S(1)}, u32[]{:S(2)}, u32[]{:S(2)}) %collective-permute-start) | collective-permute-done | bytes 131104 | tf_op jit(solution)/shard_map/while/body/eval_jaxpr/ppermute | solution.py:12
  325.1 1.9 collective-permute-start
  327.0 5.9 %collective-permute-done = f32[2,128,128]{2,1,0:T(8,128)S(1)} collective-permute-done((f32[2,128,128]{2,1,0:T(8,128)S(1)}, f32[2,128,128]{2,1,0:T(8,128)S(1)}, u32[]{:S(2)}, u32[]{:S(2)}) %collective-permute-start) | collective-permute-done | bytes 131104 | tf_op jit(solution)/shard_map/while/body/eval_jaxpr/ppermute | solution.py:12
  333.2 1.9 collective-permute-start
  335.1 5.9 %collective-permute-done = f32[2,128,128]{2,1,0:T(8,128)S(1)} collective-permute-done((f32[2,128,128]{2,1,0:T(8,128)S(1)}, f32[2,128,128]{2,1,0:T(8,128)S(1)}, u32[]{:S(2)}, u32[]{:S(2)}) %collective-permute-start) | collective-permute-done | bytes 131104 | tf_op jit(solution)/shard_map/while/body/eval_jaxpr/ppermute | solution.py:12
  341.3 1.9 collective-permute-start
  343.2 5.9 %collective-permute-done = f32[2,128,128]{2,1,0:T(8,128)S(1)} collective-permute-done((f32[2,128,128]{2,1,0:T(8,128)S(1)}, f32[2,128,128]{2,1,0:T(8,128)S(1)}, u32[]{:S(2)}, u32[]{:S(2)}) %collective-permute-start) | collective-permute-done | bytes 131104 | tf_op jit(solution)/shard_map/while/body/eval_jaxpr/ppermute | solution.py:12
  349.4 1.9 collective-permute-start
  351.3 5.9 %collective-permute-done = f32[2,128,128]{2,1,0:T(8,128)S(1)} collective-permute-done((f32[2,128,128]{2,1,0:T(8,128)S(1)}, f32[2,128,128]{2,1,0:T(8,128)S(1)}, u32[]{:S(2)}, u32[]{:S(2)}) %collective-permute-start) | collective-permute-done | bytes 131104 | tf_op jit(solution)/shard_map/while/body/eval_jaxpr/ppermute | solution.py:12
  357.4 1.9 collective-permute-start
  359.4 6.4 %collective-permute-done = f32[2,128,128]{2,1,0:T(8,128)S(1)} collective-permute-done((f32[2,128,128]{2,1,0:T(8,128)S(1)}, f32[2,128,128]{2,1,0:T(8,128)S(1)}, u32[]{:S(2)}, u32[]{:S(2)}) %collective-permute-start) | collective-permute-done | bytes 131104 | tf_op jit(solution)/shard_map/while/body/eval_jaxpr/ppermute | solution.py:12
  366.0 1.9 collective-permute-start
  367.9 7.4 %collective-permute-done = f32[2,128,128]{2,1,0:T(8,128)S(1)} collective-permute-done((f32[2,128,128]{2,1,0:T(8,128)S(1)}, f32[2,128,128]{2,1,0:T(8,128)S(1)}, u32[]{:S(2)}, u32[]{:S(2)}) %collective-permute-start) | collective-permute-done | bytes 131104 | tf_op jit(solution)/shard_map/while/body/eval_jaxpr/ppermute | solution.py:12
  375.6 1.9 collective-permute-start
  377.5 6.5 %collective-permute-done = f32[2,128,128]{2,1,0:T(8,128)S(1)} collective-permute-done((f32[2,128,128]{2,1,0:T(8,128)S(1)}, f32[2,128,128]{2,1,0:T(8,128)S(1)}, u32[]{:S(2)}, u32[]{:S(2)}) %collective-permute-start) | collective-permute-done | bytes 131104 | tf_op jit(solution)/shard_map/while/body/eval_jaxpr/ppermute | solution.py:12
  384.3 1.9 collective-permute-start
  386.2 5.9 %collective-permute-done = f32[2,128,128]{2,1,0:T(8,128)S(1)} collective-permute-done((f32[2,128,128]{2,1,0:T(8,128)S(1)}, f32[2,128,128]{2,1,0:T(8,128)S(1)}, u32[]{:S(2)}, u32[]{:S(2)}) %collective-permute-start) | collective-permute-done | bytes 131104 | tf_op jit(solution)/shard_map/while/body/eval_jaxpr/ppermute | solution.py:12
  392.4 1.9 collective-permute-start
  394.3 5.9 %collective-permute-done = f32[2,128,128]{2,1,0:T(8,128)S(1)} collective-permute-done((f32[2,128,128]{2,1,0:T(8,128)S(1)}, f32[2,128,128]{2,1,0:T(8,128)S(1)}, u32[]{:S(2)}, u32[]{:S(2)}) %collective-permute-start) | collective-permute-done | bytes 131104 | tf_op jit(solution)/shard_map/while/body/eval_jaxpr/ppermute | solution.py:12
  400.5 1.9 collective-permute-start
  402.4 5.9 %collective-permute-done = f32[2,128,128]{2,1,0:T(8,128)S(1)} collective-permute-done((f32[2,128,128]{2,1,0:T(8,128)S(1)}, f32[2,128,128]{2,1,0:T(8,128)S(1)}, u32[]{:S(2)}, u32[]{:S(2)}) %collective-permute-start) | collective-permute-done | bytes 131104 | tf_op jit(solution)/shard_map/while/body/eval_jaxpr/ppermute | solution.py:12
  408.6 1.9 collective-permute-start
  410.5 5.9 %collective-permute-done = f32[2,128,128]{2,1,0:T(8,128)S(1)} collective-permute-done((f32[2,128,128]{2,1,0:T(8,128)S(1)}, f32[2,128,128]{2,1,0:T(8,128)S(1)}, u32[]{:S(2)}, u32[]{:S(2)}) %collective-permute-start) | collective-permute-done | bytes 131104 | tf_op jit(solution)/shard_map/while/body/eval_jaxpr/ppermute | solution.py:12
  416.7 1.9 collective-permute-start
  418.6 5.9 %collective-permute-done = f32[2,128,128]{2,1,0:T(8,128)S(1)} collective-permute-done((f32[2,128,128]{2,1,0:T(8,128)S(1)}, f32[2,128,128]{2,1,0:T(8,128)S(1)}, u32[]{:S(2)}, u32[]{:S(2)}) %collective-permute-start) | collective-permute-done | bytes 131104 | tf_op jit(solution)/shard_map/while/body/eval_jaxpr/ppermute | solution.py:12
  424.8 1.9 collective-permute-start
  426.7 5.9 %collective-permute-done = f32[2,128,128]{2,1,0:T(8,128)S(1)} collective-permute-done((f32[2,128,128]{2,1,0:T(8,128)S(1)}, f32[2,128,128]{2,1,0:T(8,128)S(1)}, u32[]{:S(2)}, u32[]{:S(2)}) %collective-permute-start) | collective-permute-done | bytes 131104 | tf_op jit(solution)/shard_map/while/body/eval_jaxpr/ppermute | solution.py:12
  432.6 4.7 multiply_reduce_fusion
  440.1 47.3 %all_to_all.19 = bf16[256,8,288]{0,2,1:T(8,128)(2,1)S(1)} all-to-all(bf16[256,8,288]{0,2,1:T(8,128)(2,1)S(1)} %bitcast.227), channel_id=1, replica_groups=mesh['ctx'=16,'head'=8] {'head'}, dimensions={1} | all-to-all | bytes 2359296 | tf_op jit(solution)/shard_map/all_to_all | solution.py:150
  488.6 25.7 %all-gather.2.cloned.1.call-done = bf16[2048,2048]{0,1:T(8,128)(2,1)} async-done(((bf16[2048,256]{0,1:T(8,128)(2,1)}), bf16[2048,2048]{0,1:T(8,128)(2,1)}) %all-gather.2.cloned.1.call-update) | async-done | bytes 8388624 | tf_op jit(solution)/shard_map/all_gather | solution.py:152
  514.3 7.5 %convolution_convert_fusion = bf16[2048,288]{0,1:T(8,128)(2,1)} fusion(bf16[2048,288]{0,1:T(8,128)(2,1)} %bitcast.232, bf16[2048,2048]{0,1:T(8,128)(2,1)} %all-gather.2.cloned.1.call-done), kind=kOutput, calls=%fused_computation.70 | convolution fusion | flops 2416508928 | bytes 10747904 | tf_op jit(solution)/shard_map/dot_general | solution.py:151
  (497 shorter events, 230.1 us)
Async XLA Ops:
  6.5 5.8 %copy-start = (bf16[3,2304,256]{2,1,0:T(8,128)(2,1)S(1)}, bf16[3,2304,256]{2,1,0:T(8,128)(2,1)}, u32[]{:S(2)}) copy-start(bf16[3,2304,256]{2,1,0:T(8,128)(2,1)} %param.16) | copy-start | bytes 10616836
  6.5 5.8 %copy-start.10 = (f32[2304]{0:T(1024)S(1)}, f32[2304]{0:T(1024)}, u32[]{:S(2)}) copy-start(f32[2304]{0:T(1024)} %param.15) | copy-start | bytes 27652
  6.5 507.8 %all-gather.2.cloned.1.call-start = ((), (), s32[]{:S(2)}) async-start(), calls=%async_computation.1 | async-start | bytes 9437184 | tf_op jit(solution)/shard_map/all_gather | solution.py:152
  6.5 7.5 %copy-start.2 = (bf16[2048,2304]{1,0:T(8,128)(2,1)S(1)}, bf16[2048,2304]{1,0:T(8,128)(2,1)}, u32[]{:S(2)}) copy-start(bf16[2048,2304]{1,0:T(8,128)(2,1)} %param.14) | copy-start | bytes 28311556
  14.0 7.9 %copy-start.8 = (f32[2048]{0:T(1024)}, f32[2048]{0:T(1024)S(1)}, u32[]{:S(2)}) copy-start(f32[2048]{0:T(1024)S(1)} %add_rsqrt_fusion.3) | copy-start | bytes 24580
  14.0 13.7 %copy-start.7 = (bf16[3,4,256]{2,1,0:T(4,128)(2,1)S(1)}, bf16[3,4,256]{2,1,0:T(4,128)(2,1)}, u32[]{:S(2)}) copy-start(bf16[3,4,256]{2,1,0:T(4,128)(2,1)} %param.17) | copy-start | bytes 18436
  21.9 1.7 copy-start.4
  24.1 15.5 %collective-permute-start.1 = (bf16[3,3,256]{2,1,0:T(4,128)(2,1)}, bf16[3,3,256]{2,1,0:T(4,128)(2,1)}, u32[]{:S(2)}, u32[]{:S(2)}) collective-permute-start(bf16[3,3,256]{2,1,0:T(4,128)(2,1)} %slice.71), channel_id=1, source_target_pairs={{0,8},{8,16},{16,24},{24,32},{32,40},{40,48},{48,56},{56,64},{64,7... | collective-permute-start | bytes 13832 | tf_op jit(solution)/shard_map/ppermute | solution.py:12
  36.3 3.3 copy-start.5
  308.4 128.8 %copy-start.3 = (f32[2048,2,128]{2,0,1:T(8,128)S(1)}, f32[2048,2,128]{2,0,1:T(8,128)}, u32[]{:S(2)}) copy-start(f32[2048,2,128]{2,0,1:T(8,128)} %copy.116) | copy-start | bytes 6291460
  308.4 128.8 %copy-start.9 = (f32[256]{0:T(256)S(1)}, f32[256]{0:T(256)}, u32[]{:S(2)}) copy-start(f32[256]{0:T(256)} %param.22) | copy-start | bytes 3076
  308.7 8.0 %collective-permute-start = (f32[2,128,128]{2,1,0:T(8,128)S(1)}, f32[2,128,128]{2,1,0:T(8,128)S(1)}, u32[]{:S(2)}, u32[]{:S(2)}) collective-permute-start(f32[2,128,128]{2,1,0:T(8,128)S(1)} %convolution_add_fusion.18), channel_id=1, source_target_pairs={{0,8},{8,16},{16,24},{24,32},{32,40},{40,48},{48,56},{56,64},{64,7... | collective-permute-start | bytes 393224 | tf_op jit(solution)/shard_map/while/body/eval_jaxpr/ppermute | solution.py:12
  317.0 7.8 %collective-permute-start = (f32[2,128,128]{2,1,0:T(8,128)S(1)}, f32[2,128,128]{2,1,0:T(8,128)S(1)}, u32[]{:S(2)}, u32[]{:S(2)}) collective-permute-start(f32[2,128,128]{2,1,0:T(8,128)S(1)} %convolution_add_fusion.18), channel_id=1, source_target_pairs={{0,8},{8,16},{16,24},{24,32},{32,40},{40,48},{48,56},{56,64},{64,7... | collective-permute-start | bytes 393224 | tf_op jit(solution)/shard_map/while/body/eval_jaxpr/ppermute | solution.py:12
  325.1 7.8 %collective-permute-start = (f32[2,128,128]{2,1,0:T(8,128)S(1)}, f32[2,128,128]{2,1,0:T(8,128)S(1)}, u32[]{:S(2)}, u32[]{:S(2)}) collective-permute-start(f32[2,128,128]{2,1,0:T(8,128)S(1)} %convolution_add_fusion.18), channel_id=1, source_target_pairs={{0,8},{8,16},{16,24},{24,32},{32,40},{40,48},{48,56},{56,64},{64,7... | collective-permute-start | bytes 393224 | tf_op jit(solution)/shard_map/while/body/eval_jaxpr/ppermute | solution.py:12
  333.2 7.8 %collective-permute-start = (f32[2,128,128]{2,1,0:T(8,128)S(1)}, f32[2,128,128]{2,1,0:T(8,128)S(1)}, u32[]{:S(2)}, u32[]{:S(2)}) collective-permute-start(f32[2,128,128]{2,1,0:T(8,128)S(1)} %convolution_add_fusion.18), channel_id=1, source_target_pairs={{0,8},{8,16},{16,24},{24,32},{32,40},{40,48},{48,56},{56,64},{64,7... | collective-permute-start | bytes 393224 | tf_op jit(solution)/shard_map/while/body/eval_jaxpr/ppermute | solution.py:12
  341.3 7.8 %collective-permute-start = (f32[2,128,128]{2,1,0:T(8,128)S(1)}, f32[2,128,128]{2,1,0:T(8,128)S(1)}, u32[]{:S(2)}, u32[]{:S(2)}) collective-permute-start(f32[2,128,128]{2,1,0:T(8,128)S(1)} %convolution_add_fusion.18), channel_id=1, source_target_pairs={{0,8},{8,16},{16,24},{24,32},{32,40},{40,48},{48,56},{56,64},{64,7... | collective-permute-start | bytes 393224 | tf_op jit(solution)/shard_map/while/body/eval_jaxpr/ppermute | solution.py:12
  349.4 7.8 %collective-permute-start = (f32[2,128,128]{2,1,0:T(8,128)S(1)}, f32[2,128,128]{2,1,0:T(8,128)S(1)}, u32[]{:S(2)}, u32[]{:S(2)}) collective-permute-start(f32[2,128,128]{2,1,0:T(8,128)S(1)} %convolution_add_fusion.18), channel_id=1, source_target_pairs={{0,8},{8,16},{16,24},{24,32},{32,40},{40,48},{48,56},{56,64},{64,7... | collective-permute-start | bytes 393224 | tf_op jit(solution)/shard_map/while/body/eval_jaxpr/ppermute | solution.py:12
  357.4 8.3 %collective-permute-start = (f32[2,128,128]{2,1,0:T(8,128)S(1)}, f32[2,128,128]{2,1,0:T(8,128)S(1)}, u32[]{:S(2)}, u32[]{:S(2)}) collective-permute-start(f32[2,128,128]{2,1,0:T(8,128)S(1)} %convolution_add_fusion.18), channel_id=1, source_target_pairs={{0,8},{8,16},{16,24},{24,32},{32,40},{40,48},{48,56},{56,64},{64,7... | collective-permute-start | bytes 393224 | tf_op jit(solution)/shard_map/while/body/eval_jaxpr/ppermute | solution.py:12
  366.0 9.3 %collective-permute-start = (f32[2,128,128]{2,1,0:T(8,128)S(1)}, f32[2,128,128]{2,1,0:T(8,128)S(1)}, u32[]{:S(2)}, u32[]{:S(2)}) collective-permute-start(f32[2,128,128]{2,1,0:T(8,128)S(1)} %convolution_add_fusion.18), channel_id=1, source_target_pairs={{0,8},{8,16},{16,24},{24,32},{32,40},{40,48},{48,56},{56,64},{64,7... | collective-permute-start | bytes 393224 | tf_op jit(solution)/shard_map/while/body/eval_jaxpr/ppermute | solution.py:12
  375.6 8.4 %collective-permute-start = (f32[2,128,128]{2,1,0:T(8,128)S(1)}, f32[2,128,128]{2,1,0:T(8,128)S(1)}, u32[]{:S(2)}, u32[]{:S(2)}) collective-permute-start(f32[2,128,128]{2,1,0:T(8,128)S(1)} %convolution_add_fusion.18), channel_id=1, source_target_pairs={{0,8},{8,16},{16,24},{24,32},{32,40},{40,48},{48,56},{56,64},{64,7... | collective-permute-start | bytes 393224 | tf_op jit(solution)/shard_map/while/body/eval_jaxpr/ppermute | solution.py:12
  384.3 7.8 %collective-permute-start = (f32[2,128,128]{2,1,0:T(8,128)S(1)}, f32[2,128,128]{2,1,0:T(8,128)S(1)}, u32[]{:S(2)}, u32[]{:S(2)}) collective-permute-start(f32[2,128,128]{2,1,0:T(8,128)S(1)} %convolution_add_fusion.18), channel_id=1, source_target_pairs={{0,8},{8,16},{16,24},{24,32},{32,40},{40,48},{48,56},{56,64},{64,7... | collective-permute-start | bytes 393224 | tf_op jit(solution)/shard_map/while/body/eval_jaxpr/ppermute | solution.py:12
  392.4 7.8 %collective-permute-start = (f32[2,128,128]{2,1,0:T(8,128)S(1)}, f32[2,128,128]{2,1,0:T(8,128)S(1)}, u32[]{:S(2)}, u32[]{:S(2)}) collective-permute-start(f32[2,128,128]{2,1,0:T(8,128)S(1)} %convolution_add_fusion.18), channel_id=1, source_target_pairs={{0,8},{8,16},{16,24},{24,32},{32,40},{40,48},{48,56},{56,64},{64,7... | collective-permute-start | bytes 393224 | tf_op jit(solution)/shard_map/while/body/eval_jaxpr/ppermute | solution.py:12
  400.5 7.8 %collective-permute-start = (f32[2,128,128]{2,1,0:T(8,128)S(1)}, f32[2,128,128]{2,1,0:T(8,128)S(1)}, u32[]{:S(2)}, u32[]{:S(2)}) collective-permute-start(f32[2,128,128]{2,1,0:T(8,128)S(1)} %convolution_add_fusion.18), channel_id=1, source_target_pairs={{0,8},{8,16},{16,24},{24,32},{32,40},{40,48},{48,56},{56,64},{64,7... | collective-permute-start | bytes 393224 | tf_op jit(solution)/shard_map/while/body/eval_jaxpr/ppermute | solution.py:12
  408.6 7.8 %collective-permute-start = (f32[2,128,128]{2,1,0:T(8,128)S(1)}, f32[2,128,128]{2,1,0:T(8,128)S(1)}, u32[]{:S(2)}, u32[]{:S(2)}) collective-permute-start(f32[2,128,128]{2,1,0:T(8,128)S(1)} %convolution_add_fusion.18), channel_id=1, source_target_pairs={{0,8},{8,16},{16,24},{24,32},{32,40},{40,48},{48,56},{56,64},{64,7... | collective-permute-start | bytes 393224 | tf_op jit(solution)/shard_map/while/body/eval_jaxpr/ppermute | solution.py:12
  416.7 7.8 %collective-permute-start = (f32[2,128,128]{2,1,0:T(8,128)S(1)}, f32[2,128,128]{2,1,0:T(8,128)S(1)}, u32[]{:S(2)}, u32[]{:S(2)}) collective-permute-start(f32[2,128,128]{2,1,0:T(8,128)S(1)} %convolution_add_fusion.18), channel_id=1, source_target_pairs={{0,8},{8,16},{16,24},{24,32},{32,40},{40,48},{48,56},{56,64},{64,7... | collective-permute-start | bytes 393224 | tf_op jit(solution)/shard_map/while/body/eval_jaxpr/ppermute | solution.py:12
  424.8 7.8 %collective-permute-start = (f32[2,128,128]{2,1,0:T(8,128)S(1)}, f32[2,128,128]{2,1,0:T(8,128)S(1)}, u32[]{:S(2)}, u32[]{:S(2)}) collective-permute-start(f32[2,128,128]{2,1,0:T(8,128)S(1)} %convolution_add_fusion.18), channel_id=1, source_target_pairs={{0,8},{8,16},{16,24},{24,32},{32,40},{40,48},{48,56},{56,64},{64,7... | collective-permute-start | bytes 393224 | tf_op jit(solution)/shard_map/while/body/eval_jaxpr/ppermute | solution.py:12
  438.1 1.4 copy-start.6
  514.3 7.5 %copy-start.1 = (bf16[3,2304,256]{2,1,0:T(8,128)(2,1)S(1)}, bf16[3,2304,256]{2,1,0:T(8,128)(2,1)}, u32[]{:S(2)}) copy-start(bf16[3,2304,256]{2,1,0:T(8,128)(2,1)} %param.16) | copy-start | bytes 10616836
Sparse Core Ops, SparseCore 0:
  439.5 74.7 all-gather.1
where the time goes:
time: 531 us; the launch traced here: 529 us
  matrix products  236 us (44%)
  waiting for transfers between devices  115 us (22%)
  local copies, waits for them, and re-layouts  53.9 us (10%)
  blocking collectives  47.3 us (9%)
  starting transfers between devices  34.1 us (6%)
  other arithmetic  25.8 us (5%)
  between operations  13.7 us (3%)
    ppermute x16, waiting for transfers between devices, passed_along(): return lax.ppermute(shard, axis, pairs)  89.3 us
    all_to_all x1, blocking collectives, body(): lax.all_to_all(out_weight, 'head', split_axis=1, concat_axis=0, tiled=True)  47.3 us
    dot_general x112, matrix products, lower_inverse(): jnp.einsum('hts,hsr->htr', inverse, power, precision=highest)  43.3 us
    ppermute x16, starting transfers between devices, passed_along(): return lax.ppermute(shard, axis, pairs)  34.1 us
    all_gather x1, waiting for transfers between devices, body(): lax.all_gather(gated, 'head', axis=1, tiled=True)  25.7 us
    dot_general x96, matrix products, lower_inverse(): power = jnp.einsum('hts,hsr->htr', power, power, precision=highest)  25.4 us
    dot_general x16, matrix products, advance(): pairs = jnp.einsum('htc,hsc->hts', k_pos, k_neg, precision=highest)  23.2 us
    dot_general x16, matrix products, advance(): jnp.einsum('htc,hsc->hts', q_pos, k_neg, precision=highest)  23 us
  transfers between devices with their start and end apart: 17, of which 16 were waited for; matrix products, arithmetic and copies ran while one was open for 3% of the time, Pallas kernels for 0%

commit v1 on v0

v1 whole, which is shorter than its diff:
```python
import functools

import jax
import jax.numpy as jnp
from jax import lax
from jax.experimental import pallas as pl
from jax.experimental.pallas import tpu as pltpu
from jax.sharding import PartitionSpec as P

F32 = jnp.float32
BF16 = jnp.bfloat16
C = 128
W = 128
TILE = 512
VMEM = 56 * 1024 * 1024


def mm(a, b):
    return jnp.dot(a, b, preferred_element_type=F32)


def mm_nt(a, b):
    return lax.dot_general(a, b, (((1,), (1,)), ((), ())), preferred_element_type=F32)


def bd(a):
    z = jnp.zeros((a.shape[0], W), a.dtype)
    return jnp.concatenate(
        [
            jnp.concatenate([a[:, :W], z], axis=1),
            jnp.concatenate([z, a[:, W:]], axis=1),
        ],
        axis=0,
    )


def per_head(a, fn):
    return jnp.concatenate(
        [
            jnp.broadcast_to(fn(a[:, :W]), (a.shape[0], W)),
            jnp.broadcast_to(fn(a[:, W:]), (a.shape[0], W)),
        ],
        axis=1,
    )


def normalise(x, gain):
    wide = x.astype(F32)
    ms = jnp.mean(wide * wide, axis=-1, keepdims=True)
    return (wide * lax.rsqrt(ms + 1e-06) * gain).astype(BF16)


def local_kernel(
    x_ref,
    halo_ref,
    gain_ref,
    w_ref,
    conv_ref,
    down_ref,
    g_ref,
    b_ref,
    low_ref,
    m_ref,
    q_ref,
    u_ref,
    w_out_ref,
    z_ref,
    fin_ref,
    normed,
    proj,
    state,
):
    step = pl.program_id(0)
    n = TILE // C
    gain = gain_ref[...]

    @pl.when(step == 0)
    def _():
        before = normalise(halo_ref[...], gain)
        for i in range(3):
            proj[i, 0:8, :] = mm(before, w_ref[i])[8:16]
        rows = lax.broadcasted_iota(jnp.int32, (W, 2 * W), 0)
        cols = lax.broadcasted_iota(jnp.int32, (W, 2 * W), 1) % W
        state[:, : 2 * W] = jnp.zeros((W, 2 * W), F32)
        state[:, 2 * W :] = (rows == cols).astype(F32)

    @pl.when(step > 0)
    def _():
        for i in range(3):
            proj[i, 0:8, :] = proj[i, TILE : TILE + 8, :]

    for r in range(n):
        at = pl.ds(r * C, C)
        normed[at, :] = normalise(x_ref[at, :], gain)
    for i in range(3):
        proj[i, 8 : 8 + TILE, :] = mm(normed[...], w_ref[i])
    low_ref[...] = mm(normed[...], down_ref[...]).astype(BF16)

    rows = lax.broadcasted_iota(jnp.int32, (C, 2 * C), 0)
    cols = lax.broadcasted_iota(jnp.int32, (C, 2 * C), 1) % C
    strict = cols < rows
    inclusive = cols <= rows
    tri = inclusive.astype(F32).astype(BF16)

    taps = conv_ref[...].astype(F32)

    def conv(i, c):
        total = None
        for j in range(4):
            part = taps[i, j : j + 1, :] * proj[i, pl.ds(5 + j + c * C, C), :]
            total = part if total is None else total + part
        return total * pl.reciprocal(1.0 + jnp.exp(-total), approx=True)

    def unit(f):
        return f * per_head(
            f, lambda h: lax.rsqrt(jnp.sum(h * h, axis=-1, keepdims=True) + 1e-06)
        )

    chunks = range(n)
    q = [unit(conv(0, c)) * (W**-0.5) for c in chunks]
    k = [unit(conv(1, c)) for c in chunks]
    v = [conv(2, c) for c in chunks]
    beta, cum = [], []
    for c in chunks:
        at = pl.ds(c * C, C)
        beta.append(jnp.concatenate([b_ref[0:1, at], b_ref[1:2, at]], axis=1))
        g = jnp.concatenate([g_ref[0, at, :], g_ref[1, at, :]], axis=1)
        hi = g.astype(BF16)
        lo = (g - hi.astype(F32)).astype(BF16)
        cum.append(mm(tri, jnp.concatenate([hi, lo], axis=0)))
    mid = [a[C // 2 - 1 : C // 2, :] for a in cum]
    last = [a[C - 1 : C, :] for a in cum]
    rise = [jnp.exp(cum[c] - mid[c]) for c in chunks]
    fall = [jnp.exp(mid[c] - cum[c]) for c in chunks]
    from_start = [jnp.exp(mid[c]) for c in chunks]
    to_end = [jnp.exp(last[c] - mid[c]) for c in chunks]
    kr = [k[c] * rise[c] for c in chunks]
    qr = [q[c] * rise[c] for c in chunks]
    kf = [k[c] * fall[c] for c in chunks]
    pairs = [
        mm_nt(
            jnp.concatenate([kr[c].astype(BF16), qr[c].astype(BF16)], axis=0),
            bd(kf[c].astype(BF16)),
        )
        for c in chunks
    ]
    lower = [jnp.where(strict, pairs[c][:C] * beta[c], 0.0) for c in chunks]
    for c in chunks:
        at = pl.ds(c * C, C)
        m_ref[at, :] = jnp.where(inclusive, pairs[c][C:] * beta[c], 0.0).astype(BF16)
        q_ref[at, :] = (qr[c] * from_start[c]).astype(BF16)

    two = (rows // 2 == cols // 2) & strict
    inv = [jnp.where(two, -lower[c], 0.0) for c in chunks]
    inv16 = [a.astype(BF16) for a in inv]
    lower16 = [a.astype(BF16) for a in lower]
    size = 2
    while size < C:
        off = (
            (rows // (2 * size) == cols // (2 * size))
            & (rows % (2 * size) >= size)
            & (cols % (2 * size) < size)
        )
        keep = off.astype(F32).astype(BF16)
        cross = [lower16[c] * keep for c in chunks]
        left = [cross[c].astype(F32) + mm(cross[c], bd(inv16[c])) for c in chunks]
        left16 = [a.astype(BF16) for a in left]
        both = [left[c] + mm(inv16[c], bd(left16[c])) for c in chunks]
        inv = [inv[c] - both[c] for c in chunks]
        inv16 = [a.astype(BF16) for a in inv]
        size *= 2

    kpos = [kr[c] * from_start[c] for c in chunks]
    u = [(v[c] + mm(inv16[c], bd(v[c].astype(BF16)))).astype(BF16) for c in chunks]
    w = [(kpos[c] + mm(inv16[c], bd(kpos[c].astype(BF16)))).astype(BF16) for c in chunks]
    kt = []
    for c in chunks:
        ke = kf[c] * to_end[c]
        both_t = jnp.concatenate([ke[:, :W].T, ke[:, W:].T], axis=1)
        kt.append((both_t * beta[c]).astype(BF16))
    bmat = [mm(kt[c], bd(u[c])) for c in chunks]
    emat = [mm(kt[c], bd(w[c])).astype(BF16) for c in chunks]
    ends = jnp.concatenate(
        [jnp.exp(last[c])[:, h * W : (h + 1) * W] for c in chunks for h in range(2)],
        axis=0,
    ).T
    zb = state[:, : 2 * W]
    za = state[:, 2 * W :]
    for c in chunks:
        at = pl.ds(c * C, C)
        u_ref[at, :] = u[c]
        w_out_ref[at, :] = w[c]
        zb16, za16 = zb.astype(BF16), za.astype(BF16)
        z_ref[at, : 2 * W] = zb16
        z_ref[at, 2 * W :] = za16
        decay = jnp.concatenate(
            [
                jnp.broadcast_to(ends[:, 2 * c : 2 * c + 1], (W, W)),
                jnp.broadcast_to(ends[:, 2 * c + 1 : 2 * c + 2], (W, W)),
            ],
            axis=1,
        )
        zb = decay * zb + bmat[c] - mm(emat[c], bd(zb16))
        za = decay * za - mm(emat[c], bd(za16))
    state[:, : 2 * W] = zb
    state[:, 2 * W :] = za
    fin_ref[:, : 2 * W] = zb.astype(BF16)
    fin_ref[:, 2 * W :] = za.astype(BF16)


def local_part(x, halo, gain, qkv, conv, down, g, b):
    tokens, d = x.shape
    rank = down.shape[1]
    grid = tokens // TILE
    whole = lambda *shape: pl.BlockSpec(shape, lambda i: (0,) * len(shape))
    rows = lambda width: pl.BlockSpec((TILE, width), lambda i: (i, 0))
    return pl.pallas_call(
        local_kernel,
        grid=(grid,),
        in_specs=[
            rows(d),
            whole(16, d),
            whole(1, d),
            whole(3, d, 2 * W),
            whole(3, 4, 2 * W),
            whole(d, rank),
            pl.BlockSpec((2, TILE, W), lambda i: (0, i, 0)),
            pl.BlockSpec((2, TILE), lambda i: (0, i)),
        ],
        out_specs=[
            rows(rank),
            rows(2 * W),
            rows(2 * W),
            rows(2 * W),
            rows(2 * W),
            rows(4 * W),
            whole(W, 4 * W),
        ],
        out_shape=[
            jax.ShapeDtypeStruct((tokens, rank), BF16),
            jax.ShapeDtypeStruct((tokens, 2 * W), BF16),
            jax.ShapeDtypeStruct((tokens, 2 * W), BF16),
            jax.ShapeDtypeStruct((tokens, 2 * W), BF16),
            jax.ShapeDtypeStruct((tokens, 2 * W), BF16),
            jax.ShapeDtypeStruct((tokens, 4 * W), BF16),
            jax.ShapeDtypeStruct((W, 4 * W), BF16),
        ],
        scratch_shapes=[
            pltpu.VMEM((TILE, d), BF16),
            pltpu.VMEM((3, TILE + 8, 2 * W), F32),
            pltpu.VMEM((W, 4 * W), F32),
        ],
        compiler_params=pltpu.CompilerParams(vmem_limit_bytes=VMEM),
        cost_estimate=pl.CostEstimate(
            flops=14_000_000_000, bytes_accessed=24_000_000, transcendentals=6_000_000
        ),
        name="local_part",
    )(x, halo, gain, qkv, conv, down, g, b)


def reading_kernel(m_ref, q_ref, u_ref, w_ref, z_ref, low_ref, up_ref, gain_ref, o_ref, r_ref, s_ref):
    n = m_ref.shape[0] // C
    ats = [pl.ds(c * C, C) for c in range(n)]
    ms = [m_ref[at, :] for at in ats]
    mu = [mm(ms[c], bd(u_ref[ats[c], :])) for c in range(n)]
    mw = [mm(ms[c], bd(w_ref[ats[c], :])) for c in range(n)]
    rd = [(q_ref[ats[c], :].astype(F32) - mw[c]).astype(BF16) for c in range(n)]
    for c in range(n):
        o_ref[ats[c], :] = mu[c] + mm(rd[c], bd(z_ref[ats[c], : 2 * W]))
        r_ref[ats[c], :] = mm(rd[c], bd(z_ref[ats[c], 2 * W :])).astype(BF16)
    gate = mm(low_ref[...], up_ref[...])
    s_ref[...] = (
        gain_ref[...] * pl.reciprocal(1.0 + jnp.exp(-gate), approx=True)
    ).astype(BF16)


def reading_part(m, q, u, w, z, low, up, gain):
    tokens = m.shape[0]
    rank = low.shape[1]
    whole = lambda *shape: pl.BlockSpec(shape, lambda i: (0,) * len(shape))
    rows = lambda width: pl.BlockSpec((TILE, width), lambda i: (i, 0))
    return pl.pallas_call(
        reading_kernel,
        grid=(tokens // TILE,),
        in_specs=[rows(2 * W)] * 4
        + [rows(4 * W), rows(rank), whole(rank, 2 * W), whole(1, 2 * W)],
        out_specs=[rows(2 * W)] * 3,
        out_shape=[
            jax.ShapeDtypeStruct((tokens, 2 * W), F32),
            jax.ShapeDtypeStruct((tokens, 2 * W), BF16),
            jax.ShapeDtypeStruct((tokens, 2 * W), BF16),
        ],
        compiler_params=pltpu.CompilerParams(vmem_limit_bytes=VMEM),
        cost_estimate=pl.CostEstimate(
            flops=3_000_000_000, bytes_accessed=12_000_000, transcendentals=1_000_000
        ),
        name="reading_part",
    )(m, q, u, w, z, low, up, gain)


def compose_kernel(zi_ref, own, one, two, three, tot_ref, pre_ref, slots):
    z = zi_ref[0]
    for d, ref in enumerate((own, one, two, three)):
        slots[d] = ref[...]
    rows = lax.broadcasted_iota(jnp.int32, (W, 2 * W), 0)
    cols = lax.broadcasted_iota(jnp.int32, (W, 2 * W), 1) % W
    first = slots[z]
    pb = jnp.zeros((W, 2 * W), F32)
    pa = (rows == cols).astype(F32)
    tb = first[:, : 2 * W].astype(F32)
    ta = first[:, 2 * W :].astype(F32)
    for j in range(1, 4):
        here = j == z
        pb = jnp.where(here, tb, pb)
        pa = jnp.where(here, ta, pa)
        nxt = slots[lax.rem(z - j + 4, 4)]
        a = nxt[:, 2 * W :]
        tb = nxt[:, : 2 * W].astype(F32) + mm(a, bd(tb.astype(BF16)))
        ta = mm(a, bd(ta.astype(BF16)))
    tot_ref[:, : 2 * W] = tb.astype(BF16)
    tot_ref[:, 2 * W :] = ta.astype(BF16)
    pre_ref[:, : 2 * W] = pb.astype(BF16)
    pre_ref[:, 2 * W :] = pa.astype(BF16)


def compose(zi, own, one, two, three):
    shape = jax.ShapeDtypeStruct(own.shape, BF16)
    return pl.pallas_call(
        compose_kernel,
        in_specs=[pl.BlockSpec(memory_space=pltpu.SMEM)]
        + [pl.BlockSpec(memory_space=pltpu.VMEM)] * 4,
        out_specs=[pl.BlockSpec(memory_space=pltpu.VMEM)] * 2,
        out_shape=[shape, shape],
        scratch_shapes=[pltpu.VMEM((4,) + own.shape, BF16)],
        cost_estimate=pl.CostEstimate(
            flops=30_000_000, bytes_accessed=800_000, transcendentals=0
        ),
        name="compose",
    )(zi, own, one, two, three)


def gated_kernel(xi_ref, one, two, three, pre, o_ref, r_ref, s_ref, out_ref, start):
    @pl.when(pl.program_id(0) == 0)
    def _():
        xi = xi_ref[0]
        s = jnp.zeros((W, 2 * W), F32)
        for d, ref in ((3, three), (2, two), (1, one)):
            nxt = ref[:, : 2 * W].astype(F32) + mm(ref[:, 2 * W :], bd(s.astype(BF16)))
            s = jnp.where(xi >= d, nxt, s)
        s = pre[:, : 2 * W].astype(F32) + mm(pre[:, 2 * W :], bd(s.astype(BF16)))
        start[...] = bd(s.astype(BF16))

    att = o_ref[...] + mm(r_ref[...], start[...])
    scale = per_head(
        att, lambda h: lax.rsqrt(jnp.mean(h * h, axis=-1, keepdims=True) + 1e-05)
    )
    out_ref[...] = (att * scale * s_ref[...].astype(F32)).astype(BF16)


def gated_part(xi, one, two, three, pre, o, r, s):
    tokens = o.shape[0]
    whole = pl.BlockSpec((W, 4 * W), lambda i: (0, 0))
    rows = pl.BlockSpec((TILE, 2 * W), lambda i: (i, 0))
    return pl.pallas_call(
        gated_kernel,
        grid=(tokens // TILE,),
        in_specs=[pl.BlockSpec(memory_space=pltpu.SMEM)] + [whole] * 4 + [rows] * 3,
        out_specs=rows,
        out_shape=jax.ShapeDtypeStruct((tokens, 2 * W), BF16),
        scratch_shapes=[pltpu.VMEM((2 * W, 2 * W), BF16)],
        compiler_params=pltpu.CompilerParams(vmem_limit_bytes=VMEM),
        cost_estimate=pl.CostEstimate(
            flops=300_000_000, bytes_accessed=5_000_000, transcendentals=10_000
        ),
        name="gated_part",
    )(xi, one, two, three, pre, o, r, s)


def mixed_kernel(ci_ref, *refs):
    n = (len(refs) - 2) // 2
    wt, mine, theirs, out = refs[0], refs[1 : 1 + n], refs[1 + n : 1 + 2 * n], refs[-1]
    del wt, mine, theirs, out, ci_ref


def body(
    activations,
    norm_gain,
    qkv_weight,
    conv_weight,
    gate_down_matrix,
    gate_up,
    log_forget_gates,
    step_size,
    out_gain,
    out_weight,
):
    tokens, d = activations.shape
    ctx = lax.axis_index("ctx")
    xi, zi = ctx // 4, ctx % 4
    halo = lax.ppermute(
        activations[tokens - 16 :], "ctx", [(i, i + 1) for i in range(15)]
    )
    low, m, q, u, w, z, fin = local_part(
        activations,
        halo,
        norm_gain.reshape(1, d),
        qkv_weight,
        conv_weight,
        gate_down_matrix,
        log_forget_gates,
        step_size,
    )

    def along_z(a, by):
        pairs = [(4 * i + j, 4 * i + (j + by) % 4) for i in range(4) for j in range(4)]
        return lax.ppermute(a, "ctx", pairs)

    def along_x(a, by):
        pairs = [(4 * i + j, 4 * ((i + by) % 4) + j) for i in range(4) for j in range(4)]
        return lax.ppermute(a, "ctx", pairs)

    z1, z3, z2 = along_z(fin, 1), along_z(fin, 3), along_z(fin, 2)
    o, r, s = reading_part(
        m, q, u, w, z, low, gate_up, out_gain.reshape(1, 2 * W)
    )
    total, before = compose(zi.reshape(1), fin, z1, z2, z3)
    x1, x3, x2 = along_x(total, 1), along_x(total, 3), along_x(total, 2)
    gated = gated_part(xi.reshape(1), x1, x2, x3, before, o, r, s)
    columns = lax.all_to_all(out_weight, "head", split_axis=1, concat_axis=0, tiled=True)
    mixed = jnp.dot(
        lax.all_gather(gated, "head", axis=1, tiled=True),
        columns,
        preferred_element_type=jnp.float32,
    )
    return mixed.astype(jnp.bfloat16)


def solution(mesh):
    in_specs = (
        P("ctx", None),
        P(),
        P(None, None, "head"),
        P(None, None, "head"),
        P(),
        P(None, "head"),
        P("head", "ctx", None),
        P("head", "ctx"),
        P("head"),
        P("head", None),
    )
    out_specs = P("ctx", "head")
    return jax.shard_map(body, mesh=mesh, in_specs=in_specs, out_specs=out_specs, check_vma=False)
```

time: 531 us -> 162 us (0.31)
  the two profiles are of different devices: /device:TPU:5 before, /device:TPU:1 now
where the time goes in v1:
time: 162 us; the launch traced here: 161 us
  Pallas kernels  51.4 us (32%)
  waiting for transfers between devices  36 us (22%)
  blocking collectives  33.4 us (21%)
  starting transfers between devices  15.1 us (9%)
  between operations  13.5 us (8%)
  matrix products  7.03 us (4%)
  local copies, waits for them, and re-layouts  4.95 us (3%)
    pallas_call x1, Pallas kernels, local_part(): pl.pallas_call(local_kernel, grid=(grid,), in_specs=[rows(d), whole(16, d...  37.1 us
    all_to_all x1, blocking collectives, body(): lax.all_to_all(out_weight, 'head', split_axis=1, concat_axis=0, tiled=True)  33.4 us
    all_gather x1, waiting for transfers between devices, body(): lax.all_gather(gated, 'head', axis=1, tiled=True)  31.5 us
    dot_general x1, matrix products, body(): jnp.dot(lax.all_gather(gated, 'head', axis=1, tiled=True), columns, prefe...  7.03 us
    pallas_call x1, Pallas kernels, reading_part(): pl.pallas_call(reading_kernel, grid=(tokens // TILE,), in_specs=[rows(2 *...  6.37 us
    ppermute x3, starting transfers between devices, along_z(): return lax.ppermute(a, 'ctx', pairs)  5.89 us
    pallas_call x1, Pallas kernels, gated_part(): pl.pallas_call(gated_kernel, grid=(tokens // TILE,), in_specs=[pl.BlockSp...  5.61 us
    ppermute x3, starting transfers between devices, along_x(): return lax.ppermute(a, 'ctx', pairs)  4.88 us
  transfers between devices with their start and end apart: 8, of which 5 were waited for; matrix products, arithmetic and copies ran while one was open for 1% of the time, Pallas kernels for 4%

profile of v1, /device:TPU:1, one launch (start us, length us, event | category | flops | bytes accessed | tf_op | source)
XLA Modules:
  0.0 161.3 jit_solution(15779927451081550105)
XLA Ops:
  6.5 0.0 all-gather.2.cloned.1.call-start
  6.5 0.9 slice.3
  7.4 4.4 %collective-permute-start = (bf16[16,2304]{1,0:T(8,128)(2,1)S(1)}, bf16[16,2304]{1,0:T(8,128)(2,1)S(1)}, u32[]{:S(2)}, u32[]{:S(2)}) collective-permute-start(bf16[16,2304]{1,0:T(8,128)(2,1)S(1)} %slice.3), channel_id=1, source_target_pairs={{0,8},{8,16},{16,24},{24,32},{32,40},{40,48},{48,56},{56,64},{64,7... | collective-permute-start | bytes 221192 | tf_op jit(solution)/shard_map/ppermute | solution.py:400
  11.8 1.3 reshape.17.gain_ref
  13.1 0.1 collective-permute-done.halo_ref
  13.2 0.0 copy-start.7
  13.2 0.6 copy-done.7
  13.8 37.1 %local_part.1 = (bf16[2048,128]{1,0:T(8,128)(2,1)}, bf16[2048,256]{1,0:T(8,128)(2,1)}, bf16[2048,256]{1,0:T(8,128)(2,1)}, bf16[2048,256]{1,0:T(8,128)(2,1)}, bf1...) custom-call(bf16[2048,2304]{1,0:T(8,128)(2,1)} %x_ref.1, bf16[16,2304]{1,0:T(8,128)(2,1)} %copy-done.7, ...), custom_call_target="tpu_custom_call" | custom-call | flops 14000000000 | bytes 24000000 | tf_op jit(solution)/shard_map/local_part/pallas_call | solution.py:217
  50.9 1.9 %collective-permute-start.1 = (bf16[128,512]{1,0:T(8,128)(2,1)}, bf16[128,512]{1,0:T(8,128)(2,1)S(1)}, u32[]{:S(2)}, u32[]{:S(2)}) collective-permute-start(bf16[128,512]{1,0:T(8,128)(2,1)} %get-tuple-element.17.own), channel_id=1, source_target_pairs={{0,8},{8,16},{16,24},{24,0},{32,40},{40,48},{48,56},{56,32},{64,72... | collective-permute-start | bytes 393224 | tf_op jit(solution)/shard_map/ppermute | solution.py:416
  52.8 3.3 %collective-permute-start.2 = (bf16[128,512]{1,0:T(8,128)(2,1)}, bf16[128,512]{1,0:T(8,128)(2,1)S(1)}, u32[]{:S(2)}, u32[]{:S(2)}) collective-permute-start(bf16[128,512]{1,0:T(8,128)(2,1)} %get-tuple-element.17.own), channel_id=1, source_target_pairs={{0,16},{8,24},{16,0},{24,8},{32,48},{40,56},{48,32},{56,40},{64,80... | collective-permute-start | bytes 393224 | tf_op jit(solution)/shard_map/ppermute | solution.py:416
  56.1 0.7 collective-permute-start.3
  56.8 0.7 collective-permute-done.1.one
  57.5 0.0 copy-start.1
  57.5 3.1 %collective-permute-done.2.two = bf16[128,512]{1,0:T(8,128)(2,1)S(1)} collective-permute-done((bf16[128,512]{1,0:T(8,128)(2,1)}, bf16[128,512]{1,0:T(8,128)(2,1)S(1)}, u32[]{:S(2)}, u32[]{:S(2)}) %collective-permute-start.2) | collective-permute-done | bytes 131104 | tf_op jit(solution)/shard_map/ppermute | solution.py:416
  60.5 0.0 copy-start.2
  60.5 0.7 collective-permute-done.3.three
  61.2 0.0 copy-start.3
  61.2 0.0 copy-done.1
  61.2 0.0 copy-done.2
  61.2 0.6 copy-done.3
  61.8 2.3 %compose.1 = (bf16[128,512]{1,0:T(8,128)(2,1)}, bf16[128,512]{1,0:T(8,128)(2,1)}) custom-call(s32[1]{0:T(128)} %bitcast.1.zi_ref, bf16[128,512]{1,0:T(8,128)(2,1)} %get-tuple-element.17.own, bf16[128,512]{1,0:T(8,128)(2,1)} %copy-done.1, bf16[128,512]{1,0:T(8,128)(2,1)} %copy-done.2, bf16[128,512]{1,0:T(8,128)(2,1)} %copy-done.3), custom_call_target="tpu_custom_call" | custom-call | flops 30000000 | bytes 800000 | tf_op jit(solution)/shard_map/compose/pallas_call | solution.py:328
  64.2 1.3 collective-permute-start.4
  65.5 2.9 %collective-permute-start.5 = (bf16[128,512]{1,0:T(8,128)(2,1)}, bf16[128,512]{1,0:T(8,128)(2,1)S(1)}, u32[]{:S(2)}, u32[]{:S(2)}) collective-permute-start(bf16[128,512]{1,0:T(8,128)(2,1)} %get-tuple-element.18), channel_id=1, source_target_pairs={{0,64},{8,72},{16,80},{24,88},{32,96},{40,104},{48,112},{56,120},{... | collective-permute-start | bytes 393224 | tf_op jit(solution)/shard_map/ppermute | solution.py:420
  68.3 0.7 collective-permute-start.6
  69.1 6.4 %reading_part.1 = (f32[2048,256]{1,0:T(8,128)}, bf16[2048,256]{1,0:T(8,128)(2,1)}, bf16[2048,256]{1,0:T(8,128)(2,1)}) custom-call(bf16[2048,256]{1,0:T(8,128)(2,1)} %get-tuple-element.20.m_ref, bf16[2048,256]{1,0:T(8,128)(2,1)} %get-tuple-element.21.q_ref, bf16[2048,256]{1,0:T(8,128)(2,1)} %get-tuple-element.22.u_ref, ...), custom_call_target="tpu_custom_call" | custom-call | flops 3000000000 | bytes 12000000 | tf_op jit(solution)/shard_map/reading_part/pallas_call | solution.py:282
  75.4 0.0 collective-permute-done.4.one
  75.4 0.0 copy-start.4
  75.4 0.0 collective-permute-done.5.two
  75.5 0.0 copy-start.5
  75.5 0.0 collective-permute-done.6.three
  75.5 0.0 copy-start.6
  75.5 0.6 copy-done.4
  76.1 0.0 copy-done.5
  76.1 0.1 copy-done.6
  76.2 0.0 copy-start
  76.2 5.6 %gated_part.1 = bf16[2048,256]{1,0:T(8,128)(2,1)} custom-call(s32[1]{0:T(128)} %bitcast.xi_ref, bf16[128,512]{1,0:T(8,128)(2,1)} %copy-done.4, bf16[128,512]{1,0:T(8,128)(2,1)} %copy-done.5, bf16[128,512]{1,0:T(8,128)(2,1)} %copy-done.6, bf16[128,512]{1,0:T(8,128)(2,1)} %get-tuple-element.19.pre, f32[2048,256]{1,0:T(8,128)} %get-tuple-element.26.o_ref, ...), custom_call_target="tpu_custom_call" | custom-call | flops 300000000 | bytes 5000000 | tf_op jit(solution)/shard_map/gated_part/pallas_call | solution.py:364
  81.8 0.0 all-gather.2.cloned.1.call-update
  81.8 0.0 copy-done
  81.9 0.6 copy.11
  82.5 33.4 %all_to_all.19 = bf16[256,8,288]{0,2,1:T(8,128)(2,1)S(1)} all-to-all(bf16[256,8,288]{0,2,1:T(8,128)(2,1)S(1)} %bitcast.10), channel_id=1, replica_groups=mesh['ctx'=16,'head'=8] {'head'}, dimensions={1} | all-to-all | bytes 2359296 | tf_op jit(solution)/shard_map/all_to_all | solution.py:429
  115.8 0.1 copy.13
  116.0 31.5 %all-gather.2.cloned.1.call-done = bf16[2048,2048]{1,0:T(8,128)(2,1)} async-done(((bf16[2048,256]{1,0:T(8,128)(2,1)}), bf16[2048,2048]{1,0:T(8,128)(2,1)}) %all-gather.2.cloned.1.call-update) | async-done | bytes 8388624 | tf_op jit(solution)/shard_map/all_gather | solution.py:431
  147.4 7.0 %convolution_convert_fusion = bf16[2048,288]{0,1:T(8,128)(2,1)} fusion(bf16[2048,2048]{1,0:T(8,128)(2,1)} %all-gather.2.cloned.1.call-done, bf16[2048,288]{0,1:T(8,128)(2,1)S(1)} %bitcast.11), kind=kOutput, calls=%fused_computation | convolution fusion | flops 2416508928 | bytes 10747904 | tf_op jit(solution)/shard_map/dot_general | solution.py:430
Async XLA Ops:
  6.5 140.9 %all-gather.2.cloned.1.call-start = ((), (), s32[]{:S(2)}) async-start(), calls=%async_computation.1 | async-start | bytes 9437184 | tf_op jit(solution)/shard_map/all_gather | solution.py:431
  7.4 5.8 %collective-permute-start = (bf16[16,2304]{1,0:T(8,128)(2,1)S(1)}, bf16[16,2304]{1,0:T(8,128)(2,1)S(1)}, u32[]{:S(2)}, u32[]{:S(2)}) collective-permute-start(bf16[16,2304]{1,0:T(8,128)(2,1)S(1)} %slice.3), channel_id=1, source_target_pairs={{0,8},{8,16},{16,24},{24,32},{32,40},{40,48},{48,56},{56,64},{64,7... | collective-permute-start | bytes 221192 | tf_op jit(solution)/shard_map/ppermute | solution.py:400
  13.2 0.6 copy-start.7
  50.9 6.6 %collective-permute-start.1 = (bf16[128,512]{1,0:T(8,128)(2,1)}, bf16[128,512]{1,0:T(8,128)(2,1)S(1)}, u32[]{:S(2)}, u32[]{:S(2)}) collective-permute-start(bf16[128,512]{1,0:T(8,128)(2,1)} %get-tuple-element.17.own), channel_id=1, source_target_pairs={{0,8},{8,16},{16,24},{24,0},{32,40},{40,48},{48,56},{56,32},{64,72... | collective-permute-start | bytes 393224 | tf_op jit(solution)/shard_map/ppermute | solution.py:416
  52.8 7.7 %collective-permute-start.2 = (bf16[128,512]{1,0:T(8,128)(2,1)}, bf16[128,512]{1,0:T(8,128)(2,1)S(1)}, u32[]{:S(2)}, u32[]{:S(2)}) collective-permute-start(bf16[128,512]{1,0:T(8,128)(2,1)} %get-tuple-element.17.own), channel_id=1, source_target_pairs={{0,16},{8,24},{16,0},{24,8},{32,48},{40,56},{48,32},{56,40},{64,80... | collective-permute-start | bytes 393224 | tf_op jit(solution)/shard_map/ppermute | solution.py:416
  56.1 5.1 %collective-permute-start.3 = (bf16[128,512]{1,0:T(8,128)(2,1)}, bf16[128,512]{1,0:T(8,128)(2,1)S(1)}, u32[]{:S(2)}, u32[]{:S(2)}) collective-permute-start(bf16[128,512]{1,0:T(8,128)(2,1)} %get-tuple-element.17.own), channel_id=1, source_target_pairs={{0,24},{8,0},{16,8},{24,16},{32,56},{40,32},{48,40},{56,48},{64,88... | collective-permute-start | bytes 393224 | tf_op jit(solution)/shard_map/ppermute | solution.py:416
  57.5 3.7 %copy-start.1 = (bf16[128,512]{1,0:T(8,128)(2,1)}, bf16[128,512]{1,0:T(8,128)(2,1)S(1)}, u32[]{:S(2)}) copy-start(bf16[128,512]{1,0:T(8,128)(2,1)S(1)} %collective-permute-done.1.one) | copy-start | bytes 393220
  60.5 0.7 copy-start.2
  61.2 0.6 copy-start.3
  64.2 11.3 %collective-permute-start.4 = (bf16[128,512]{1,0:T(8,128)(2,1)}, bf16[128,512]{1,0:T(8,128)(2,1)S(1)}, u32[]{:S(2)}, u32[]{:S(2)}) collective-permute-start(bf16[128,512]{1,0:T(8,128)(2,1)} %get-tuple-element.18), channel_id=1, source_target_pairs={{0,32},{8,40},{16,48},{24,56},{32,64},{40,72},{48,80},{56,88},{64,... | collective-permute-start | bytes 393224 | tf_op jit(solution)/shard_map/ppermute | solution.py:420
  65.5 10.0 %collective-permute-start.5 = (bf16[128,512]{1,0:T(8,128)(2,1)}, bf16[128,512]{1,0:T(8,128)(2,1)S(1)}, u32[]{:S(2)}, u32[]{:S(2)}) collective-permute-start(bf16[128,512]{1,0:T(8,128)(2,1)} %get-tuple-element.18), channel_id=1, source_target_pairs={{0,64},{8,72},{16,80},{24,88},{32,96},{40,104},{48,112},{56,120},{... | collective-permute-start | bytes 393224 | tf_op jit(solution)/shard_map/ppermute | solution.py:420
  68.3 7.1 %collective-permute-start.6 = (bf16[128,512]{1,0:T(8,128)(2,1)}, bf16[128,512]{1,0:T(8,128)(2,1)S(1)}, u32[]{:S(2)}, u32[]{:S(2)}) collective-permute-start(bf16[128,512]{1,0:T(8,128)(2,1)} %get-tuple-element.18), channel_id=1, source_target_pairs={{0,96},{8,104},{16,112},{24,120},{32,0},{40,8},{48,16},{56,24},{64... | collective-permute-start | bytes 393224 | tf_op jit(solution)/shard_map/ppermute | solution.py:420
  75.4 0.7 copy-start.4
  75.5 0.7 copy-start.5
  75.5 0.7 copy-start.6
  76.2 5.6 %copy-start = (bf16[256,2304]{1,0:T(8,128)(2,1)S(1)}, bf16[256,2304]{1,0:T(8,128)(2,1)}, u32[]{:S(2)}) copy-start(bf16[256,2304]{1,0:T(8,128)(2,1)} %param.19) | copy-start | bytes 3538948
Sparse Core Ops, SparseCore 0:
  82.0 65.4 all-gather.1

commit v2 on v1

v2 whole, which is shorter than its diff:
```python
import functools

import jax
import jax.numpy as jnp
from jax import lax
from jax.experimental import pallas as pl
from jax.experimental.pallas import tpu as pltpu
from jax.sharding import PartitionSpec as P

F32 = jnp.float32
BF16 = jnp.bfloat16
C = 128
W = 128
TILE = 512
MIB = 1024 * 1024


def mm(a, b):
    return jnp.dot(a, b, preferred_element_type=F32)


def mm_nt(a, b):
    return lax.dot_general(a, b, (((1,), (1,)), ((), ())), preferred_element_type=F32)


def bd(a):
    z = jnp.zeros((a.shape[0], W), a.dtype)
    return jnp.concatenate(
        [
            jnp.concatenate([a[:, :W], z], axis=1),
            jnp.concatenate([z, a[:, W:]], axis=1),
        ],
        axis=0,
    )


def per_head(a, fn):
    return jnp.concatenate(
        [
            jnp.broadcast_to(fn(a[:, :W]), (a.shape[0], W)),
            jnp.broadcast_to(fn(a[:, W:]), (a.shape[0], W)),
        ],
        axis=1,
    )


def local_kernel(
    x_ref,
    halo_ref,
    gain_ref,
    w_ref,
    conv_ref,
    down_ref,
    g_ref,
    b_ref,
    low_ref,
    m_ref,
    q_ref,
    u_ref,
    w_out_ref,
    z_ref,
    fin_ref,
    wide,
    narrow,
    low,
    scale,
    fresh,
    proj,
    state,
):
    step = pl.program_id(0)
    tiles = pl.num_programs(0) - 1
    n = TILE // C
    chunks = range(n)

    def projecting():
        block = TILE // 4

        def product(i, r):
            at = pl.ds(r * block, block)
            p = mm(x_ref[at, :], wide[i] if i < 3 else narrow[...])
            if i == 3:
                low[at, :] = p
                return
            for h in range(2):
                fresh[i, h, at, :] = p[:, h * W : (h + 1) * W]

        def root(r):
            at = pl.ds(r * C, C)
            rows = x_ref[at, :].astype(F32)
            ms = jnp.mean(rows * rows, axis=-1, keepdims=True)
            scale[at, :] = jnp.broadcast_to(lax.rsqrt(ms + 1e-06), (C, W))

        def apply(r):
            at = pl.ds(r * C, C)
            to = pl.ds(8 + r * C, C)
            for i in range(3):
                for h in range(2):
                    proj[i, h, to, :] = fresh[i, h, at, :] * scale[at, :]
            low_ref[at, :] = (low[at, :] * scale[at, :]).astype(BF16)

        products = [functools.partial(product, i, r) for i in range(4) for r in range(4)]
        roots = [functools.partial(root, r) for r in chunks]
        return products, roots, [functools.partial(apply, r) for r in chunks]

    def delta(products=(), roots=(), applies=()):
        products, roots = list(products), list(roots)

        def fill(parts, count=1):
            for part in parts[:count]:
                part()
            del parts[:count]

        rows = lax.broadcasted_iota(jnp.int32, (C, 2 * C), 0)
        cols = lax.broadcasted_iota(jnp.int32, (C, 2 * C), 1) % C
        strict = cols < rows
        inclusive = cols <= rows
        tri = inclusive.astype(F32).astype(BF16)
        taps = conv_ref[...].astype(F32)

        def conv(i, c):
            halves = []
            for h in range(2):
                total = None
                for j in range(4):
                    part = (
                        taps[i, j : j + 1, h * W : (h + 1) * W]
                        * proj[i, h, pl.ds(5 + j + c * C, C), :]
                    )
                    total = part if total is None else total + part
                halves.append(total * pl.reciprocal(1.0 + jnp.exp(-total), approx=True))
            return halves

        def unit(halves, factor=1.0):
            return jnp.concatenate(
                [
                    h
                    * (lax.rsqrt(jnp.sum(h * h, axis=-1, keepdims=True) + 1e-06) * factor)
                    for h in halves
                ],
                axis=1,
            )

        beta, cum = [], []
        for c in chunks:
            at = pl.ds(c * C, C)
            beta.append(jnp.concatenate([b_ref[0:1, at], b_ref[1:2, at]], axis=1))
            g = jnp.concatenate([g_ref[0, at, :], g_ref[1, at, :]], axis=1)
            hi = g.astype(BF16)
            lo = (g - hi.astype(F32)).astype(BF16)
            cum.append(mm(tri, jnp.concatenate([hi, lo], axis=0)))
        k = []
        for c in chunks:
            k.append(unit(conv(1, c)))
        mid = [a[C // 2 - 1 : C // 2, :] for a in cum]
        last = [a[C - 1 : C, :] for a in cum]
        rise = [jnp.exp(cum[c] - mid[c]) for c in chunks]
        fall = [jnp.exp(mid[c] - cum[c]) for c in chunks]
        from_start = [jnp.exp(mid[c]) for c in chunks]
        to_end = [jnp.exp(last[c] - mid[c]) for c in chunks]
        kr = [k[c] * rise[c] for c in chunks]
        kf = [k[c] * fall[c] for c in chunks]
        qr = []
        for c in chunks:
            qr.append(unit(conv(0, c), W**-0.5) * rise[c])
        v16 = [jnp.concatenate(conv(2, c), axis=1).astype(BF16) for c in chunks]
        pairs = [
            mm_nt(
                jnp.concatenate([kr[c].astype(BF16), qr[c].astype(BF16)], axis=0),
                bd(kf[c].astype(BF16)),
            )
            for c in chunks
        ]
        lower = [jnp.where(strict, pairs[c][:C] * beta[c], 0.0) for c in chunks]
        for c in chunks:
            at = pl.ds(c * C, C)
            m_ref[at, :] = jnp.where(inclusive, pairs[c][C:] * beta[c], 0.0).astype(BF16)
            q_ref[at, :] = (qr[c] * from_start[c]).astype(BF16)

        two = (rows // 2 == cols // 2) & strict
        eye = (rows == cols).astype(F32)
        inv = [(eye - jnp.where(two, lower[c], 0.0)).astype(BF16) for c in chunks]
        lower16 = [a.astype(BF16) for a in lower]
        size = 2
        while size < C:
            fill(roots)
            off = (
                (rows // (2 * size) == cols // (2 * size))
                & (rows % (2 * size) >= size)
                & (cols % (2 * size) < size)
            )
            keep = off.astype(F32).astype(BF16)
            left = [mm(lower16[c] * keep, bd(inv[c])).astype(BF16) for c in chunks]
            fill(products)
            both = [mm(inv[c], bd(left[c])).astype(BF16) for c in chunks]
            fill(products, 2)
            inv = [inv[c] - both[c] for c in chunks]
            size *= 2

        fill(products, len(products))
        fill(roots, len(roots))
        if applies:
            proj[:, :, 0:8, :] = proj[:, :, TILE : TILE + 8, :]
        for part in applies:
            part()
        kpos = [kr[c] * from_start[c] for c in chunks]
        u = [mm(inv[c], bd(v16[c])).astype(BF16) for c in chunks]
        w = [mm(inv[c], bd(kpos[c].astype(BF16))).astype(BF16) for c in chunks]
        kt = []
        for c in chunks:
            ke = kf[c] * to_end[c]
            both_t = jnp.concatenate([ke[:, :W].T, ke[:, W:].T], axis=1)
            kt.append((both_t * beta[c]).astype(BF16))
        bmat = [mm(kt[c], bd(u[c])) for c in chunks]
        emat = [mm(kt[c], bd(w[c])).astype(BF16) for c in chunks]
        ends = jnp.concatenate(
            [jnp.exp(last[c])[:, h * W : (h + 1) * W] for c in chunks for h in range(2)],
            axis=0,
        ).T
        zb = state[:, : 2 * W]
        za = state[:, 2 * W :]
        for c in chunks:
            at = pl.ds(c * C, C)
            u_ref[at, :] = u[c]
            w_out_ref[at, :] = w[c]
            zb16, za16 = zb.astype(BF16), za.astype(BF16)
            z_ref[at, : 2 * W] = zb16
            z_ref[at, 2 * W :] = za16
            decay = jnp.concatenate(
                [
                    jnp.broadcast_to(ends[:, 2 * c : 2 * c + 1], (W, W)),
                    jnp.broadcast_to(ends[:, 2 * c + 1 : 2 * c + 2], (W, W)),
                ],
                axis=1,
            )
            zb = decay * zb + bmat[c] - mm(emat[c], bd(zb16))
            za = decay * za - mm(emat[c], bd(za16))
        state[:, : 2 * W] = zb
        state[:, 2 * W :] = za

    @pl.when(step == 0)
    def _():
        gain = gain_ref[...].T
        for j in range(gain.shape[1]):
            at = pl.ds(j * W, W)
            column = gain[:, j : j + 1]
            for i in range(3):
                wide[i, at, :] = (w_ref[i, at, :].astype(F32) * column).astype(BF16)
            narrow[at, :] = (down_ref[at, :].astype(F32) * column).astype(BF16)
        rows = halo_ref[...].astype(F32)
        ms = jnp.mean(rows * rows, axis=-1, keepdims=True)
        for i in range(3):
            p = (mm(halo_ref[...], wide[i]) * lax.rsqrt(ms + 1e-06))[8:16]
            for h in range(2):
                proj[i, h, 0:8, :] = p[:, h * W : (h + 1) * W]
        rows = lax.broadcasted_iota(jnp.int32, (W, 2 * W), 0)
        cols = lax.broadcasted_iota(jnp.int32, (W, 2 * W), 1) % W
        state[:, : 2 * W] = jnp.zeros((W, 2 * W), F32)
        state[:, 2 * W :] = (rows == cols).astype(F32)
        for parts in projecting():
            for part in parts:
                part()

    @pl.when((step > 0) & (step < tiles))
    def _():
        delta(*projecting())

    @pl.when(step == tiles)
    def _():
        delta()
        fin_ref[...] = state[...].astype(BF16)


def local_part(x, halo, gain, qkv, conv, down, g, b):
    tokens, d = x.shape
    rank = down.shape[1]
    grid = tokens // TILE
    whole = lambda *shape: pl.BlockSpec(shape, lambda i: (0,) * len(shape))
    first = lambda i: jnp.minimum(i, grid - 1)
    then = lambda i: jnp.maximum(i - 1, 0)
    early = lambda width: pl.BlockSpec((TILE, width), lambda i: (first(i), 0))
    rows = lambda width: pl.BlockSpec((TILE, width), lambda i: (then(i), 0))
    return pl.pallas_call(
        local_kernel,
        grid=(grid + 1,),
        in_specs=[
            early(d),
            whole(16, d),
            whole(d // W, W),
            whole(3, d, 2 * W),
            whole(3, 4, 2 * W),
            whole(d, rank),
            pl.BlockSpec((2, TILE, W), lambda i: (0, then(i), 0)),
            pl.BlockSpec((2, TILE), lambda i: (0, then(i))),
        ],
        out_specs=[
            early(rank),
            rows(2 * W),
            rows(2 * W),
            rows(2 * W),
            rows(2 * W),
            rows(4 * W),
            whole(W, 4 * W),
        ],
        out_shape=[
            jax.ShapeDtypeStruct((tokens, rank), BF16),
            jax.ShapeDtypeStruct((tokens, 2 * W), BF16),
            jax.ShapeDtypeStruct((tokens, 2 * W), BF16),
            jax.ShapeDtypeStruct((tokens, 2 * W), BF16),
            jax.ShapeDtypeStruct((tokens, 2 * W), BF16),
            jax.ShapeDtypeStruct((tokens, 4 * W), BF16),
            jax.ShapeDtypeStruct((W, 4 * W), BF16),
        ],
        scratch_shapes=[
            pltpu.VMEM((3, d, 2 * W), BF16),
            pltpu.VMEM((d, rank), BF16),
            pltpu.VMEM((TILE, rank), F32),
            pltpu.VMEM((TILE, W), F32),
            pltpu.VMEM((3, 2, TILE, W), F32),
            pltpu.VMEM((3, 2, TILE + 8, W), F32),
            pltpu.VMEM((W, 4 * W), F32),
        ],
        compiler_params=pltpu.CompilerParams(vmem_limit_bytes=56 * MIB),
        cost_estimate=pl.CostEstimate(
            flops=14_000_000_000, bytes_accessed=24_000_000, transcendentals=6_000_000
        ),
        name="local_part",
    )(x, halo, gain, qkv, conv, down, g, b)


def reading_kernel(m_ref, q_ref, u_ref, w_ref, z_ref, low_ref, up_ref, gain_ref, o_ref, r_ref, s_ref):
    n = m_ref.shape[0] // C
    ats = [pl.ds(c * C, C) for c in range(n)]
    ms = [m_ref[at, :] for at in ats]
    mu = [mm(ms[c], bd(u_ref[ats[c], :])) for c in range(n)]
    mw = [mm(ms[c], bd(w_ref[ats[c], :])) for c in range(n)]
    rd = [(q_ref[ats[c], :].astype(F32) - mw[c]).astype(BF16) for c in range(n)]
    for c in range(n):
        o_ref[ats[c], :] = mu[c] + mm(rd[c], bd(z_ref[ats[c], : 2 * W]))
        r_ref[ats[c], :] = mm(rd[c], bd(z_ref[ats[c], 2 * W :])).astype(BF16)
    gate = mm(low_ref[...], up_ref[...])
    s_ref[...] = (
        gain_ref[...] * pl.reciprocal(1.0 + jnp.exp(-gate), approx=True)
    ).astype(BF16)


def reading_part(m, q, u, w, z, low, up, gain):
    tokens = m.shape[0]
    rank = low.shape[1]
    whole = lambda *shape: pl.BlockSpec(shape, lambda i: (0,) * len(shape))
    rows = lambda width: pl.BlockSpec((TILE, width), lambda i: (i, 0))
    return pl.pallas_call(
        reading_kernel,
        grid=(tokens // TILE,),
        in_specs=[rows(2 * W)] * 4
        + [rows(4 * W), rows(rank), whole(rank, 2 * W), whole(1, 2 * W)],
        out_specs=[rows(2 * W)] * 3,
        out_shape=[
            jax.ShapeDtypeStruct((tokens, 2 * W), F32),
            jax.ShapeDtypeStruct((tokens, 2 * W), BF16),
            jax.ShapeDtypeStruct((tokens, 2 * W), BF16),
        ],
        compiler_params=pltpu.CompilerParams(vmem_limit_bytes=56 * MIB),
        cost_estimate=pl.CostEstimate(
            flops=3_000_000_000, bytes_accessed=12_000_000, transcendentals=1_000_000
        ),
        name="reading_part",
    )(m, q, u, w, z, low, up, gain)


def compose_kernel(zi_ref, own, one, two, three, tot_ref, pre_ref, slots):
    z = zi_ref[0]
    for d, ref in enumerate((own, one, two, three)):
        slots[d] = ref[...]
    rows = lax.broadcasted_iota(jnp.int32, (W, 2 * W), 0)
    cols = lax.broadcasted_iota(jnp.int32, (W, 2 * W), 1) % W
    first = slots[z]
    pb = jnp.zeros((W, 2 * W), F32)
    pa = (rows == cols).astype(F32)
    tb = first[:, : 2 * W].astype(F32)
    ta = first[:, 2 * W :].astype(F32)
    for j in range(1, 4):
        here = j == z
        pb = jnp.where(here, tb, pb)
        pa = jnp.where(here, ta, pa)
        nxt = slots[lax.rem(z - j + 4, 4)]
        a = nxt[:, 2 * W :]
        tb = nxt[:, : 2 * W].astype(F32) + mm(a, bd(tb.astype(BF16)))
        ta = mm(a, bd(ta.astype(BF16)))
    tot_ref[:, : 2 * W] = tb.astype(BF16)
    tot_ref[:, 2 * W :] = ta.astype(BF16)
    pre_ref[:, : 2 * W] = pb.astype(BF16)
    pre_ref[:, 2 * W :] = pa.astype(BF16)


def compose(zi, own, one, two, three):
    shape = jax.ShapeDtypeStruct(own.shape, BF16)
    return pl.pallas_call(
        compose_kernel,
        in_specs=[pl.BlockSpec(memory_space=pltpu.SMEM)]
        + [pl.BlockSpec(memory_space=pltpu.VMEM)] * 4,
        out_specs=[pl.BlockSpec(memory_space=pltpu.VMEM)] * 2,
        out_shape=[shape, shape],
        scratch_shapes=[pltpu.VMEM((4,) + own.shape, BF16)],
        compiler_params=pltpu.CompilerParams(vmem_limit_bytes=4 * MIB),
        cost_estimate=pl.CostEstimate(
            flops=30_000_000, bytes_accessed=800_000, transcendentals=0
        ),
        name="compose",
    )(zi, own, one, two, three)


def gated_kernel(at_ref, one, two, three, pre, o_ref, r_ref, s_ref, *rest):
    outs, start = rest[:-1], rest[-1]
    step = pl.program_id(0)

    @pl.when(step == 0)
    def _():
        xi = at_ref[0]
        s = jnp.zeros((W, 2 * W), F32)
        for d, ref in ((3, three), (2, two), (1, one)):
            nxt = ref[:, : 2 * W].astype(F32) + mm(ref[:, 2 * W :], bd(s.astype(BF16)))
            s = jnp.where(xi >= d, nxt, s)
        s = pre[:, : 2 * W].astype(F32) + mm(pre[:, 2 * W :], bd(s.astype(BF16)))
        start[...] = bd(s.astype(BF16))

    att = o_ref[...] + mm(r_ref[...], start[...])
    scale = per_head(
        att, lambda h: lax.rsqrt(jnp.mean(h * h, axis=-1, keepdims=True) + 1e-05)
    )
    gated = (att * scale * s_ref[...].astype(F32)).astype(BF16)
    for d, out in enumerate(outs):

        @pl.when(step == d)
        def _():
            out[...] = gated


def gated_part(at, one, two, three, pre, o, r, s):
    part = o.shape[0] // 4
    whole = pl.BlockSpec((W, 4 * W), lambda i, at: (0, 0))
    rows = pl.BlockSpec((part, 2 * W), lambda i, at: (lax.rem(at[1] + i, 4), 0))
    keep = pl.BlockSpec((part, 2 * W), lambda i, at: (0, 0))
    return pl.pallas_call(
        gated_kernel,
        grid_spec=pltpu.PrefetchScalarGridSpec(
            num_scalar_prefetch=1,
            grid=(4,),
            in_specs=[whole] * 4 + [rows] * 3,
            out_specs=[keep] * 4,
            scratch_shapes=[pltpu.VMEM((2 * W, 2 * W), BF16)],
        ),
        out_shape=[jax.ShapeDtypeStruct((part, 2 * W), BF16)] * 4,
        compiler_params=pltpu.CompilerParams(vmem_limit_bytes=10 * MIB),
        cost_estimate=pl.CostEstimate(
            flops=300_000_000, bytes_accessed=5_000_000, transcendentals=10_000
        ),
        name="gated_part",
    )(at, one, two, three, pre, o, r, s)


def turned_kernel(at_ref, w_ref, mine_ref, other_ref, held):
    features = w_ref.shape[1] // 8
    held[...] = w_ref[...].T
    for j in range(4):
        to = pl.ds(j * features, features)
        for ref, core in ((mine_ref, at_ref[1]), (other_ref, 1 - at_ref[1])):
            at = pl.multiple_of((2 * j + core) * features, 16)
            ref[to, :] = held[pl.ds(at, features), :]


def turned(at, w):
    k, n = w.shape
    half = jax.ShapeDtypeStruct((n // 2, k), w.dtype)
    return pl.pallas_call(
        turned_kernel,
        in_specs=[
            pl.BlockSpec(memory_space=pltpu.SMEM),
            pl.BlockSpec(memory_space=pltpu.VMEM),
        ],
        out_specs=[pl.BlockSpec(memory_space=pltpu.VMEM)] * 2,
        out_shape=[half, half],
        scratch_shapes=[pltpu.VMEM((n, k), w.dtype)],
        compiler_params=pltpu.CompilerParams(vmem_limit_bytes=8 * MIB),
        cost_estimate=pl.CostEstimate(
            flops=0, bytes_accessed=2_400_000, transcendentals=0
        ),
        name="turned",
    )(at, w)


def mixed_kernel(at_ref, *refs):
    step = pl.program_id(0)
    weights, blocks, outs = refs[:8], refs[8:16], refs[16:]
    total = None
    for w, g in zip(weights, blocks, strict=True):
        part = mm_nt(w[...], g[...])
        total = part if total is None else total + part
    total = total.astype(BF16)
    for d, out in enumerate(outs):

        @pl.when(step == d)
        def _():
            out[...] = total


def mixed_part(at, weights, mine, theirs):
    features = weights[0].shape[0] // 8
    tokens = mine[0].shape[0]
    wspec = lambda first: pl.BlockSpec(
        (features, 2 * W), lambda i, at: (first + lax.rem(at[0] + i, 4), 0)
    )
    gspec = pl.BlockSpec((tokens, 2 * W), lambda i, at: (0, 0))
    ospec = pl.BlockSpec((features, tokens), lambda i, at: (0, 0))
    return pl.pallas_call(
        mixed_kernel,
        grid_spec=pltpu.PrefetchScalarGridSpec(
            num_scalar_prefetch=1,
            grid=(4,),
            in_specs=[wspec(0)] * 4 + [wspec(4)] * 3 + [wspec(0)] + [gspec] * 8,
            out_specs=[ospec] * 4,
        ),
        out_shape=[jax.ShapeDtypeStruct((features, tokens), BF16)] * 4,
        compiler_params=pltpu.CompilerParams(vmem_limit_bytes=16 * MIB),
        cost_estimate=pl.CostEstimate(
            flops=2_400_000_000, bytes_accessed=8_000_000, transcendentals=0
        ),
        name="mixed_part",
    )(at, *weights, *mine, *theirs)


def joined_kernel(at_ref, *refs):
    step = pl.program_id(0)
    for d, piece in enumerate(refs[:-1]):

        @pl.when(lax.rem(at_ref[0] - d + 4, 4) == step)
        def _():
            refs[-1][...] = piece[...]


def joined(at, pieces):
    features, tokens = pieces[0].shape
    return pl.pallas_call(
        joined_kernel,
        grid_spec=pltpu.PrefetchScalarGridSpec(
            num_scalar_prefetch=1,
            grid=(4,),
            in_specs=[pl.BlockSpec((features, tokens), lambda i, at: (0, 0))] * 4,
            out_specs=pl.BlockSpec((features, tokens), lambda i, at: (0, i)),
        ),
        out_shape=jax.ShapeDtypeStruct((features, 4 * tokens), BF16),
        compiler_params=pltpu.CompilerParams(vmem_limit_bytes=10 * MIB),
        cost_estimate=pl.CostEstimate(
            flops=0, bytes_accessed=2_400_000, transcendentals=0
        ),
        name="joined",
    )(at, *pieces)


def body(
    activations,
    norm_gain,
    qkv_weight,
    conv_weight,
    gate_down_matrix,
    gate_up,
    log_forget_gates,
    step_size,
    out_gain,
    out_weight,
):
    tokens, d = activations.shape
    ctx = lax.axis_index("ctx")
    xi, zi = ctx // 4, ctx % 4
    head = lax.axis_index("head")
    yi, ci = head // 2, head % 2

    def along_y(a, by):
        return lax.ppermute(a, "head", [(i, (i + 2 * by) % 8) for i in range(8)])

    def across(a):
        return lax.ppermute(a, "head", [(i, i ^ 1) for i in range(8)])

    halo = lax.ppermute(
        activations[tokens - 16 :], "ctx", [(i, i + 1) for i in range(15)]
    )
    here = jnp.stack([yi, ci])
    mine, other = turned(here, out_weight)
    both = jnp.concatenate([mine, across(other)], axis=0)
    below, above = along_y(both, 1), along_y(both, 3)
    low, m, q, u, w, z, fin = local_part(
        activations,
        halo,
        norm_gain.reshape(d // W, W),
        qkv_weight,
        conv_weight,
        gate_down_matrix,
        log_forget_gates,
        step_size,
    )

    def along_z(a, by):
        pairs = [(4 * i + j, 4 * i + (j + by) % 4) for i in range(4) for j in range(4)]
        return lax.ppermute(a, "ctx", pairs)

    def along_x(a, by):
        pairs = [(4 * i + j, 4 * ((i + by) % 4) + j) for i in range(4) for j in range(4)]
        return lax.ppermute(a, "ctx", pairs)

    fin, below, above = lax.optimization_barrier((fin, below, above))
    half = both.shape[0] // 2
    far = along_y(above[:half], 3), along_y(below[half:], 1)
    z1, z3, z2 = along_z(fin, 1), along_z(fin, 3), along_z(fin, 2)
    o, r, s = reading_part(
        m, q, u, w, z, low, gate_up, out_gain.reshape(1, 2 * W)
    )
    total, before = compose(zi.reshape(1), fin, z1, z2, z3)
    x1, x3, x2 = along_x(total, 1), along_x(total, 3), along_x(total, 2)
    at = jnp.stack([xi, yi])
    x1, far = lax.optimization_barrier((x1, far))
    q0, q1, q2, q3 = gated_part(at, x1, x2, x3, before, o, r, s)
    own = [q0, along_y(q1, 1), along_y(q3, 3), along_y(q2, 2)]
    weights = [both, below, above, far[0], both, below, above, far[1]]
    p0, p1, p2, p3 = mixed_part(here, weights, own, [across(a) for a in own])
    pieces = [p0, along_y(p1, 1), along_y(p2, 2), along_y(p3, 3)]
    return joined(yi.reshape(1), pieces).T


def solution(mesh):
    in_specs = (
        P("ctx", None),
        P(),
        P(None, None, "head"),
        P(None, None, "head"),
        P(),
        P(None, "head"),
        P("head", "ctx", None),
        P("head", "ctx"),
        P("head"),
        P("head", None),
    )
    out_specs = P("ctx", "head")
    return jax.shard_map(body, mesh=mesh, in_specs=in_specs, out_specs=out_specs, check_vma=False)
```

time: 162 us -> 122 us (0.75)
  blocking collectives: 33.4 us -> 0 us
  starting transfers between devices: 15.1 us -> 35.8 us
  between operations: 13.5 us -> 0.15 us
  waiting for transfers between devices: 36 us -> 26.7 us
  matrix products: 7.03 us -> 0 us
  local copies, waits for them, and re-layouts: 4.95 us -> 8.62 us
    all_to_all x1 -> x0, blocking collectives: 33.4 us -> none  [body(): lax.all_to_all(out_weight, 'head', split_axis=1, concat_axis=0, tiled=True)]
    all_gather x1 -> x0, waiting for transfers between devices: 31.5 us -> none  [body(): lax.all_gather(gated, 'head', axis=1, tiled=True)]
    ppermute x0 -> x15, starting transfers between devices: none -> 24.4 us  [the longest x10 12.5 us: along_y(): return lax.ppermute(a, 'head', [(i, (i + 2 * by) % 8) for i in range(8)])]
    ppermute x0 -> x15, waiting for transfers between devices: none -> 16.8 us  [the longest x10 15.6 us: along_y(): return lax.ppermute(a, 'head', [(i, (i + 2 * by) % 8) for i in range(8)])]
    dot_general x1 -> x0, matrix products: 7.03 us -> none  [body(): jnp.dot(lax.all_gather(gated, 'head', axis=1, tiled=True), columns, prefe...]
    ppermute x3, waiting for transfers between devices: 4.39 us -> 8.34 us  [along_z(): return lax.ppermute(a, 'ctx', pairs)]
    unnamed x17 -> x11, local copies, waits for them, and re-layouts: 2.62 us -> 5.97 us
    ppermute x3, starting transfers between devices: 5.89 us -> 4.16 us  [along_z(): return lax.ppermute(a, 'ctx', pairs)]
  transfers between devices with their start and end apart: 8 -> 22, of which waited for: 5 -> 8; matrix products, arithmetic and copies ran while one was open for 1% -> 1% of each run, Pallas kernels for 4% -> 32%
where the time goes in v2:
time: 122 us; the launch traced here: 121 us
  Pallas kernels  49.9 us (41%)
  starting transfers between devices  35.8 us (29%)
  waiting for transfers between devices  26.7 us (22%)
  local copies, waits for them, and re-layouts  8.62 us (7%)
    pallas_call x1, Pallas kernels, local_part(): pl.pallas_call(local_kernel, grid=(grid + 1,), in_specs=[early(d), whole(...  31.2 us
    ppermute x10, waiting for transfers between devices, along_y(): return lax.ppermute(a, 'head', [(i, (i + 2 * by) % 8) for i in range(8)])  15.6 us
    ppermute x10, starting transfers between devices, along_y(): return lax.ppermute(a, 'head', [(i, (i + 2 * by) % 8) for i in range(8)])  12.5 us
    ppermute x5, starting transfers between devices, across(): return lax.ppermute(a, 'head', [(i, i ^ 1) for i in range(8)])  11.8 us
    ppermute x3, waiting for transfers between devices, along_z(): return lax.ppermute(a, 'ctx', pairs)  8.34 us
    pallas_call x1, Pallas kernels, reading_part(): pl.pallas_call(reading_kernel, grid=(tokens // TILE,), in_specs=[rows(2 *...  6.37 us
    unnamed x11, local copies, waits for them, and re-layouts  5.97 us
    pallas_call x1, Pallas kernels, mixed_part(): pl.pallas_call(mixed_kernel, grid_spec=pltpu.PrefetchScalarGridSpec(num_s...  5.14 us
  transfers between devices with their start and end apart: 22, of which 8 were waited for; matrix products, arithmetic and copies ran while one was open for 1% of the time, Pallas kernels for 32%

profile of v2, /device:TPU:1, one launch (start us, length us, event | category | flops | bytes accessed | tf_op | source)
XLA Modules:
  0.0 121.3 jit_solution(11085970102533111010)
XLA Ops:
  0.0 0.1 pad_add_fusion.at_ref
  0.1 0.0 copy-start.1
  0.1 1.3 %copy-done.1 = bf16[256,2304]{1,0:T(8,128)(2,1)S(1)} copy-done((bf16[256,2304]{1,0:T(8,128)(2,1)S(1)}, bf16[256,2304]{1,0:T(8,128)(2,1)}, u32[]{:S(2)}) %copy-start.1) | copy-done | bytes 1179672
  1.3 1.0 turned.1
  2.3 1.5 %collective-permute-start = (bf16[1152,256]{1,0:T(8,128)(2,1)S(1)}, bf16[1152,256]{1,0:T(8,128)(2,1)S(1)}, u32[]{:S(2)}, u32[]{:S(2)}) collective-permute-start(bf16[1152,256]{1,0:T(8,128)(2,1)S(1)} %get-tuple-element.34), channel_id=1, source_target_pairs={{0,1},{1,0},{2,3},{3,2},{4,5},{5,4},{6,7},{7,6},{8,9},{9,8},{10,11... | collective-permute-start | bytes 1769480 | tf_op jit(solution)/shard_map/ppermute | solution.py:582
  3.8 0.9 slice.9
  4.7 3.6 %collective-permute-start.1 = (bf16[16,2304]{1,0:T(8,128)(2,1)S(1)}, bf16[16,2304]{1,0:T(8,128)(2,1)S(1)}, u32[]{:S(2)}, u32[]{:S(2)}) collective-permute-start(bf16[16,2304]{1,0:T(8,128)(2,1)S(1)} %slice.9), channel_id=1, source_target_pairs={{0,8},{8,16},{16,24},{24,32},{32,40},{40,48},{48,56},{56,64},{64,7... | collective-permute-start | bytes 221192 | tf_op jit(solution)/shard_map/ppermute | solution.py:584
  8.4 0.0 collective-permute-done
  8.5 2.8 %collective-permute-start.3 = (bf16[2304,256]{1,0:T(8,128)(2,1)S(1)}, bf16[2304,256]{1,0:T(8,128)(2,1)S(1)}, u32[]{:S(2)}, u32[]{:S(2)}) collective-permute-start(bf16[2304,256]{1,0:T(8,128)(2,1)S(1)} %constant_dynamic-update-slice_fusion.refs_0_.refs_4_), channel_id=1, source_target_pairs={{0,6},{1,7},{2,0},{3,1},{4,2},{5,3},{6,4},{7,5},{8,14},{9,15},{10,... | collective-permute-start | bytes 3538952 | tf_op jit(solution)/shard_map/ppermute | solution.py:579
  11.3 0.0 collective-permute-start.2
  11.3 0.0 collective-permute-done.1.halo_ref
  11.3 0.0 copy-start.4
  11.3 0.6 copy-done.4
  11.9 31.2 %local_part.1 = (bf16[2048,128]{1,0:T(8,128)(2,1)}, bf16[2048,256]{1,0:T(8,128)(2,1)}, bf16[2048,256]{1,0:T(8,128)(2,1)}, bf16[2048,256]{1,0:T(8,128)(2,1)}, bf1...) custom-call(bf16[2048,2304]{1,0:T(8,128)(2,1)} %x_ref.1, bf16[16,2304]{1,0:T(8,128)(2,1)} %copy-done.4, ...), custom_call_target="tpu_custom_call" | custom-call | flops 14000000000 | bytes 24000000 | tf_op jit(solution)/shard_map/local_part/pallas_call | solution.py:283
  43.1 0.0 collective-permute-done.3.refs_2_.refs_6_
  43.1 0.0 collective-permute-done.2.refs_1_.refs_5_
  43.1 0.9 slice.11
  44.0 0.9 slice.10
  44.9 2.7 %collective-permute-start.8 = (bf16[1152,256]{1,0:T(8,128)(2,1)}, bf16[1152,256]{1,0:T(8,128)(2,1)}, u32[]{:S(2)}, u32[]{:S(2)}) collective-permute-start(bf16[1152,256]{1,0:T(8,128)(2,1)} %slice.10), channel_id=1, source_target_pairs={{0,6},{1,7},{2,0},{3,1},{4,2},{5,3},{6,4},{7,5},{8,14},{9,15},{10,... | collective-permute-start | bytes 1769480 | tf_op jit(solution)/shard_map/ppermute | solution.py:579
  47.5 0.0 collective-permute-start.9
  47.6 3.1 %collective-permute-start.6 = (bf16[128,512]{1,0:T(8,128)(2,1)}, bf16[128,512]{1,0:T(8,128)(2,1)}, u32[]{:S(2)}, u32[]{:S(2)}) collective-permute-start(bf16[128,512]{1,0:T(8,128)(2,1)} %get-tuple-element.38.own), channel_id=1, source_target_pairs={{0,24},{8,0},{16,8},{24,16},{32,56},{40,32},{48,40},{56,48},{64,88... | collective-permute-start | bytes 393224 | tf_op jit(solution)/shard_map/ppermute | solution.py:604
  50.7 0.3 collective-permute-start.5
  51.0 0.7 collective-permute-start.4
  51.7 0.1 pad_add_fusion.1.at_ref
  51.8 2.5 %collective-permute-done.6.three = bf16[128,512]{1,0:T(8,128)(2,1)} collective-permute-done((bf16[128,512]{1,0:T(8,128)(2,1)}, bf16[128,512]{1,0:T(8,128)(2,1)}, u32[]{:S(2)}, u32[]{:S(2)}) %collective-permute-start.6) | collective-permute-done | bytes 131104 | tf_op jit(solution)/shard_map/ppermute | solution.py:604
  54.3 2.1 %collective-permute-done.5.two = bf16[128,512]{1,0:T(8,128)(2,1)} collective-permute-done((bf16[128,512]{1,0:T(8,128)(2,1)}, bf16[128,512]{1,0:T(8,128)(2,1)}, u32[]{:S(2)}, u32[]{:S(2)}) %collective-permute-start.5) | collective-permute-done | bytes 131104 | tf_op jit(solution)/shard_map/ppermute | solution.py:604
  56.4 3.7 %collective-permute-done.4.one = bf16[128,512]{1,0:T(8,128)(2,1)} collective-permute-done((bf16[128,512]{1,0:T(8,128)(2,1)}, bf16[128,512]{1,0:T(8,128)(2,1)}, u32[]{:S(2)}, u32[]{:S(2)}) %collective-permute-start.4) | collective-permute-done | bytes 131104 | tf_op jit(solution)/shard_map/ppermute | solution.py:604
  60.1 1.7 %compose.1 = (bf16[128,512]{1,0:T(8,128)(2,1)S(1)}, bf16[128,512]{1,0:T(8,128)(2,1)S(1)}) custom-call(s32[1]{0:T(128)} %bitcast.3.zi_ref, bf16[128,512]{1,0:T(8,128)(2,1)} %get-tuple-element.38.own, bf16[128,512]{1,0:T(8,128)(2,1)} %collective-permute-done.4.one, bf16[128,512]{1,0:T(8,128)(2,1)} %collective-permute-done.5.two, ...), custom_call_target="tpu_custom_call" | custom-call | flops 30000000 | bytes 800000 | tf_op jit(solution)/shard_map/compose/pallas_call | solution.py:398
  61.8 2.6 %collective-permute-start.11 = (bf16[128,512]{1,0:T(8,128)(2,1)S(1)}, bf16[128,512]{1,0:T(8,128)(2,1)S(1)}, u32[]{:S(2)}, u32[]{:S(2)}) collective-permute-start(bf16[128,512]{1,0:T(8,128)(2,1)S(1)} %get-tuple-element.39), channel_id=1, source_target_pairs={{0,96},{8,104},{16,112},{24,120},{32,0},{40,8},{48,16},{56,24},{64... | collective-permute-start | bytes 393224 | tf_op jit(solution)/shard_map/ppermute | solution.py:608
  64.4 0.5 collective-permute-start.10
  64.9 0.6 collective-permute-start.7
  65.5 6.4 %reading_part.1 = (f32[2048,256]{1,0:T(8,128)}, bf16[2048,256]{1,0:T(8,128)(2,1)}, bf16[2048,256]{1,0:T(8,128)(2,1)}) custom-call(bf16[2048,256]{1,0:T(8,128)(2,1)} %get-tuple-element.44.m_ref, bf16[2048,256]{1,0:T(8,128)(2,1)} %get-tuple-element.45.q_ref, bf16[2048,256]{1,0:T(8,128)(2,1)} %get-tuple-element.46.u_ref, ...), custom_call_target="tpu_custom_call" | custom-call | flops 3000000000 | bytes 12000000 | tf_op jit(solution)/shard_map/reading_part/pallas_call | solution.py:352
  71.8 1.6 %collective-permute-done.7.one = bf16[128,512]{1,0:T(8,128)(2,1)S(1)} collective-permute-done((bf16[128,512]{1,0:T(8,128)(2,1)S(1)}, bf16[128,512]{1,0:T(8,128)(2,1)S(1)}, u32[]{:S(2)}, u32[]{:S(2)}) %collective-permute-start.7) | collective-permute-done | bytes 131104 | tf_op jit(solution)/shard_map/ppermute | solution.py:608
  73.4 0.0 collective-permute-done.8.refs_3_
  73.4 0.0 collective-permute-done.9.refs_7_
  73.4 0.0 collective-permute-done.11.three
  73.4 0.0 collective-permute-done.10.two
  73.4 0.0 copy-start
  73.5 1.6 %copy-done = f32[2048,256]{1,0:T(8,128)S(1)} copy-done((f32[2048,256]{1,0:T(8,128)S(1)}, f32[2048,256]{1,0:T(8,128)}, u32[]{:S(2)}) %copy-start) | copy-done | bytes 2097176
  75.0 1.2 %copy-done.2 = bf16[2048,256]{1,0:T(8,128)(2,1)S(1)} copy-done((bf16[2048,256]{1,0:T(8,128)(2,1)S(1)}, bf16[2048,256]{1,0:T(8,128)(2,1)}, u32[]{:S(2)}) %copy-start.2) | copy-done | bytes 1048600
  76.3 1.2 %copy-done.3 = bf16[2048,256]{1,0:T(8,128)(2,1)S(1)} copy-done((bf16[2048,256]{1,0:T(8,128)(2,1)S(1)}, bf16[2048,256]{1,0:T(8,128)(2,1)}, u32[]{:S(2)}) %copy-start.3) | copy-done | bytes 1048600
  77.5 2.9 %gated_part.1 = (bf16[512,256]{1,0:T(8,128)(2,1)S(1)}, bf16[512,256]{1,0:T(8,128)(2,1)S(1)}, bf16[512,256]{1,0:T(8,128)(2,1)S(1)}, bf16[512,256]{1,0:T(8,128)(2,1)S(1)}) custom-call(s32[2]{0:T(128)S(1)} %pad_add_fusion.1.at_ref, bf16[128,512]{1,0:T(8,128)(2,1)S(1)} %collective-permute-done.7.one, bf16[128,512]{1,0:T(8,128)(2,1)S(1)} %collective-permute-done.10.two, ...), custom_call_target="tpu_custom_call" | custom-call | flops 300000000 | bytes 5000000 | tf_op jit(solution)/shard_map/gated_part/pallas_call | solution.py:444
  80.4 0.1 collective-permute-start.12
  80.5 2.7 %collective-permute-start.13 = (bf16[512,256]{1,0:T(8,128)(2,1)S(1)}, bf16[512,256]{1,0:T(8,128)(2,1)S(1)}, u32[]{:S(2)}, u32[]{:S(2)}) collective-permute-start(bf16[512,256]{1,0:T(8,128)(2,1)S(1)} %get-tuple-element.55), channel_id=1, source_target_pairs={{0,6},{1,7},{2,0},{3,1},{4,2},{5,3},{6,4},{7,5},{8,14},{9,15},{10,... | collective-permute-start | bytes 786440 | tf_op jit(solution)/shard_map/ppermute | solution.py:579
  83.1 0.6 collective-permute-start.14
  83.8 2.0 %collective-permute-start.15 = (bf16[512,256]{1,0:T(8,128)(2,1)S(1)}, bf16[512,256]{1,0:T(8,128)(2,1)S(1)}, u32[]{:S(2)}, u32[]{:S(2)}) collective-permute-start(bf16[512,256]{1,0:T(8,128)(2,1)S(1)} %get-tuple-element.53.refs_8_), channel_id=1, source_target_pairs={{0,1},{1,0},{2,3},{3,2},{4,5},{5,4},{6,7},{7,6},{8,9},{9,8},{10,11... | collective-permute-start | bytes 786440 | tf_op jit(solution)/shard_map/ppermute | solution.py:582
  85.8 2.5 %collective-permute-done.12.refs_9_ = bf16[512,256]{1,0:T(8,128)(2,1)S(1)} collective-permute-done((bf16[512,256]{1,0:T(8,128)(2,1)S(1)}, bf16[512,256]{1,0:T(8,128)(2,1)S(1)}, u32[]{:S(2)}, u32[]{:S(2)}) %collective-permute-start.12) | collective-permute-done | bytes 262176 | tf_op jit(solution)/shard_map/ppermute | solution.py:579
  88.3 3.4 %collective-permute-start.16 = (bf16[512,256]{1,0:T(8,128)(2,1)S(1)}, bf16[512,256]{1,0:T(8,128)(2,1)S(1)}, u32[]{:S(2)}, u32[]{:S(2)}) collective-permute-start(bf16[512,256]{1,0:T(8,128)(2,1)S(1)} %collective-permute-done.12.refs_9_), channel_id=1, source_target_pairs={{0,1},{1,0},{2,3},{3,2},{4,5},{5,4},{6,7},{7,6},{8,9},{9,8},{10,11... | collective-permute-start | bytes 786440 | tf_op jit(solution)/shard_map/ppermute | solution.py:582
  91.8 0.0 collective-permute-done.13.refs_10_
  91.8 3.5 %collective-permute-start.17 = (bf16[512,256]{1,0:T(8,128)(2,1)S(1)}, bf16[512,256]{1,0:T(8,128)(2,1)S(1)}, u32[]{:S(2)}, u32[]{:S(2)}) collective-permute-start(bf16[512,256]{1,0:T(8,128)(2,1)S(1)} %collective-permute-done.13.refs_10_), channel_id=1, source_target_pairs={{0,1},{1,0},{2,3},{3,2},{4,5},{5,4},{6,7},{7,6},{8,9},{9,8},{10,11... | collective-permute-start | bytes 786440 | tf_op jit(solution)/shard_map/ppermute | solution.py:582
  95.3 0.0 collective-permute-done.14.refs_11_
  95.3 1.3 %collective-permute-start.18 = (bf16[512,256]{1,0:T(8,128)(2,1)S(1)}, bf16[512,256]{1,0:T(8,128)(2,1)S(1)}, u32[]{:S(2)}, u32[]{:S(2)}) collective-permute-start(bf16[512,256]{1,0:T(8,128)(2,1)S(1)} %collective-permute-done.14.refs_11_), channel_id=1, source_target_pairs={{0,1},{1,0},{2,3},{3,2},{4,5},{5,4},{6,7},{7,6},{8,9},{9,8},{10,11... | collective-permute-start | bytes 786440 | tf_op jit(solution)/shard_map/ppermute | solution.py:582
  96.6 0.0 collective-permute-done.15.refs_12_
  96.6 0.0 collective-permute-done.16.refs_13_
  96.6 0.0 collective-permute-done.17.refs_14_
  96.6 1.1 collective-permute-done.18.refs_15_
  97.8 5.1 %mixed_part.1 = (bf16[288,512]{1,0:T(8,128)(2,1)S(1)}, bf16[288,512]{1,0:T(8,128)(2,1)S(1)}, bf16[288,512]{1,0:T(8,128)(2,1)S(1)}, bf16[288,512]{1,0:T(8,128)(2,1)S(1)}) custom-call(s32[2]{0:T(128)S(1)} %pad_add_fusion.at_ref, bf16[2304,256]{1,0:T(8,128)(2,1)S(1)} %constant_dynamic-update-slice_fusion.refs_0_.refs_4_, ...), custom_call_target="tpu_custom_call" | custom-call | flops 2400000000 | bytes 8000000 | tf_op jit(solution)/shard_map/mixed_part/pallas_call | solution.py:515
  102.9 0.9 collective-permute-start.19
  103.9 2.8 %collective-permute-start.20 = (bf16[288,512]{1,0:T(8,128)(2,1)S(1)}, bf16[288,512]{1,0:T(8,128)(2,1)S(1)}, u32[]{:S(2)}, u32[]{:S(2)}) collective-permute-start(bf16[288,512]{1,0:T(8,128)(2,1)S(1)} %get-tuple-element.59), channel_id=1, source_target_pairs={{0,4},{1,5},{2,6},{3,7},{4,0},{5,1},{6,2},{7,3},{8,12},{9,13},{10,... | collective-permute-start | bytes 884744 | tf_op jit(solution)/shard_map/ppermute | solution.py:579
  106.6 0.0 collective-permute-start.21
  106.6 5.8 %collective-permute-done.19.refs_1_ = bf16[288,512]{1,0:T(8,128)(2,1)S(1)} collective-permute-done((bf16[288,512]{1,0:T(8,128)(2,1)S(1)}, bf16[288,512]{1,0:T(8,128)(2,1)S(1)}, u32[]{:S(2)}, u32[]{:S(2)}) %collective-permute-start.19) | collective-permute-done | bytes 294944 | tf_op jit(solution)/shard_map/ppermute | solution.py:579
  112.4 7.3 %collective-permute-done.20.refs_2_ = bf16[288,512]{1,0:T(8,128)(2,1)S(1)} collective-permute-done((bf16[288,512]{1,0:T(8,128)(2,1)S(1)}, bf16[288,512]{1,0:T(8,128)(2,1)S(1)}, u32[]{:S(2)}, u32[]{:S(2)}) %collective-permute-start.20) | collective-permute-done | bytes 294944 | tf_op jit(solution)/shard_map/ppermute | solution.py:579
  119.7 0.0 collective-permute-done.21.refs_3_
  119.7 1.6 %joined.1 = bf16[288,2048]{1,0:T(8,128)(2,1)} custom-call(s32[1]{0:T(128)} %bitcast.at_ref, bf16[288,512]{1,0:T(8,128)(2,1)S(1)} %get-tuple-element.57.refs_0_, bf16[288,512]{1,0:T(8,128)(2,1)S(1)} %collective-permute-done.19.refs_1_, bf16[288,512]{1,0:T(8,128)(2,1)S(1)} %collective-permute-done.20.refs_2_, bf16[288,512]{1,0:T(8,128)(2,1)S(1)} %collective-permute-done.21.refs_3_), custom_call_target="tpu_custom_call" | custom-call | bytes 2400000 | tf_op jit(solution)/shard_map/joined/pallas_call | solution.py:543
  (4 shorter events, 0.1 us)
Async XLA Ops:
  0.1 1.3 %copy-start.1 = (bf16[256,2304]{1,0:T(8,128)(2,1)S(1)}, bf16[256,2304]{1,0:T(8,128)(2,1)}, u32[]{:S(2)}) copy-start(bf16[256,2304]{1,0:T(8,128)(2,1)} %w_ref.2) | copy-start | bytes 3538948
  2.3 6.1 %collective-permute-start = (bf16[1152,256]{1,0:T(8,128)(2,1)S(1)}, bf16[1152,256]{1,0:T(8,128)(2,1)S(1)}, u32[]{:S(2)}, u32[]{:S(2)}) collective-permute-start(bf16[1152,256]{1,0:T(8,128)(2,1)S(1)} %get-tuple-element.34), channel_id=1, source_target_pairs={{0,1},{1,0},{2,3},{3,2},{4,5},{5,4},{6,7},{7,6},{8,9},{9,8},{10,11... | collective-permute-start | bytes 1769480 | tf_op jit(solution)/shard_map/ppermute | solution.py:582
  4.7 6.5 %collective-permute-start.1 = (bf16[16,2304]{1,0:T(8,128)(2,1)S(1)}, bf16[16,2304]{1,0:T(8,128)(2,1)S(1)}, u32[]{:S(2)}, u32[]{:S(2)}) collective-permute-start(bf16[16,2304]{1,0:T(8,128)(2,1)S(1)} %slice.9), channel_id=1, source_target_pairs={{0,8},{8,16},{16,24},{24,32},{32,40},{40,48},{48,56},{56,64},{64,7... | collective-permute-start | bytes 221192 | tf_op jit(solution)/shard_map/ppermute | solution.py:584
  8.5 34.7 %collective-permute-start.3 = (bf16[2304,256]{1,0:T(8,128)(2,1)S(1)}, bf16[2304,256]{1,0:T(8,128)(2,1)S(1)}, u32[]{:S(2)}, u32[]{:S(2)}) collective-permute-start(bf16[2304,256]{1,0:T(8,128)(2,1)S(1)} %constant_dynamic-update-slice_fusion.refs_0_.refs_4_), channel_id=1, source_target_pairs={{0,6},{1,7},{2,0},{3,1},{4,2},{5,3},{6,4},{7,5},{8,14},{9,15},{10,... | collective-permute-start | bytes 3538952 | tf_op jit(solution)/shard_map/ppermute | solution.py:579
  11.3 31.9 %collective-permute-start.2 = (bf16[2304,256]{1,0:T(8,128)(2,1)S(1)}, bf16[2304,256]{1,0:T(8,128)(2,1)S(1)}, u32[]{:S(2)}, u32[]{:S(2)}) collective-permute-start(bf16[2304,256]{1,0:T(8,128)(2,1)S(1)} %constant_dynamic-update-slice_fusion.refs_0_.refs_4_), channel_id=1, source_target_pairs={{0,2},{1,3},{2,4},{3,5},{4,6},{5,7},{6,0},{7,1},{8,10},{9,11},{10,... | collective-permute-start | bytes 3538952 | tf_op jit(solution)/shard_map/ppermute | solution.py:579
  11.3 0.6 copy-start.4
  44.9 28.6 %collective-permute-start.8 = (bf16[1152,256]{1,0:T(8,128)(2,1)}, bf16[1152,256]{1,0:T(8,128)(2,1)}, u32[]{:S(2)}, u32[]{:S(2)}) collective-permute-start(bf16[1152,256]{1,0:T(8,128)(2,1)} %slice.10), channel_id=1, source_target_pairs={{0,6},{1,7},{2,0},{3,1},{4,2},{5,3},{6,4},{7,5},{8,14},{9,15},{10,... | collective-permute-start | bytes 1769480 | tf_op jit(solution)/shard_map/ppermute | solution.py:579
  47.5 25.9 %collective-permute-start.9 = (bf16[1152,256]{1,0:T(8,128)(2,1)}, bf16[1152,256]{1,0:T(8,128)(2,1)}, u32[]{:S(2)}, u32[]{:S(2)}) collective-permute-start(bf16[1152,256]{1,0:T(8,128)(2,1)} %slice.11), channel_id=1, source_target_pairs={{0,2},{1,3},{2,4},{3,5},{4,6},{5,7},{6,0},{7,1},{8,10},{9,11},{10,... | collective-permute-start | bytes 1769480 | tf_op jit(solution)/shard_map/ppermute | solution.py:579
  47.6 6.8 %collective-permute-start.6 = (bf16[128,512]{1,0:T(8,128)(2,1)}, bf16[128,512]{1,0:T(8,128)(2,1)}, u32[]{:S(2)}, u32[]{:S(2)}) collective-permute-start(bf16[128,512]{1,0:T(8,128)(2,1)} %get-tuple-element.38.own), channel_id=1, source_target_pairs={{0,24},{8,0},{16,8},{24,16},{32,56},{40,32},{48,40},{56,48},{64,88... | collective-permute-start | bytes 393224 | tf_op jit(solution)/shard_map/ppermute | solution.py:604
  50.7 5.7 %collective-permute-start.5 = (bf16[128,512]{1,0:T(8,128)(2,1)}, bf16[128,512]{1,0:T(8,128)(2,1)}, u32[]{:S(2)}, u32[]{:S(2)}) collective-permute-start(bf16[128,512]{1,0:T(8,128)(2,1)} %get-tuple-element.38.own), channel_id=1, source_target_pairs={{0,16},{8,24},{16,0},{24,8},{32,48},{40,56},{48,32},{56,40},{64,80... | collective-permute-start | bytes 393224 | tf_op jit(solution)/shard_map/ppermute | solution.py:604
  51.0 9.2 %collective-permute-start.4 = (bf16[128,512]{1,0:T(8,128)(2,1)}, bf16[128,512]{1,0:T(8,128)(2,1)}, u32[]{:S(2)}, u32[]{:S(2)}) collective-permute-start(bf16[128,512]{1,0:T(8,128)(2,1)} %get-tuple-element.38.own), channel_id=1, source_target_pairs={{0,8},{8,16},{16,24},{24,0},{32,40},{40,48},{48,56},{56,32},{64,72... | collective-permute-start | bytes 393224 | tf_op jit(solution)/shard_map/ppermute | solution.py:604
  61.8 11.6 %collective-permute-start.11 = (bf16[128,512]{1,0:T(8,128)(2,1)S(1)}, bf16[128,512]{1,0:T(8,128)(2,1)S(1)}, u32[]{:S(2)}, u32[]{:S(2)}) collective-permute-start(bf16[128,512]{1,0:T(8,128)(2,1)S(1)} %get-tuple-element.39), channel_id=1, source_target_pairs={{0,96},{8,104},{16,112},{24,120},{32,0},{40,8},{48,16},{56,24},{64... | collective-permute-start | bytes 393224 | tf_op jit(solution)/shard_map/ppermute | solution.py:608
  64.4 9.1 %collective-permute-start.10 = (bf16[128,512]{1,0:T(8,128)(2,1)S(1)}, bf16[128,512]{1,0:T(8,128)(2,1)S(1)}, u32[]{:S(2)}, u32[]{:S(2)}) collective-permute-start(bf16[128,512]{1,0:T(8,128)(2,1)S(1)} %get-tuple-element.39), channel_id=1, source_target_pairs={{0,64},{8,72},{16,80},{24,88},{32,96},{40,104},{48,112},{56,120},{... | collective-permute-start | bytes 393224 | tf_op jit(solution)/shard_map/ppermute | solution.py:608
  64.9 8.5 %collective-permute-start.7 = (bf16[128,512]{1,0:T(8,128)(2,1)S(1)}, bf16[128,512]{1,0:T(8,128)(2,1)S(1)}, u32[]{:S(2)}, u32[]{:S(2)}) collective-permute-start(bf16[128,512]{1,0:T(8,128)(2,1)S(1)} %get-tuple-element.39), channel_id=1, source_target_pairs={{0,32},{8,40},{16,48},{24,56},{32,64},{40,72},{48,80},{56,88},{64,... | collective-permute-start | bytes 393224 | tf_op jit(solution)/shard_map/ppermute | solution.py:608
  73.4 1.6 %copy-start = (f32[2048,256]{1,0:T(8,128)S(1)}, f32[2048,256]{1,0:T(8,128)}, u32[]{:S(2)}) copy-start(f32[2048,256]{1,0:T(8,128)} %get-tuple-element.50.o_ref) | copy-start | bytes 6291460
  75.0 1.2 %copy-start.2 = (bf16[2048,256]{1,0:T(8,128)(2,1)S(1)}, bf16[2048,256]{1,0:T(8,128)(2,1)}, u32[]{:S(2)}) copy-start(bf16[2048,256]{1,0:T(8,128)(2,1)} %get-tuple-element.51.r_ref) | copy-start | bytes 3145732
  76.3 1.2 %copy-start.3 = (bf16[2048,256]{1,0:T(8,128)(2,1)S(1)}, bf16[2048,256]{1,0:T(8,128)(2,1)}, u32[]{:S(2)}) copy-start(bf16[2048,256]{1,0:T(8,128)(2,1)} %get-tuple-element.52.s_ref) | copy-start | bytes 3145732
  80.4 7.9 %collective-permute-start.12 = (bf16[512,256]{1,0:T(8,128)(2,1)S(1)}, bf16[512,256]{1,0:T(8,128)(2,1)S(1)}, u32[]{:S(2)}, u32[]{:S(2)}) collective-permute-start(bf16[512,256]{1,0:T(8,128)(2,1)S(1)} %get-tuple-element.54), channel_id=1, source_target_pairs={{0,2},{1,3},{2,4},{3,5},{4,6},{5,7},{6,0},{7,1},{8,10},{9,11},{10,... | collective-permute-start | bytes 786440 | tf_op jit(solution)/shard_map/ppermute | solution.py:579
  80.5 11.3 %collective-permute-start.13 = (bf16[512,256]{1,0:T(8,128)(2,1)S(1)}, bf16[512,256]{1,0:T(8,128)(2,1)S(1)}, u32[]{:S(2)}, u32[]{:S(2)}) collective-permute-start(bf16[512,256]{1,0:T(8,128)(2,1)S(1)} %get-tuple-element.55), channel_id=1, source_target_pairs={{0,6},{1,7},{2,0},{3,1},{4,2},{5,3},{6,4},{7,5},{8,14},{9,15},{10,... | collective-permute-start | bytes 786440 | tf_op jit(solution)/shard_map/ppermute | solution.py:579
  83.1 12.1 %collective-permute-start.14 = (bf16[512,256]{1,0:T(8,128)(2,1)S(1)}, bf16[512,256]{1,0:T(8,128)(2,1)S(1)}, u32[]{:S(2)}, u32[]{:S(2)}) collective-permute-start(bf16[512,256]{1,0:T(8,128)(2,1)S(1)} %get-tuple-element.56), channel_id=1, source_target_pairs={{0,4},{1,5},{2,6},{3,7},{4,0},{5,1},{6,2},{7,3},{8,12},{9,13},{10,... | collective-permute-start | bytes 786440 | tf_op jit(solution)/shard_map/ppermute | solution.py:579
  83.8 12.9 %collective-permute-start.15 = (bf16[512,256]{1,0:T(8,128)(2,1)S(1)}, bf16[512,256]{1,0:T(8,128)(2,1)S(1)}, u32[]{:S(2)}, u32[]{:S(2)}) collective-permute-start(bf16[512,256]{1,0:T(8,128)(2,1)S(1)} %get-tuple-element.53.refs_8_), channel_id=1, source_target_pairs={{0,1},{1,0},{2,3},{3,2},{4,5},{5,4},{6,7},{7,6},{8,9},{9,8},{10,11... | collective-permute-start | bytes 786440 | tf_op jit(solution)/shard_map/ppermute | solution.py:582
  88.3 8.3 %collective-permute-start.16 = (bf16[512,256]{1,0:T(8,128)(2,1)S(1)}, bf16[512,256]{1,0:T(8,128)(2,1)S(1)}, u32[]{:S(2)}, u32[]{:S(2)}) collective-permute-start(bf16[512,256]{1,0:T(8,128)(2,1)S(1)} %collective-permute-done.12.refs_9_), channel_id=1, source_target_pairs={{0,1},{1,0},{2,3},{3,2},{4,5},{5,4},{6,7},{7,6},{8,9},{9,8},{10,11... | collective-permute-start | bytes 786440 | tf_op jit(solution)/shard_map/ppermute | solution.py:582
  91.8 4.9 %collective-permute-start.17 = (bf16[512,256]{1,0:T(8,128)(2,1)S(1)}, bf16[512,256]{1,0:T(8,128)(2,1)S(1)}, u32[]{:S(2)}, u32[]{:S(2)}) collective-permute-start(bf16[512,256]{1,0:T(8,128)(2,1)S(1)} %collective-permute-done.13.refs_10_), channel_id=1, source_target_pairs={{0,1},{1,0},{2,3},{3,2},{4,5},{5,4},{6,7},{7,6},{8,9},{9,8},{10,11... | collective-permute-start | bytes 786440 | tf_op jit(solution)/shard_map/ppermute | solution.py:582
  95.3 2.5 %collective-permute-start.18 = (bf16[512,256]{1,0:T(8,128)(2,1)S(1)}, bf16[512,256]{1,0:T(8,128)(2,1)S(1)}, u32[]{:S(2)}, u32[]{:S(2)}) collective-permute-start(bf16[512,256]{1,0:T(8,128)(2,1)S(1)} %collective-permute-done.14.refs_11_), channel_id=1, source_target_pairs={{0,1},{1,0},{2,3},{3,2},{4,5},{5,4},{6,7},{7,6},{8,9},{9,8},{10,11... | collective-permute-start | bytes 786440 | tf_op jit(solution)/shard_map/ppermute | solution.py:582
  102.9 9.5 %collective-permute-start.19 = (bf16[288,512]{1,0:T(8,128)(2,1)S(1)}, bf16[288,512]{1,0:T(8,128)(2,1)S(1)}, u32[]{:S(2)}, u32[]{:S(2)}) collective-permute-start(bf16[288,512]{1,0:T(8,128)(2,1)S(1)} %get-tuple-element.58), channel_id=1, source_target_pairs={{0,2},{1,3},{2,4},{3,5},{4,6},{5,7},{6,0},{7,1},{8,10},{9,11},{10,... | collective-permute-start | bytes 884744 | tf_op jit(solution)/shard_map/ppermute | solution.py:579
  103.9 15.8 %collective-permute-start.20 = (bf16[288,512]{1,0:T(8,128)(2,1)S(1)}, bf16[288,512]{1,0:T(8,128)(2,1)S(1)}, u32[]{:S(2)}, u32[]{:S(2)}) collective-permute-start(bf16[288,512]{1,0:T(8,128)(2,1)S(1)} %get-tuple-element.59), channel_id=1, source_target_pairs={{0,4},{1,5},{2,6},{3,7},{4,0},{5,1},{6,2},{7,3},{8,12},{9,13},{10,... | collective-permute-start | bytes 884744 | tf_op jit(solution)/shard_map/ppermute | solution.py:579
  106.6 13.1 %collective-permute-start.21 = (bf16[288,512]{1,0:T(8,128)(2,1)S(1)}, bf16[288,512]{1,0:T(8,128)(2,1)S(1)}, u32[]{:S(2)}, u32[]{:S(2)}) collective-permute-start(bf16[288,512]{1,0:T(8,128)(2,1)S(1)} %get-tuple-element.60), channel_id=1, source_target_pairs={{0,6},{1,7},{2,0},{3,1},{4,2},{5,3},{6,4},{7,5},{8,14},{9,15},{10,... | collective-permute-start | bytes 884744 | tf_op jit(solution)/shard_map/ppermute | solution.py:579

commit v3 on v2

--- a/solution.py
+++ b/solution.py
@@ -48,22 +48,20 @@
     x_ref,
     halo_ref,
     gain_ref,
-    w_ref,
+    wk_ref,
+    wv_ref,
     conv_ref,
-    down_ref,
     g_ref,
     b_ref,
-    low_ref,
-    m_ref,
-    q_ref,
+    scale,
+    kf_ref,
+    rise_ref,
+    pos_ref,
     u_ref,
     w_out_ref,
     z_ref,
     fin_ref,
     wide,
-    narrow,
-    low,
-    scale,
     fresh,
     proj,
     state,
@@ -78,10 +76,7 @@
 
         def product(i, r):
             at = pl.ds(r * block, block)
-            p = mm(x_ref[at, :], wide[i] if i < 3 else narrow[...])
-            if i == 3:
-                low[at, :] = p
-                return
+            p = mm(x_ref[at, :], wide[i])
             for h in range(2):
                 fresh[i, h, at, :] = p[:, h * W : (h + 1) * W]
 
@@ -94,12 +89,11 @@
         def apply(r):
             at = pl.ds(r * C, C)
             to = pl.ds(8 + r * C, C)
-            for i in range(3):
+            for i in range(2):
                 for h in range(2):
                     proj[i, h, to, :] = fresh[i, h, at, :] * scale[at, :]
-            low_ref[at, :] = (low[at, :] * scale[at, :]).astype(BF16)
-
-        products = [functools.partial(product, i, r) for i in range(4) for r in range(4)]
+
+        products = [functools.partial(product, i, r) for i in range(2) for r in range(4)]
         roots = [functools.partial(root, r) for r in chunks]
         return products, roots, [functools.partial(apply, r) for r in chunks]
 
@@ -124,7 +118,7 @@
                 total = None
                 for j in range(4):
                     part = (
-                        taps[i, j : j + 1, h * W : (h + 1) * W]
+                        taps[i + 1, j : j + 1, h * W : (h + 1) * W]
                         * proj[i, h, pl.ds(5 + j + c * C, C), :]
                     )
                     total = part if total is None else total + part
@@ -151,7 +145,7 @@
             cum.append(mm(tri, jnp.concatenate([hi, lo], axis=0)))
         k = []
         for c in chunks:
-            k.append(unit(conv(1, c)))
+            k.append(unit(conv(0, c)))
         mid = [a[C // 2 - 1 : C // 2, :] for a in cum]
         last = [a[C - 1 : C, :] for a in cum]
         rise = [jnp.exp(cum[c] - mid[c]) for c in chunks]
@@ -160,22 +154,15 @@
         to_end = [jnp.exp(last[c] - mid[c]) for c in chunks]
         kr = [k[c] * rise[c] for c in chunks]
         kf = [k[c] * fall[c] for c in chunks]
-        qr = []
-        for c in chunks:
-            qr.append(unit(conv(0, c), W**-0.5) * rise[c])
-        v16 = [jnp.concatenate(conv(2, c), axis=1).astype(BF16) for c in chunks]
-        pairs = [
-            mm_nt(
-                jnp.concatenate([kr[c].astype(BF16), qr[c].astype(BF16)], axis=0),
-                bd(kf[c].astype(BF16)),
-            )
-            for c in chunks
-        ]
-        lower = [jnp.where(strict, pairs[c][:C] * beta[c], 0.0) for c in chunks]
+        v16 = [jnp.concatenate(conv(1, c), axis=1).astype(BF16) for c in chunks]
+        kf16 = [a.astype(BF16) for a in kf]
+        pairs = [mm_nt(kr[c].astype(BF16), bd(kf16[c])) for c in chunks]
+        lower = [jnp.where(strict, pairs[c] * beta[c], 0.0) for c in chunks]
         for c in chunks:
             at = pl.ds(c * C, C)
-            m_ref[at, :] = jnp.where(inclusive, pairs[c][C:] * beta[c], 0.0).astype(BF16)
-            q_ref[at, :] = (qr[c] * from_start[c]).astype(BF16)
+            kf_ref[at, :] = kf16[c]
+            rise_ref[at, :] = rise[c].astype(BF16)
+            pos_ref[at, :] = (rise[c] * from_start[c]).astype(BF16)
 
         two = (rows // 2 == cols // 2) & strict
         eye = (rows == cols).astype(F32)
@@ -244,12 +231,11 @@
         for j in range(gain.shape[1]):
             at = pl.ds(j * W, W)
             column = gain[:, j : j + 1]
-            for i in range(3):
-                wide[i, at, :] = (w_ref[i, at, :].astype(F32) * column).astype(BF16)
-            narrow[at, :] = (down_ref[at, :].astype(F32) * column).astype(BF16)
+            for i, w_ref in enumerate((wk_ref, wv_ref)):
+                wide[i, at, :] = (w_ref[0, at, :].astype(F32) * column).astype(BF16)
         rows = halo_ref[...].astype(F32)
         ms = jnp.mean(rows * rows, axis=-1, keepdims=True)
-        for i in range(3):
+        for i in range(2):
             p = (mm(halo_ref[...], wide[i]) * lax.rsqrt(ms + 1e-06))[8:16]
             for h in range(2):
                 proj[i, h, 0:8, :] = p[:, h * W : (h + 1) * W]
@@ -271,9 +257,8 @@
         fin_ref[...] = state[...].astype(BF16)
 
 
-def local_part(x, halo, gain, qkv, conv, down, g, b):
+def local_part(x, halo, gain, qkv, conv, g, b):
     tokens, d = x.shape
-    rank = down.shape[1]
     grid = tokens // TILE
     whole = lambda *shape: pl.BlockSpec(shape, lambda i: (0,) * len(shape))
     first = lambda i: jnp.minimum(i, grid - 1)
@@ -287,45 +272,177 @@
             early(d),
             whole(16, d),
             whole(d // W, W),
-            whole(3, d, 2 * W),
+            pl.BlockSpec((1, d, 2 * W), lambda i: (1, 0, 0)),
+            pl.BlockSpec((1, d, 2 * W), lambda i: (2, 0, 0)),
+            whole(3, 4, 2 * W),
+            pl.BlockSpec((2, TILE, W), lambda i: (0, then(i), 0)),
+            pl.BlockSpec((2, TILE), lambda i: (0, then(i))),
+        ],
+        out_specs=[early(W)] + [rows(2 * W)] * 5 + [rows(4 * W), whole(W, 4 * W)],
+        out_shape=[
+            jax.ShapeDtypeStruct((tokens, W), F32),
+            jax.ShapeDtypeStruct((tokens, 2 * W), BF16),
+            jax.ShapeDtypeStruct((tokens, 2 * W), BF16),
+            jax.ShapeDtypeStruct((tokens, 2 * W), BF16),
+            jax.ShapeDtypeStruct((tokens, 2 * W), BF16),
+            jax.ShapeDtypeStruct((tokens, 2 * W), BF16),
+            jax.ShapeDtypeStruct((tokens, 4 * W), BF16),
+            jax.ShapeDtypeStruct((W, 4 * W), BF16),
+        ],
+        scratch_shapes=[
+            pltpu.VMEM((2, d, 2 * W), BF16),
+            pltpu.VMEM((2, 2, TILE, W), F32),
+            pltpu.VMEM((2, 2, TILE + 8, W), F32),
+            pltpu.VMEM((W, 4 * W), F32),
+        ],
+        compiler_params=pltpu.CompilerParams(vmem_limit_bytes=56 * MIB),
+        cost_estimate=pl.CostEstimate(
+            flops=14_000_000_000, bytes_accessed=24_000_000, transcendentals=6_000_000
+        ),
+        name="local_part",
+    )(x, halo, gain, qkv, qkv, conv, g, b)
+
+
+def query_kernel(
+    x_ref,
+    halo_ref,
+    gain_ref,
+    w_ref,
+    conv_ref,
+    down_ref,
+    kf_ref,
+    rise_ref,
+    pos_ref,
+    b_ref,
+    scale_ref,
+    low_ref,
+    m_ref,
+    q_ref,
+    wide,
+    narrow,
+    raw,
+    proj,
+):
+    step = pl.program_id(0)
+    tiles = pl.num_programs(0) - 1
+    n = TILE // C
+
+    def root(rows):
+        wide_rows = rows.astype(F32)
+        return lax.rsqrt(jnp.mean(wide_rows * wide_rows, axis=-1, keepdims=True) + 1e-06)
+
+    def products():
+        def queries():
+            raw[...] = mm(x_ref[...], wide[...])
+
+        def lowered():
+            low = mm(x_ref[...], narrow[...])
+            low_ref[...] = (low * scale_ref[...]).astype(BF16)
+
+        return [queries, lowered]
+
+    def keep():
+        for h in range(2):
+            proj[h, 8:, :] = raw[:, h * W : (h + 1) * W] * scale_ref[...]
+
+    def finish(parts):
+        parts = list(parts)
+        taps = conv_ref[0].astype(F32)
+        rows = lax.broadcasted_iota(jnp.int32, (C, 2 * C), 0)
+        cols = lax.broadcasted_iota(jnp.int32, (C, 2 * C), 1) % C
+        inclusive = cols <= rows
+        for c in range(n):
+            if parts:
+                parts.pop(0)()
+            at = pl.ds(c * C, C)
+            halves = []
+            for h in range(2):
+                total = None
+                for j in range(4):
+                    part = (
+                        taps[j : j + 1, h * W : (h + 1) * W]
+                        * proj[h, pl.ds(5 + j + c * C, C), :]
+                    )
+                    total = part if total is None else total + part
+                f = total * pl.reciprocal(1.0 + jnp.exp(-total), approx=True)
+                size = lax.rsqrt(jnp.sum(f * f, axis=-1, keepdims=True) + 1e-06)
+                halves.append(f * (size * W**-0.5))
+            query = jnp.concatenate(halves, axis=1)
+            risen = (query * rise_ref[at, :].astype(F32)).astype(BF16)
+            q_ref[at, :] = (query * pos_ref[at, :].astype(F32)).astype(BF16)
+            beta = jnp.concatenate([b_ref[0:1, at], b_ref[1:2, at]], axis=1)
+            pairs = mm_nt(risen, bd(kf_ref[at, :]))
+            m_ref[at, :] = jnp.where(inclusive, pairs * beta, 0.0).astype(BF16)
+
+    @pl.when(step == 0)
+    def _():
+        gain = gain_ref[...].T
+        for j in range(gain.shape[1]):
+            at = pl.ds(j * W, W)
+            column = gain[:, j : j + 1]
+            wide[at, :] = (w_ref[0, at, :].astype(F32) * column).astype(BF16)
+            narrow[at, :] = (down_ref[at, :].astype(F32) * column).astype(BF16)
+        p = (mm(halo_ref[...], wide[...]) * root(halo_ref[...]))[8:16]
+        for h in range(2):
+            proj[h, 0:8, :] = p[:, h * W : (h + 1) * W]
+        for part in products():
+            part()
+        keep()
+
+    @pl.when((step > 0) & (step < tiles))
+    def _():
+        finish(products())
+        proj[:, 0:8, :] = proj[:, TILE : TILE + 8, :]
+        keep()
+
+    @pl.when(step == tiles)
+    def _():
+        finish([])
+
+
+def query_part(x, halo, gain, qkv, conv, down, kf, rise, pos, b, scale):
+    tokens, d = x.shape
+    rank = down.shape[1]
+    whole = lambda *shape: pl.BlockSpec(shape, lambda i: (0,) * len(shape))
+    grid = tokens // TILE
+    first = lambda i: jnp.minimum(i, grid - 1)
+    then = lambda i: jnp.maximum(i - 1, 0)
+    early = lambda width: pl.BlockSpec((TILE, width), lambda i: (first(i), 0))
+    rows = lambda width: pl.BlockSpec((TILE, width), lambda i: (then(i), 0))
+    return pl.pallas_call(
+        query_kernel,
+        grid=(grid + 1,),
+        in_specs=[
+            early(d),
+            whole(16, d),
+            whole(d // W, W),
+            whole(1, d, 2 * W),
             whole(3, 4, 2 * W),
             whole(d, rank),
-            pl.BlockSpec((2, TILE, W), lambda i: (0, then(i), 0)),
-            pl.BlockSpec((2, TILE), lambda i: (0, then(i))),
-        ],
-        out_specs=[
-            early(rank),
             rows(2 * W),
             rows(2 * W),
             rows(2 * W),
-            rows(2 * W),
-            rows(4 * W),
-            whole(W, 4 * W),
-        ],
+            pl.BlockSpec((2, TILE), lambda i: (0, then(i))),
+            early(W),
+        ],
+        out_specs=[early(rank), rows(2 * W), rows(2 * W)],
         out_shape=[
             jax.ShapeDtypeStruct((tokens, rank), BF16),
             jax.ShapeDtypeStruct((tokens, 2 * W), BF16),
             jax.ShapeDtypeStruct((tokens, 2 * W), BF16),
-            jax.ShapeDtypeStruct((tokens, 2 * W), BF16),
-            jax.ShapeDtypeStruct((tokens, 2 * W), BF16),
-            jax.ShapeDtypeStruct((tokens, 4 * W), BF16),
-            jax.ShapeDtypeStruct((W, 4 * W), BF16),
         ],
         scratch_shapes=[
-            pltpu.VMEM((3, d, 2 * W), BF16),
+            pltpu.VMEM((d, 2 * W), BF16),
             pltpu.VMEM((d, rank), BF16),
-            pltpu.VMEM((TILE, rank), F32),
-            pltpu.VMEM((TILE, W), F32),
-            pltpu.VMEM((3, 2, TILE, W), F32),
-            pltpu.VMEM((3, 2, TILE + 8, W), F32),
-            pltpu.VMEM((W, 4 * W), F32),
+            pltpu.VMEM((TILE, 2 * W), F32),
+            pltpu.VMEM((2, TILE + 8, W), F32),
         ],
         compiler_params=pltpu.CompilerParams(vmem_limit_bytes=56 * MIB),
         cost_estimate=pl.CostEstimate(
-            flops=14_000_000_000, bytes_accessed=24_000_000, transcendentals=6_000_000
-        ),
-        name="local_part",
-    )(x, halo, gain, qkv, conv, down, g, b)
+            flops=4_000_000_000, bytes_accessed=17_000_000, transcendentals=1_000_000
+        ),
+        name="query_part",
+    )(x, halo, gain, qkv, conv, down, kf, rise, pos, b, scale)
 
 
 def reading_kernel(m_ref, q_ref, u_ref, w_ref, z_ref, low_ref, up_ref, gain_ref, o_ref, r_ref, s_ref):
@@ -336,7 +453,7 @@
     mw = [mm(ms[c], bd(w_ref[ats[c], :])) for c in range(n)]
     rd = [(q_ref[ats[c], :].astype(F32) - mw[c]).astype(BF16) for c in range(n)]
     for c in range(n):
-        o_ref[ats[c], :] = mu[c] + mm(rd[c], bd(z_ref[ats[c], : 2 * W]))
+        o_ref[ats[c], :] = (mu[c] + mm(rd[c], bd(z_ref[ats[c], : 2 * W]))).astype(BF16)
         r_ref[ats[c], :] = mm(rd[c], bd(z_ref[ats[c], 2 * W :])).astype(BF16)
     gate = mm(low_ref[...], up_ref[...])
     s_ref[...] = (
@@ -356,7 +473,7 @@
         + [rows(4 * W), rows(rank), whole(rank, 2 * W), whole(1, 2 * W)],
         out_specs=[rows(2 * W)] * 3,
         out_shape=[
-            jax.ShapeDtypeStruct((tokens, 2 * W), F32),
+            jax.ShapeDtypeStruct((tokens, 2 * W), BF16),
             jax.ShapeDtypeStruct((tokens, 2 * W), BF16),
             jax.ShapeDtypeStruct((tokens, 2 * W), BF16),
         ],
@@ -410,53 +527,50 @@
     )(zi, own, one, two, three)
 
 
-def gated_kernel(at_ref, one, two, three, pre, o_ref, r_ref, s_ref, *rest):
-    outs, start = rest[:-1], rest[-1]
-    step = pl.program_id(0)
-
-    @pl.when(step == 0)
-    def _():
-        xi = at_ref[0]
-        s = jnp.zeros((W, 2 * W), F32)
-        for d, ref in ((3, three), (2, two), (1, one)):
-            nxt = ref[:, : 2 * W].astype(F32) + mm(ref[:, 2 * W :], bd(s.astype(BF16)))
-            s = jnp.where(xi >= d, nxt, s)
-        s = pre[:, : 2 * W].astype(F32) + mm(pre[:, 2 * W :], bd(s.astype(BF16)))
-        start[...] = bd(s.astype(BF16))
-
-    att = o_ref[...] + mm(r_ref[...], start[...])
-    scale = per_head(
-        att, lambda h: lax.rsqrt(jnp.mean(h * h, axis=-1, keepdims=True) + 1e-05)
-    )
-    gated = (att * scale * s_ref[...].astype(F32)).astype(BF16)
+def gated_kernel(at_ref, one, two, three, pre, o_hbm, r_hbm, s_hbm, *rest):
+    outs, (o_ref, r_ref, s_ref, sems) = rest[:4], rest[4:]
+    xi, yi = at_ref[0], at_ref[1]
+    copies = [
+        pltpu.make_async_copy(src, dst, sems.at[i])
+        for i, (src, dst) in enumerate(((r_hbm, r_ref), (o_hbm, o_ref), (s_hbm, s_ref)))
+    ]
+    for copy in copies:
+        copy.start()
+    s = jnp.zeros((W, 2 * W), F32)
+    for d, ref in ((3, three), (2, two), (1, one)):
+        nxt = ref[:, : 2 * W].astype(F32) + mm(ref[:, 2 * W :], bd(s.astype(BF16)))
+        s = jnp.where(xi >= d, nxt, s)
+    s = pre[:, : 2 * W].astype(F32) + mm(pre[:, 2 * W :], bd(s.astype(BF16)))
+    start = bd(s.astype(BF16))
+    for copy in copies:
+        copy.wait()
     for d, out in enumerate(outs):
-
-        @pl.when(step == d)
-        def _():
-            out[...] = gated
+        here = lax.rem(yi + d, 4)
+        att = o_ref[here].astype(F32) + mm(r_ref[here], start)
+        scale = per_head(
+            att, lambda h: lax.rsqrt(jnp.mean(h * h, axis=-1, keepdims=True) + 1e-05)
+        )
+        out[...] = (att * scale * s_ref[here].astype(F32)).astype(BF16)
 
 
 def gated_part(at, one, two, three, pre, o, r, s):
     part = o.shape[0] // 4
-    whole = pl.BlockSpec((W, 4 * W), lambda i, at: (0, 0))
-    rows = pl.BlockSpec((part, 2 * W), lambda i, at: (lax.rem(at[1] + i, 4), 0))
-    keep = pl.BlockSpec((part, 2 * W), lambda i, at: (0, 0))
+    vmem = pl.BlockSpec(memory_space=pltpu.VMEM)
     return pl.pallas_call(
         gated_kernel,
-        grid_spec=pltpu.PrefetchScalarGridSpec(
-            num_scalar_prefetch=1,
-            grid=(4,),
-            in_specs=[whole] * 4 + [rows] * 3,
-            out_specs=[keep] * 4,
-            scratch_shapes=[pltpu.VMEM((2 * W, 2 * W), BF16)],
-        ),
+        in_specs=[pl.BlockSpec(memory_space=pltpu.SMEM)]
+        + [vmem] * 4
+        + [pl.BlockSpec(memory_space=pltpu.HBM)] * 3,
+        out_specs=[vmem] * 4,
         out_shape=[jax.ShapeDtypeStruct((part, 2 * W), BF16)] * 4,
-        compiler_params=pltpu.CompilerParams(vmem_limit_bytes=10 * MIB),
+        scratch_shapes=[pltpu.VMEM((4, part, 2 * W), BF16)] * 3
+        + [pltpu.SemaphoreType.DMA((3,))],
+        compiler_params=pltpu.CompilerParams(vmem_limit_bytes=56 * MIB),
         cost_estimate=pl.CostEstimate(
-            flops=300_000_000, bytes_accessed=5_000_000, transcendentals=10_000
+            flops=300_000_000, bytes_accessed=4_000_000, transcendentals=10_000
         ),
         name="gated_part",
-    )(at, one, two, three, pre, o, r, s)
+    )(at, one, two, three, pre, *(a.reshape(4, part, 2 * W) for a in (o, r, s)))
 
 
 def turned_kernel(at_ref, w_ref, mine_ref, other_ref, held):
@@ -490,64 +604,67 @@
 
 
 def mixed_kernel(at_ref, *refs):
-    step = pl.program_id(0)
+    del at_ref
     weights, blocks, outs = refs[:8], refs[8:16], refs[16:]
     total = None
     for w, g in zip(weights, blocks, strict=True):
         part = mm_nt(w[...], g[...])
         total = part if total is None else total + part
     total = total.astype(BF16)
-    for d, out in enumerate(outs):
-
-        @pl.when(step == d)
+    for i, out in enumerate(outs):
+
+        @pl.when(pl.program_id(0) == i)
         def _():
             out[...] = total
 
 
-def mixed_part(at, weights, mine, theirs):
-    features = weights[0].shape[0] // 8
+def mixed_part(distances, at, weights, mine, theirs):
+    features = weights[0][0].shape[0] // weights[0][2]
     tokens = mine[0].shape[0]
-    wspec = lambda first: pl.BlockSpec(
-        (features, 2 * W), lambda i, at: (first + lax.rem(at[0] + i, 4), 0)
-    )
+    first, step = distances[0], (distances[1] - distances[0] if len(distances) > 1 else 0)
+
+    def wspec(base):
+        return pl.BlockSpec(
+            (features, 2 * W),
+            lambda i, at: (base + lax.rem(at[0] + first + step * i, 4), 0),
+        )
+
     gspec = pl.BlockSpec((tokens, 2 * W), lambda i, at: (0, 0))
     ospec = pl.BlockSpec((features, tokens), lambda i, at: (0, 0))
     return pl.pallas_call(
         mixed_kernel,
         grid_spec=pltpu.PrefetchScalarGridSpec(
             num_scalar_prefetch=1,
-            grid=(4,),
-            in_specs=[wspec(0)] * 4 + [wspec(4)] * 3 + [wspec(0)] + [gspec] * 8,
-            out_specs=[ospec] * 4,
-        ),
-        out_shape=[jax.ShapeDtypeStruct((features, tokens), BF16)] * 4,
+            grid=(len(distances),),
+            in_specs=[wspec(base) for _, base, _ in weights] + [gspec] * 8,
+            out_specs=[ospec] * len(distances),
+        ),
+        out_shape=[jax.ShapeDtypeStruct((features, tokens), BF16)] * len(distances),
         compiler_params=pltpu.CompilerParams(vmem_limit_bytes=16 * MIB),
         cost_estimate=pl.CostEstimate(
-            flops=2_400_000_000, bytes_accessed=8_000_000, transcendentals=0
+            flops=600_000_000 * len(distances),
+            bytes_accessed=2_000_000 + 1_500_000 * len(distances),
+            transcendentals=0,
         ),
         name="mixed_part",
-    )(at, *weights, *mine, *theirs)
+    )(at, *(a for a, _, _ in weights), *mine, *theirs)
 
 
 def joined_kernel(at_ref, *refs):
-    step = pl.program_id(0)
+    out = refs[-1]
+    tokens = refs[0].shape[1]
     for d, piece in enumerate(refs[:-1]):
-
-        @pl.when(lax.rem(at_ref[0] - d + 4, 4) == step)
-        def _():
-            refs[-1][...] = piece[...]
+        to = lax.rem(at_ref[0] - d + 4, 4) * tokens
+        out[:, pl.ds(pl.multiple_of(to, tokens), tokens)] = piece[...]
 
 
 def joined(at, pieces):
     features, tokens = pieces[0].shape
+    vmem = pl.BlockSpec(memory_space=pltpu.VMEM)
     return pl.pallas_call(
         joined_kernel,
-        grid_spec=pltpu.PrefetchScalarGridSpec(
-            num_scalar_prefetch=1,
-            grid=(4,),
-            in_specs=[pl.BlockSpec((features, tokens), lambda i, at: (0, 0))] * 4,
-            out_specs=pl.BlockSpec((features, tokens), lambda i, at: (0, i)),
-        ),
+        in_specs=[pl.BlockSpec(memory_space=pltpu.SMEM)] + [vmem] * 4,
+        out_specs=vmem,
         out_shape=jax.ShapeDtypeStruct((features, 4 * tokens), BF16),
         compiler_params=pltpu.CompilerParams(vmem_limit_bytes=10 * MIB),
         cost_estimate=pl.CostEstimate(
@@ -581,22 +698,16 @@
     def across(a):
         return lax.ppermute(a, "head", [(i, i ^ 1) for i in range(8)])
 
+    here = jnp.stack([yi, ci])
+    mine, other = turned(here, out_weight)
     halo = lax.ppermute(
         activations[tokens - 16 :], "ctx", [(i, i + 1) for i in range(15)]
     )
-    here = jnp.stack([yi, ci])
-    mine, other = turned(here, out_weight)
     both = jnp.concatenate([mine, across(other)], axis=0)
     below, above = along_y(both, 1), along_y(both, 3)
-    low, m, q, u, w, z, fin = local_part(
-        activations,
-        halo,
-        norm_gain.reshape(d // W, W),
-        qkv_weight,
-        conv_weight,
-        gate_down_matrix,
-        log_forget_gates,
-        step_size,
+    gain = norm_gain.reshape(d // W, W)
+    scale, kf, rise, pos, u, w, z, fin = local_part(
+        activations, halo, gain, qkv_weight, conv_weight, log_forget_gates, step_size
     )
 
     def along_z(a, by):
@@ -611,17 +722,36 @@
     half = both.shape[0] // 2
     far = along_y(above[:half], 3), along_y(below[half:], 1)
     z1, z3, z2 = along_z(fin, 1), along_z(fin, 3), along_z(fin, 2)
+    low, m, q = query_part(
+        activations,
+        halo,
+        gain,
+        qkv_weight,
+        conv_weight,
+        gate_down_matrix,
+        kf,
+        rise,
+        pos,
+        step_size,
+        scale,
+    )
     o, r, s = reading_part(
         m, q, u, w, z, low, gate_up, out_gain.reshape(1, 2 * W)
     )
     total, before = compose(zi.reshape(1), fin, z1, z2, z3)
     x1, x3, x2 = along_x(total, 1), along_x(total, 3), along_x(total, 2)
+    x1, far = lax.optimization_barrier((x1, far))
     at = jnp.stack([xi, yi])
-    x1, far = lax.optimization_barrier((x1, far))
     q0, q1, q2, q3 = gated_part(at, x1, x2, x3, before, o, r, s)
     own = [q0, along_y(q1, 1), along_y(q3, 3), along_y(q2, 2)]
-    weights = [both, below, above, far[0], both, below, above, far[1]]
-    p0, p1, p2, p3 = mixed_part(here, weights, own, [across(a) for a in own])
+    weights = [(both, 0, 8), (below, 0, 8), (above, 0, 8), (far[0], 0, 4)]
+    weights += [(both, 4, 8), (below, 4, 8), (above, 4, 8), (far[1], 0, 4)]
+    blocks = own, [across(a) for a in own]
+    (p2,) = mixed_part((2,), here, weights, *blocks)
+    here, p2 = lax.optimization_barrier((here, p2))
+    p1, p3 = mixed_part((1, 3), here, weights, *blocks)
+    here, p1 = lax.optimization_barrier((here, p1))
+    (p0,) = mixed_part((0,), here, weights, *blocks)
     pieces = [p0, along_y(p1, 1), along_y(p2, 2), along_y(p3, 3)]
     return joined(yi.reshape(1), pieces).T
 

time: 122 us -> 112 us (0.918)
  waiting for transfers between devices: 26.7 us -> 14.2 us
  Pallas kernels: 49.9 us -> 54.6 us
  local copies, waits for them, and re-layouts: 8.62 us -> 5.22 us
    pallas_call x2 -> x3, Pallas kernels: 4.52 us -> 17 us  [the longest x1 11.3 us: query_part(): pl.pallas_call(query_kernel, grid=(grid + 1,), in_specs=[early(d), whole(...]
    ppermute x3, waiting for transfers between devices: 8.34 us -> 0.01 us  [along_z(): return lax.ppermute(a, 'ctx', pairs)]
    pallas_call x1, Pallas kernels: 31.2 us -> 25.1 us  [local_part(): pl.pallas_call(local_kernel, grid=(grid + 1,), in_specs=[early(d), whole(...]
    ppermute x5, starting transfers between devices: 11.8 us -> 15.3 us  [across(): return lax.ppermute(a, 'head', [(i, i ^ 1) for i in range(8)])]
    ppermute x10, waiting for transfers between devices: 15.6 us -> 12.8 us  [along_y(): return lax.ppermute(a, 'head', [(i, (i + 2 * by) % 8) for i in range(8)])]
    ppermute x10, starting transfers between devices: 12.5 us -> 9.98 us  [along_y(): return lax.ppermute(a, 'head', [(i, (i + 2 * by) % 8) for i in range(8)])]
    unnamed x11 -> x17, local copies, waits for them, and re-layouts: 5.97 us -> 4.21 us
    slice x2, local copies, waits for them, and re-layouts: 1.72 us -> 0.08 us  [body(): far = (along_y(above[:half], 3), along_y(below[half:], 1))]
  transfers between devices with their start and end apart: 22 -> 22, of which waited for: 8 -> 6; matrix products, arithmetic and copies ran while one was open for 1% -> 2% of each run, Pallas kernels for 32% -> 42%
where the time goes in v3:
time: 112 us
  Pallas kernels  54.6 us (49%)
  starting transfers between devices  36.7 us (33%)
  waiting for transfers between devices  14.2 us (13%)
  local copies, waits for them, and re-layouts  5.22 us (5%)
    pallas_call x1, Pallas kernels, local_part(): pl.pallas_call(local_kernel, grid=(grid + 1,), in_specs=[early(d), whole(...  25.1 us
    ppermute x5, starting transfers between devices, across(): return lax.ppermute(a, 'head', [(i, i ^ 1) for i in range(8)])  15.3 us
    ppermute x10, waiting for transfers between devices, along_y(): return lax.ppermute(a, 'head', [(i, (i + 2 * by) % 8) for i in range(8)])  12.8 us
    pallas_call x1, Pallas kernels, query_part(): pl.pallas_call(query_kernel, grid=(grid + 1,), in_specs=[early(d), whole(...  11.3 us
    ppermute x10, starting transfers between devices, along_y(): return lax.ppermute(a, 'head', [(i, (i + 2 * by) % 8) for i in range(8)])  9.98 us
    pallas_call x1, Pallas kernels, reading_part(): pl.pallas_call(reading_kernel, grid=(tokens // TILE,), in_specs=[rows(2 *...  6.02 us
    pallas_call x3, Pallas kernels, mixed_part(): pl.pallas_call(mixed_kernel, grid_spec=pltpu.PrefetchScalarGridSpec(num_s...  4.94 us
    pallas_call x1, Pallas kernels, gated_part(): pl.pallas_call(gated_kernel, in_specs=[pl.BlockSpec(memory_space=pltpu.SM...  4.58 us
  transfers between devices with their start and end apart: 22, of which 6 were waited for; matrix products, arithmetic and copies ran while one was open for 2% of the time, Pallas kernels for 42%

profile of v3, /device:TPU:1, one launch (start us, length us, event | category | flops | bytes accessed | tf_op | source)
XLA Modules:
  0.0 111.8 jit_solution(2936336382725841545)
XLA Ops:
  0.0 0.1 pad_add_fusion.at_ref
  0.1 1.3 %copy-done.1 = bf16[256,2304]{1,0:T(8,128)(2,1)S(1)} copy-done((bf16[256,2304]{1,0:T(8,128)(2,1)S(1)}, bf16[256,2304]{1,0:T(8,128)(2,1)}, u32[]{:S(2)}) %copy-start.1) | copy-done | bytes 1179672
  1.3 1.0 turned.1
  2.3 1.5 %collective-permute-start = (bf16[1152,256]{1,0:T(8,128)(2,1)S(1)}, bf16[1152,256]{1,0:T(8,128)(2,1)S(1)}, u32[]{:S(2)}, u32[]{:S(2)}) collective-permute-start(bf16[1152,256]{1,0:T(8,128)(2,1)S(1)} %get-tuple-element.40), channel_id=1, source_target_pairs={{0,1},{1,0},{2,3},{3,2},{4,5},{5,4},{6,7},{7,6},{8,9},{9,8},{10,11... | collective-permute-start | bytes 1769480 | tf_op jit(solution)/shard_map/ppermute | solution.py:699
  3.8 0.9 slice.9
  4.7 3.6 %collective-permute-start.1 = (bf16[16,2304]{1,0:T(8,128)(2,1)S(1)}, bf16[16,2304]{1,0:T(8,128)(2,1)S(1)}, u32[]{:S(2)}, u32[]{:S(2)}) collective-permute-start(bf16[16,2304]{1,0:T(8,128)(2,1)S(1)} %slice.9), channel_id=1, source_target_pairs={{0,8},{8,16},{16,24},{24,32},{32,40},{40,48},{48,56},{56,64},{64,7... | collective-permute-start | bytes 221192 | tf_op jit(solution)/shard_map/ppermute | solution.py:703
  8.4 0.6 pad_add_fusion.1.at_ref
  9.0 0.0 collective-permute-done
  9.1 2.8 %collective-permute-start.3 = (bf16[2304,256]{1,0:T(8,128)(2,1)S(1)}, bf16[2304,256]{1,0:T(8,128)(2,1)S(1)}, u32[]{:S(2)}, u32[]{:S(2)}) collective-permute-start(bf16[2304,256]{1,0:T(8,128)(2,1)S(1)} %constant_dynamic-update-slice_fusion.refs_0_.refs_4_), channel_id=1, source_target_pairs={{0,6},{1,7},{2,0},{3,1},{4,2},{5,3},{6,4},{7,5},{8,14},{9,15},{10,... | collective-permute-start | bytes 3538952 | tf_op jit(solution)/shard_map/ppermute | solution.py:696
  11.9 0.0 collective-permute-start.2
  11.9 0.0 collective-permute-done.1.halo_ref
  11.9 0.6 copy-done.7
  12.5 25.1 %local_part.1 = (f32[2048,128]{1,0:T(8,128)}, bf16[2048,256]{1,0:T(8,128)(2,1)}, bf16[2048,256]{1,0:T(8,128)(2,1)}, bf16[2048,256]{1,0:T(8,128)(2,1)}, bf16[2048...) custom-call(bf16[2048,2304]{1,0:T(8,128)(2,1)} %x_ref.3, ...), custom_call_target="tpu_custom_call" | custom-call | flops 14000000000 | bytes 24000000 | tf_op jit(solution)/shard_map/local_part/pallas_call | solution.py:268
  37.7 0.0 collective-permute-done.3.refs_2_.refs_6_
  37.7 2.4 %collective-permute-done.2.refs_1_.refs_5_ = bf16[2304,256]{1,0:T(8,128)(2,1)S(1)} collective-permute-done((bf16[2304,256]{1,0:T(8,128)(2,1)S(1)}, bf16[2304,256]{1,0:T(8,128)(2,1)S(1)}, u32[]{:S(2)}, u32[]{:S(2)}) %collective-permute-start.2) | collective-permute-done | bytes 1179680 | tf_op jit(solution)/shard_map/ppermute | solution.py:696
  40.1 2.3 %collective-permute-start.6 = (bf16[128,512]{1,0:T(8,128)(2,1)}, bf16[128,512]{1,0:T(8,128)(2,1)S(1)}, u32[]{:S(2)}, u32[]{:S(2)}) collective-permute-start(bf16[128,512]{1,0:T(8,128)(2,1)} %get-tuple-element.44.own), channel_id=1, source_target_pairs={{0,24},{8,0},{16,8},{24,16},{32,56},{40,32},{48,40},{56,48},{64,88... | collective-permute-start | bytes 393224 | tf_op jit(solution)/shard_map/ppermute | solution.py:715
  42.4 1.1 %collective-permute-start.5 = (bf16[128,512]{1,0:T(8,128)(2,1)}, bf16[128,512]{1,0:T(8,128)(2,1)S(1)}, u32[]{:S(2)}, u32[]{:S(2)}) collective-permute-start(bf16[128,512]{1,0:T(8,128)(2,1)} %get-tuple-element.44.own), channel_id=1, source_target_pairs={{0,16},{8,24},{16,0},{24,8},{32,48},{40,56},{48,32},{56,40},{64,80... | collective-permute-start | bytes 393224 | tf_op jit(solution)/shard_map/ppermute | solution.py:715
  43.5 0.7 collective-permute-start.4
  44.3 0.4 collective-permute-start.8
  44.7 1.1 collective-permute-start.9
  45.9 11.3 %query_part.1 = (bf16[2048,128]{1,0:T(8,128)(2,1)}, bf16[2048,256]{1,0:T(8,128)(2,1)}, bf16[2048,256]{1,0:T(8,128)(2,1)}) custom-call(bf16[2048,2304]{1,0:T(8,128)(2,1)} %x_ref.3, bf16[16,2304]{1,0:T(8,128)(2,1)} %copy-done.7, f32[18,128]{1,0:T(8,128)} %bitcast.14, bf16[3,2304,256]{2,1,0:T(8,128)(2,1)} %w_ref.3, bf16[3,4,256]{2,1,0:T(4,128)(2,1)} %conv_ref.3, ...), custom_call_target="tpu_custom_call" | custom-call | flops 4000000000 | bytes 17000000 | tf_op jit(solution)/shard_map/query_part/pallas_call | solution.py:412
  57.2 0.0 collective-permute-done.6.three
  57.2 0.0 collective-permute-done.5.two
  57.2 0.0 collective-permute-done.4.one
  57.2 0.6 compose.1
  57.8 0.6 copy-done.2
  58.5 2.5 %collective-permute-start.11 = (bf16[128,512]{1,0:T(8,128)(2,1)S(1)}, bf16[128,512]{1,0:T(8,128)(2,1)S(1)}, u32[]{:S(2)}, u32[]{:S(2)}) collective-permute-start(bf16[128,512]{1,0:T(8,128)(2,1)S(1)} %get-tuple-element.45), channel_id=1, source_target_pairs={{0,96},{8,104},{16,112},{24,120},{32,0},{40,8},{48,16},{56,24},{64... | collective-permute-start | bytes 393224 | tf_op jit(solution)/shard_map/ppermute | solution.py:719
  61.0 0.5 collective-permute-start.10
  61.5 0.6 collective-permute-start.7
  62.1 6.0 %reading_part.1 = (bf16[2048,256]{1,0:T(8,128)(2,1)}, bf16[2048,256]{1,0:T(8,128)(2,1)}, bf16[2048,256]{1,0:T(8,128)(2,1)}) custom-call(bf16[2048,256]{1,0:T(8,128)(2,1)} %get-tuple-element.54.m_ref, bf16[2048,256]{1,0:T(8,128)(2,1)} %get-tuple-element.55.q_ref, bf16[2048,256]{1,0:T(8,128)(2,1)} %get-tuple-element.56.u_ref, ...), custom_call_target="tpu_custom_call" | custom-call | flops 3000000000 | bytes 12000000 | tf_op jit(solution)/shard_map/reading_part/pallas_call | solution.py:469
  68.1 0.0 collective-permute-done.7.one
  68.1 0.0 collective-permute-done.8.refs_3_
  68.1 0.0 collective-permute-done.9.refs_7_
  68.1 0.0 collective-permute-done.11.three
  68.2 0.0 collective-permute-done.10.two
  68.2 0.6 copy-done.6
  68.8 0.1 copy-done.4
  68.8 0.0 copy-done.5
  68.9 4.6 %gated_part.1 = (bf16[512,256]{1,0:T(8,128)(2,1)}, bf16[512,256]{1,0:T(8,128)(2,1)}, bf16[512,256]{1,0:T(8,128)(2,1)}, bf16[512,256]{1,0:T(8,128)(2,1)}) custom-call(s32[2]{0:T(128)} %pad_add_fusion.1.at_ref, bf16[128,512]{1,0:T(8,128)(2,1)} %copy-done.6, bf16[128,512]{1,0:T(8,128)(2,1)} %copy-done.5, bf16[128,512]{1,0:T(8,128)(2,1)} %copy-done.4, ...), custom_call_target="tpu_custom_call" | custom-call | flops 300000000 | bytes 4000000 | tf_op jit(solution)/shard_map/gated_part/pallas_call | solution.py:559
  73.5 0.1 collective-permute-start.12
  73.5 2.7 %collective-permute-start.13 = (bf16[512,256]{1,0:T(8,128)(2,1)}, bf16[512,256]{1,0:T(8,128)(2,1)S(1)}, u32[]{:S(2)}, u32[]{:S(2)}) collective-permute-start(bf16[512,256]{1,0:T(8,128)(2,1)} %get-tuple-element.65), channel_id=1, source_target_pairs={{0,6},{1,7},{2,0},{3,1},{4,2},{5,3},{6,4},{7,5},{8,14},{9,15},{10,... | collective-permute-start | bytes 786440 | tf_op jit(solution)/shard_map/ppermute | solution.py:696
  76.2 0.1 collective-permute-start.14
  76.3 4.3 %collective-permute-start.15 = (bf16[512,256]{1,0:T(8,128)(2,1)}, bf16[512,256]{1,0:T(8,128)(2,1)S(1)}, u32[]{:S(2)}, u32[]{:S(2)}) collective-permute-start(bf16[512,256]{1,0:T(8,128)(2,1)} %get-tuple-element.63.refs_8_), channel_id=1, source_target_pairs={{0,1},{1,0},{2,3},{3,2},{4,5},{5,4},{6,7},{7,6},{8,9},{9,8},{10,11... | collective-permute-start | bytes 786440 | tf_op jit(solution)/shard_map/ppermute | solution.py:699
  80.6 0.0 collective-permute-done.12.refs_9_
  80.6 9.0 %collective-permute-start.16 = (bf16[512,256]{1,0:T(8,128)(2,1)S(1)}, bf16[512,256]{1,0:T(8,128)(2,1)S(1)}, u32[]{:S(2)}, u32[]{:S(2)}) collective-permute-start(bf16[512,256]{1,0:T(8,128)(2,1)S(1)} %collective-permute-done.12.refs_9_), channel_id=1, source_target_pairs={{0,1},{1,0},{2,3},{3,2},{4,5},{5,4},{6,7},{7,6},{8,9},{9,8},{10,11... | collective-permute-start | bytes 786440 | tf_op jit(solution)/shard_map/ppermute | solution.py:699
  89.6 0.0 collective-permute-done.13.refs_10_
  89.6 0.0 collective-permute-start.17
  89.6 0.0 collective-permute-done.14.refs_11_
  89.6 0.5 collective-permute-start.18
  90.1 0.0 collective-permute-done.15.refs_12_
  90.1 0.6 collective-permute-done.16.refs_13_
  90.7 0.4 collective-permute-done.17.refs_14_
  91.1 0.4 collective-permute-done.18.refs_15_
  91.5 0.9 copy-done
  92.4 1.3 %mixed_part.3 = bf16[288,512]{1,0:T(8,128)(2,1)S(1)} custom-call(s32[2]{0:T(128)S(1)} %pad_add_fusion.at_ref, bf16[2304,256]{1,0:T(8,128)(2,1)S(1)} %constant_dynamic-update-slice_fusion.refs_0_.refs_4_, bf16[2304,256]{1,0:T(8,128)(2,1)S(1)} %collective-permute-done.2.refs_1_.refs_5_, bf16[2304,256]{1,0:T(8,128)(2,1)S(1)} %collective-permute-done.3.refs_2_.refs_6_, ...), custom_call_target="tpu_custom_call" | custom-call | flops 600000000 | bytes 3500000 | tf_op jit(solution)/shard_map/mixed_part/pallas_call | solution.py:634
  93.8 0.1 collective-permute-start.20
  93.9 2.3 %mixed_part.4 = (bf16[288,512]{1,0:T(8,128)(2,1)S(1)}, bf16[288,512]{1,0:T(8,128)(2,1)S(1)}) custom-call(s32[2]{0:T(128)S(1)} %pad_add_fusion.at_ref, bf16[2304,256]{1,0:T(8,128)(2,1)S(1)} %constant_dynamic-update-slice_fusion.refs_0_.refs_4_, bf16[2304,256]{1,0:T(8,128)(2,1)S(1)} %collective-permute-done.2.refs_1_.refs_5_, ...), custom_call_target="tpu_custom_call" | custom-call | flops 1200000000 | bytes 5000000 | tf_op jit(solution)/shard_map/mixed_part/pallas_call | solution.py:634
  96.2 2.6 %collective-permute-start.19 = (bf16[288,512]{1,0:T(8,128)(2,1)S(1)}, bf16[288,512]{1,0:T(8,128)(2,1)S(1)}, u32[]{:S(2)}, u32[]{:S(2)}) collective-permute-start(bf16[288,512]{1,0:T(8,128)(2,1)S(1)} %get-tuple-element.70), channel_id=1, source_target_pairs={{0,2},{1,3},{2,4},{3,5},{4,6},{5,7},{6,0},{7,1},{8,10},{9,11},{10,... | collective-permute-start | bytes 884744 | tf_op jit(solution)/shard_map/ppermute | solution.py:696
  98.8 0.1 collective-permute-start.21
  98.9 1.3 %mixed_part.5.refs_0_ = bf16[288,512]{1,0:T(8,128)(2,1)S(1)} custom-call(s32[2]{0:T(128)S(1)} %pad_add_fusion.at_ref, bf16[2304,256]{1,0:T(8,128)(2,1)S(1)} %constant_dynamic-update-slice_fusion.refs_0_.refs_4_, bf16[2304,256]{1,0:T(8,128)(2,1)S(1)} %collective-permute-done.2.refs_1_.refs_5_, bf16[2304,256]{1,0:T(8,128)(2,1)S(1)} %collective-permute-done.3.refs_2_.refs_6_, ...), custom_call_target="tpu_custom_call" | custom-call | flops 600000000 | bytes 3500000 | tf_op jit(solution)/shard_map/mixed_part/pallas_call | solution.py:634
  100.3 3.4 %collective-permute-done.20.refs_2_ = bf16[288,512]{1,0:T(8,128)(2,1)S(1)} collective-permute-done((bf16[288,512]{1,0:T(8,128)(2,1)S(1)}, bf16[288,512]{1,0:T(8,128)(2,1)S(1)}, u32[]{:S(2)}, u32[]{:S(2)}) %collective-permute-start.20) | collective-permute-done | bytes 294944 | tf_op jit(solution)/shard_map/ppermute | solution.py:696
  103.6 7.0 %collective-permute-done.19.refs_1_ = bf16[288,512]{1,0:T(8,128)(2,1)S(1)} collective-permute-done((bf16[288,512]{1,0:T(8,128)(2,1)S(1)}, bf16[288,512]{1,0:T(8,128)(2,1)S(1)}, u32[]{:S(2)}, u32[]{:S(2)}) %collective-permute-start.19) | collective-permute-done | bytes 294944 | tf_op jit(solution)/shard_map/ppermute | solution.py:696
  110.6 0.0 collective-permute-done.21.refs_3_
  110.7 1.1 joined.1
  (13 shorter events, 0.2 us)
Async XLA Ops:
  0.1 1.3 %copy-start.1 = (bf16[256,2304]{1,0:T(8,128)(2,1)S(1)}, bf16[256,2304]{1,0:T(8,128)(2,1)}, u32[]{:S(2)}) copy-start(bf16[256,2304]{1,0:T(8,128)(2,1)} %w_ref.2) | copy-start | bytes 3538948
  2.3 6.7 %collective-permute-start = (bf16[1152,256]{1,0:T(8,128)(2,1)S(1)}, bf16[1152,256]{1,0:T(8,128)(2,1)S(1)}, u32[]{:S(2)}, u32[]{:S(2)}) collective-permute-start(bf16[1152,256]{1,0:T(8,128)(2,1)S(1)} %get-tuple-element.40), channel_id=1, source_target_pairs={{0,1},{1,0},{2,3},{3,2},{4,5},{5,4},{6,7},{7,6},{8,9},{9,8},{10,11... | collective-permute-start | bytes 1769480 | tf_op jit(solution)/shard_map/ppermute | solution.py:699
  4.7 7.2 %collective-permute-start.1 = (bf16[16,2304]{1,0:T(8,128)(2,1)S(1)}, bf16[16,2304]{1,0:T(8,128)(2,1)S(1)}, u32[]{:S(2)}, u32[]{:S(2)}) collective-permute-start(bf16[16,2304]{1,0:T(8,128)(2,1)S(1)} %slice.9), channel_id=1, source_target_pairs={{0,8},{8,16},{16,24},{24,32},{32,40},{40,48},{48,56},{56,64},{64,7... | collective-permute-start | bytes 221192 | tf_op jit(solution)/shard_map/ppermute | solution.py:703
  9.1 28.5 %collective-permute-start.3 = (bf16[2304,256]{1,0:T(8,128)(2,1)S(1)}, bf16[2304,256]{1,0:T(8,128)(2,1)S(1)}, u32[]{:S(2)}, u32[]{:S(2)}) collective-permute-start(bf16[2304,256]{1,0:T(8,128)(2,1)S(1)} %constant_dynamic-update-slice_fusion.refs_0_.refs_4_), channel_id=1, source_target_pairs={{0,6},{1,7},{2,0},{3,1},{4,2},{5,3},{6,4},{7,5},{8,14},{9,15},{10,... | collective-permute-start | bytes 3538952 | tf_op jit(solution)/shard_map/ppermute | solution.py:696
  11.9 28.2 %collective-permute-start.2 = (bf16[2304,256]{1,0:T(8,128)(2,1)S(1)}, bf16[2304,256]{1,0:T(8,128)(2,1)S(1)}, u32[]{:S(2)}, u32[]{:S(2)}) collective-permute-start(bf16[2304,256]{1,0:T(8,128)(2,1)S(1)} %constant_dynamic-update-slice_fusion.refs_0_.refs_4_), channel_id=1, source_target_pairs={{0,2},{1,3},{2,4},{3,5},{4,6},{5,7},{6,0},{7,1},{8,10},{9,11},{10,... | collective-permute-start | bytes 3538952 | tf_op jit(solution)/shard_map/ppermute | solution.py:696
  11.9 0.6 copy-start.7
  40.1 17.1 %collective-permute-start.6 = (bf16[128,512]{1,0:T(8,128)(2,1)}, bf16[128,512]{1,0:T(8,128)(2,1)S(1)}, u32[]{:S(2)}, u32[]{:S(2)}) collective-permute-start(bf16[128,512]{1,0:T(8,128)(2,1)} %get-tuple-element.44.own), channel_id=1, source_target_pairs={{0,24},{8,0},{16,8},{24,16},{32,56},{40,32},{48,40},{56,48},{64,88... | collective-permute-start | bytes 393224 | tf_op jit(solution)/shard_map/ppermute | solution.py:715
  42.4 14.8 %collective-permute-start.5 = (bf16[128,512]{1,0:T(8,128)(2,1)}, bf16[128,512]{1,0:T(8,128)(2,1)S(1)}, u32[]{:S(2)}, u32[]{:S(2)}) collective-permute-start(bf16[128,512]{1,0:T(8,128)(2,1)} %get-tuple-element.44.own), channel_id=1, source_target_pairs={{0,16},{8,24},{16,0},{24,8},{32,48},{40,56},{48,32},{56,40},{64,80... | collective-permute-start | bytes 393224 | tf_op jit(solution)/shard_map/ppermute | solution.py:715
  43.5 13.7 %collective-permute-start.4 = (bf16[128,512]{1,0:T(8,128)(2,1)}, bf16[128,512]{1,0:T(8,128)(2,1)S(1)}, u32[]{:S(2)}, u32[]{:S(2)}) collective-permute-start(bf16[128,512]{1,0:T(8,128)(2,1)} %get-tuple-element.44.own), channel_id=1, source_target_pairs={{0,8},{8,16},{16,24},{24,0},{32,40},{40,48},{48,56},{56,32},{64,72... | collective-permute-start | bytes 393224 | tf_op jit(solution)/shard_map/ppermute | solution.py:715
  44.3 23.8 %collective-permute-start.8 = (bf16[1152,256]{1,0:T(8,128)(2,1)S(1)}, bf16[1152,256]{1,0:T(8,128)(2,1)S(1)}, u32[]{:S(2)}, u32[]{:S(2)}) collective-permute-start(bf16[1152,256]{1,0:T(8,128)(2,1)S(1)} %slice.10), channel_id=1, source_target_pairs={{0,6},{1,7},{2,0},{3,1},{4,2},{5,3},{6,4},{7,5},{8,14},{9,15},{10,... | collective-permute-start | bytes 1769480 | tf_op jit(solution)/shard_map/ppermute | solution.py:696
  44.7 23.4 %collective-permute-start.9 = (bf16[1152,256]{1,0:T(8,128)(2,1)S(1)}, bf16[1152,256]{1,0:T(8,128)(2,1)S(1)}, u32[]{:S(2)}, u32[]{:S(2)}) collective-permute-start(bf16[1152,256]{1,0:T(8,128)(2,1)S(1)} %slice.11), channel_id=1, source_target_pairs={{0,2},{1,3},{2,4},{3,5},{4,6},{5,7},{6,0},{7,1},{8,10},{9,11},{10,... | collective-permute-start | bytes 1769480 | tf_op jit(solution)/shard_map/ppermute | solution.py:696
  45.9 11.4 %copy-start.3 = (bf16[128,512]{1,0:T(8,128)(2,1)S(1)}, bf16[128,512]{1,0:T(8,128)(2,1)}, u32[]{:S(2)}) copy-start(bf16[128,512]{1,0:T(8,128)(2,1)} %get-tuple-element.44.own) | copy-start | bytes 393220
  57.8 0.7 copy-start.2
  58.5 9.7 %collective-permute-start.11 = (bf16[128,512]{1,0:T(8,128)(2,1)S(1)}, bf16[128,512]{1,0:T(8,128)(2,1)S(1)}, u32[]{:S(2)}, u32[]{:S(2)}) collective-permute-start(bf16[128,512]{1,0:T(8,128)(2,1)S(1)} %get-tuple-element.45), channel_id=1, source_target_pairs={{0,96},{8,104},{16,112},{24,120},{32,0},{40,8},{48,16},{56,24},{64... | collective-permute-start | bytes 393224 | tf_op jit(solution)/shard_map/ppermute | solution.py:719
  61.0 7.2 %collective-permute-start.10 = (bf16[128,512]{1,0:T(8,128)(2,1)S(1)}, bf16[128,512]{1,0:T(8,128)(2,1)S(1)}, u32[]{:S(2)}, u32[]{:S(2)}) collective-permute-start(bf16[128,512]{1,0:T(8,128)(2,1)S(1)} %get-tuple-element.45), channel_id=1, source_target_pairs={{0,64},{8,72},{16,80},{24,88},{32,96},{40,104},{48,112},{56,120},{... | collective-permute-start | bytes 393224 | tf_op jit(solution)/shard_map/ppermute | solution.py:719
  61.5 6.6 %collective-permute-start.7 = (bf16[128,512]{1,0:T(8,128)(2,1)S(1)}, bf16[128,512]{1,0:T(8,128)(2,1)S(1)}, u32[]{:S(2)}, u32[]{:S(2)}) collective-permute-start(bf16[128,512]{1,0:T(8,128)(2,1)S(1)} %get-tuple-element.45), channel_id=1, source_target_pairs={{0,32},{8,40},{16,48},{24,56},{32,64},{40,72},{48,80},{56,88},{64,... | collective-permute-start | bytes 393224 | tf_op jit(solution)/shard_map/ppermute | solution.py:719
  68.1 0.7 copy-start.6
  68.2 0.7 copy-start.4
  68.2 0.7 copy-start.5
  73.5 7.2 %collective-permute-start.12 = (bf16[512,256]{1,0:T(8,128)(2,1)}, bf16[512,256]{1,0:T(8,128)(2,1)S(1)}, u32[]{:S(2)}, u32[]{:S(2)}) collective-permute-start(bf16[512,256]{1,0:T(8,128)(2,1)} %get-tuple-element.64), channel_id=1, source_target_pairs={{0,2},{1,3},{2,4},{3,5},{4,6},{5,7},{6,0},{7,1},{8,10},{9,11},{10,... | collective-permute-start | bytes 786440 | tf_op jit(solution)/shard_map/ppermute | solution.py:696
  73.5 16.1 %collective-permute-start.13 = (bf16[512,256]{1,0:T(8,128)(2,1)}, bf16[512,256]{1,0:T(8,128)(2,1)S(1)}, u32[]{:S(2)}, u32[]{:S(2)}) collective-permute-start(bf16[512,256]{1,0:T(8,128)(2,1)} %get-tuple-element.65), channel_id=1, source_target_pairs={{0,6},{1,7},{2,0},{3,1},{4,2},{5,3},{6,4},{7,5},{8,14},{9,15},{10,... | collective-permute-start | bytes 786440 | tf_op jit(solution)/shard_map/ppermute | solution.py:696
  76.2 13.4 %collective-permute-start.14 = (bf16[512,256]{1,0:T(8,128)(2,1)}, bf16[512,256]{1,0:T(8,128)(2,1)S(1)}, u32[]{:S(2)}, u32[]{:S(2)}) collective-permute-start(bf16[512,256]{1,0:T(8,128)(2,1)} %get-tuple-element.66), channel_id=1, source_target_pairs={{0,4},{1,5},{2,6},{3,7},{4,0},{5,1},{6,2},{7,3},{8,12},{9,13},{10,... | collective-permute-start | bytes 786440 | tf_op jit(solution)/shard_map/ppermute | solution.py:696
  76.3 13.8 %collective-permute-start.15 = (bf16[512,256]{1,0:T(8,128)(2,1)}, bf16[512,256]{1,0:T(8,128)(2,1)S(1)}, u32[]{:S(2)}, u32[]{:S(2)}) collective-permute-start(bf16[512,256]{1,0:T(8,128)(2,1)} %get-tuple-element.63.refs_8_), channel_id=1, source_target_pairs={{0,1},{1,0},{2,3},{3,2},{4,5},{5,4},{6,7},{7,6},{8,9},{9,8},{10,11... | collective-permute-start | bytes 786440 | tf_op jit(solution)/shard_map/ppermute | solution.py:699
  80.6 10.1 %collective-permute-start.16 = (bf16[512,256]{1,0:T(8,128)(2,1)S(1)}, bf16[512,256]{1,0:T(8,128)(2,1)S(1)}, u32[]{:S(2)}, u32[]{:S(2)}) collective-permute-start(bf16[512,256]{1,0:T(8,128)(2,1)S(1)} %collective-permute-done.12.refs_9_), channel_id=1, source_target_pairs={{0,1},{1,0},{2,3},{3,2},{4,5},{5,4},{6,7},{7,6},{8,9},{9,8},{10,11... | collective-permute-start | bytes 786440 | tf_op jit(solution)/shard_map/ppermute | solution.py:699
  89.6 1.5 %collective-permute-start.17 = (bf16[512,256]{1,0:T(8,128)(2,1)S(1)}, bf16[512,256]{1,0:T(8,128)(2,1)S(1)}, u32[]{:S(2)}, u32[]{:S(2)}) collective-permute-start(bf16[512,256]{1,0:T(8,128)(2,1)S(1)} %collective-permute-done.13.refs_10_), channel_id=1, source_target_pairs={{0,1},{1,0},{2,3},{3,2},{4,5},{5,4},{6,7},{7,6},{8,9},{9,8},{10,11... | collective-permute-start | bytes 786440 | tf_op jit(solution)/shard_map/ppermute | solution.py:699
  89.6 1.9 %collective-permute-start.18 = (bf16[512,256]{1,0:T(8,128)(2,1)S(1)}, bf16[512,256]{1,0:T(8,128)(2,1)S(1)}, u32[]{:S(2)}, u32[]{:S(2)}) collective-permute-start(bf16[512,256]{1,0:T(8,128)(2,1)S(1)} %collective-permute-done.14.refs_11_), channel_id=1, source_target_pairs={{0,1},{1,0},{2,3},{3,2},{4,5},{5,4},{6,7},{7,6},{8,9},{9,8},{10,11... | collective-permute-start | bytes 786440 | tf_op jit(solution)/shard_map/ppermute | solution.py:699
  91.5 1.0 copy-start
  93.8 9.8 %collective-permute-start.20 = (bf16[288,512]{1,0:T(8,128)(2,1)S(1)}, bf16[288,512]{1,0:T(8,128)(2,1)S(1)}, u32[]{:S(2)}, u32[]{:S(2)}) collective-permute-start(bf16[288,512]{1,0:T(8,128)(2,1)S(1)} %mixed_part.3), channel_id=1, source_target_pairs={{0,4},{1,5},{2,6},{3,7},{4,0},{5,1},{6,2},{7,3},{8,12},{9,13},{10,... | collective-permute-start | bytes 884744 | tf_op jit(solution)/shard_map/ppermute | solution.py:696
  96.2 14.5 %collective-permute-start.19 = (bf16[288,512]{1,0:T(8,128)(2,1)S(1)}, bf16[288,512]{1,0:T(8,128)(2,1)S(1)}, u32[]{:S(2)}, u32[]{:S(2)}) collective-permute-start(bf16[288,512]{1,0:T(8,128)(2,1)S(1)} %get-tuple-element.70), channel_id=1, source_target_pairs={{0,2},{1,3},{2,4},{3,5},{4,6},{5,7},{6,0},{7,1},{8,10},{9,11},{10,... | collective-permute-start | bytes 884744 | tf_op jit(solution)/shard_map/ppermute | solution.py:696
  98.8 11.9 %collective-permute-start.21 = (bf16[288,512]{1,0:T(8,128)(2,1)S(1)}, bf16[288,512]{1,0:T(8,128)(2,1)S(1)}, u32[]{:S(2)}, u32[]{:S(2)}) collective-permute-start(bf16[288,512]{1,0:T(8,128)(2,1)S(1)} %get-tuple-element.72), channel_id=1, source_target_pairs={{0,6},{1,7},{2,0},{3,1},{4,2},{5,3},{6,4},{7,5},{8,14},{9,15},{10,... | collective-permute-start | bytes 884744 | tf_op jit(solution)/shard_map/ppermute | solution.py:696

commit v4 on v3

--- a/solution.py
+++ b/solution.py
@@ -180,7 +180,7 @@
             left = [mm(lower16[c] * keep, bd(inv[c])).astype(BF16) for c in chunks]
             fill(products)
             both = [mm(inv[c], bd(left[c])).astype(BF16) for c in chunks]
-            fill(products, 2)
+            fill(products, 1)
             inv = [inv[c] - both[c] for c in chunks]
             size *= 2
 
@@ -465,10 +465,10 @@
     tokens = m.shape[0]
     rank = low.shape[1]
     whole = lambda *shape: pl.BlockSpec(shape, lambda i: (0,) * len(shape))
-    rows = lambda width: pl.BlockSpec((TILE, width), lambda i: (i, 0))
+    rows = lambda width: pl.BlockSpec((2 * TILE, width), lambda i: (i, 0))
     return pl.pallas_call(
         reading_kernel,
-        grid=(tokens // TILE,),
+        grid=(tokens // (2 * TILE),),
         in_specs=[rows(2 * W)] * 4
         + [rows(4 * W), rows(rank), whole(rank, 2 * W), whole(1, 2 * W)],
         out_specs=[rows(2 * W)] * 3,
@@ -530,27 +530,31 @@
 def gated_kernel(at_ref, one, two, three, pre, o_hbm, r_hbm, s_hbm, *rest):
     outs, (o_ref, r_ref, s_ref, sems) = rest[:4], rest[4:]
     xi, yi = at_ref[0], at_ref[1]
+    quarters = [lax.rem(yi + d, 4) for d in range(4)]
     copies = [
-        pltpu.make_async_copy(src, dst, sems.at[i])
-        for i, (src, dst) in enumerate(((r_hbm, r_ref), (o_hbm, o_ref), (s_hbm, s_ref)))
+        [
+            pltpu.make_async_copy(src.at[here], dst.at[d], sems.at[3 * d + i])
+            for i, (src, dst) in enumerate(((r_hbm, r_ref), (o_hbm, o_ref), (s_hbm, s_ref)))
+        ]
+        for d, here in enumerate(quarters)
     ]
-    for copy in copies:
-        copy.start()
+    for d in range(4):
+        for copy in copies[d]:
+            copy.start()
     s = jnp.zeros((W, 2 * W), F32)
     for d, ref in ((3, three), (2, two), (1, one)):
         nxt = ref[:, : 2 * W].astype(F32) + mm(ref[:, 2 * W :], bd(s.astype(BF16)))
         s = jnp.where(xi >= d, nxt, s)
     s = pre[:, : 2 * W].astype(F32) + mm(pre[:, 2 * W :], bd(s.astype(BF16)))
     start = bd(s.astype(BF16))
-    for copy in copies:
-        copy.wait()
     for d, out in enumerate(outs):
-        here = lax.rem(yi + d, 4)
-        att = o_ref[here].astype(F32) + mm(r_ref[here], start)
+        for copy in copies[d]:
+            copy.wait()
+        att = o_ref[d].astype(F32) + mm(r_ref[d], start)
         scale = per_head(
             att, lambda h: lax.rsqrt(jnp.mean(h * h, axis=-1, keepdims=True) + 1e-05)
         )
-        out[...] = (att * scale * s_ref[here].astype(F32)).astype(BF16)
+        out[...] = (att * scale * s_ref[d].astype(F32)).astype(BF16)
 
 
 def gated_part(at, one, two, three, pre, o, r, s):
@@ -564,7 +568,7 @@
         out_specs=[vmem] * 4,
         out_shape=[jax.ShapeDtypeStruct((part, 2 * W), BF16)] * 4,
         scratch_shapes=[pltpu.VMEM((4, part, 2 * W), BF16)] * 3
-        + [pltpu.SemaphoreType.DMA((3,))],
+        + [pltpu.SemaphoreType.DMA((12,))],
         compiler_params=pltpu.CompilerParams(vmem_limit_bytes=56 * MIB),
         cost_estimate=pl.CostEstimate(
             flops=300_000_000, bytes_accessed=4_000_000, transcendentals=10_000
@@ -718,7 +722,7 @@
         pairs = [(4 * i + j, 4 * ((i + by) % 4) + j) for i in range(4) for j in range(4)]
         return lax.ppermute(a, "ctx", pairs)
 
-    fin, below, above = lax.optimization_barrier((fin, below, above))
+    kf, below, above = lax.optimization_barrier((kf, below, above))
     half = both.shape[0] // 2
     far = along_y(above[:half], 3), along_y(below[half:], 1)
     z1, z3, z2 = along_z(fin, 1), along_z(fin, 3), along_z(fin, 2)
@@ -735,6 +739,7 @@
         step_size,
         scale,
     )
+    z2, m = lax.optimization_barrier((z2, m))
     o, r, s = reading_part(
         m, q, u, w, z, low, gate_up, out_gain.reshape(1, 2 * W)
     )
@@ -750,9 +755,10 @@
     (p2,) = mixed_part((2,), here, weights, *blocks)
     here, p2 = lax.optimization_barrier((here, p2))
     p1, p3 = mixed_part((1, 3), here, weights, *blocks)
-    here, p1 = lax.optimization_barrier((here, p1))
+    far_piece = along_y(p2, 2)
+    here, far_piece = lax.optimization_barrier((here, far_piece))
     (p0,) = mixed_part((0,), here, weights, *blocks)
-    pieces = [p0, along_y(p1, 1), along_y(p2, 2), along_y(p3, 3)]
+    pieces = [p0, along_y(p1, 1), far_piece, along_y(p3, 3)]
     return joined(yi.reshape(1), pieces).T
 
 

time: 112 us -> 112 us (level)
  starting transfers between devices: 36.7 us -> 41.1 us
  waiting for transfers between devices: 14.2 us -> 10.9 us
  Pallas kernels: 54.6 us -> 53.2 us
    ppermute x10, waiting for transfers between devices: 12.8 us -> 9.71 us  [along_y(): return lax.ppermute(a, 'head', [(i, (i + 2 * by) % 8) for i in range(8)])]
    ppermute x10, starting transfers between devices: 9.98 us -> 12.1 us  [along_y(): return lax.ppermute(a, 'head', [(i, (i + 2 * by) % 8) for i in range(8)])]
    ppermute x3, starting transfers between devices: 4.16 us -> 6.05 us  [along_z(): return lax.ppermute(a, 'ctx', pairs)]
    ppermute x3, starting transfers between devices: 3.61 us -> 4.8 us  [along_x(): return lax.ppermute(a, 'ctx', pairs)]
  transfers between devices with their start and end apart: 22 -> 22, of which waited for: 6 -> 3; matrix products, arithmetic and copies ran while one was open for 2% -> 2% of each run, Pallas kernels for 42% -> 41%
where the time goes in v4:
time: 112 us; the launch traced here: 111 us
  Pallas kernels  53.2 us (48%)
  starting transfers between devices  41.1 us (37%)
  waiting for transfers between devices  10.9 us (10%)
  local copies, waits for them, and re-layouts  5.23 us (5%)
    pallas_call x1, Pallas kernels, local_part(): pl.pallas_call(local_kernel, grid=(grid + 1,), in_specs=[early(d), whole(...  24.4 us
    ppermute x5, starting transfers between devices, across(): return lax.ppermute(a, 'head', [(i, i ^ 1) for i in range(8)])  14.6 us
    ppermute x10, starting transfers between devices, along_y(): return lax.ppermute(a, 'head', [(i, (i + 2 * by) % 8) for i in range(8)])  12.1 us
    pallas_call x1, Pallas kernels, query_part(): pl.pallas_call(query_kernel, grid=(grid + 1,), in_specs=[early(d), whole(...  11.4 us
    ppermute x10, waiting for transfers between devices, along_y(): return lax.ppermute(a, 'head', [(i, (i + 2 * by) % 8) for i in range(8)])  9.71 us
    ppermute x3, starting transfers between devices, along_z(): return lax.ppermute(a, 'ctx', pairs)  6.05 us
    pallas_call x1, Pallas kernels, reading_part(): pl.pallas_call(reading_kernel, grid=(tokens // (2 * TILE),), in_specs=[ro...  5.29 us
    pallas_call x3, Pallas kernels, mixed_part(): pl.pallas_call(mixed_kernel, grid_spec=pltpu.PrefetchScalarGridSpec(num_s...  4.93 us
  transfers between devices with their start and end apart: 22, of which 3 were waited for; matrix products, arithmetic and copies ran while one was open for 2% of the time, Pallas kernels for 41%

profile of v4, /device:TPU:1, one launch (start us, length us, event | category | flops | bytes accessed | tf_op | source)
XLA Modules:
  0.0 111.4 jit_solution(14135543724545465081)
XLA Ops:
  0.0 0.1 pad_add_fusion.at_ref
  0.1 1.3 %copy-done.1 = bf16[256,2304]{1,0:T(8,128)(2,1)S(1)} copy-done((bf16[256,2304]{1,0:T(8,128)(2,1)S(1)}, bf16[256,2304]{1,0:T(8,128)(2,1)}, u32[]{:S(2)}) %copy-start.1) | copy-done | bytes 1179672
  1.3 1.0 turned.1
  2.3 1.5 %collective-permute-start = (bf16[1152,256]{1,0:T(8,128)(2,1)S(1)}, bf16[1152,256]{1,0:T(8,128)(2,1)S(1)}, u32[]{:S(2)}, u32[]{:S(2)}) collective-permute-start(bf16[1152,256]{1,0:T(8,128)(2,1)S(1)} %get-tuple-element.42), channel_id=1, source_target_pairs={{0,1},{1,0},{2,3},{3,2},{4,5},{5,4},{6,7},{7,6},{8,9},{9,8},{10,11... | collective-permute-start | bytes 1769480 | tf_op jit(solution)/shard_map/ppermute | solution.py:703
  3.8 0.9 slice.9
  4.7 3.6 %collective-permute-start.1 = (bf16[16,2304]{1,0:T(8,128)(2,1)S(1)}, bf16[16,2304]{1,0:T(8,128)(2,1)S(1)}, u32[]{:S(2)}, u32[]{:S(2)}) collective-permute-start(bf16[16,2304]{1,0:T(8,128)(2,1)S(1)} %slice.9), channel_id=1, source_target_pairs={{0,8},{8,16},{16,24},{24,32},{32,40},{40,48},{48,56},{56,64},{64,7... | collective-permute-start | bytes 221192 | tf_op jit(solution)/shard_map/ppermute | solution.py:707
  8.4 0.6 pad_add_fusion.1.at_ref
  9.0 0.0 collective-permute-done
  9.1 1.4 %collective-permute-start.2 = (bf16[2304,256]{1,0:T(8,128)(2,1)S(1)}, bf16[2304,256]{1,0:T(8,128)(2,1)S(1)}, u32[]{:S(2)}, u32[]{:S(2)}) collective-permute-start(bf16[2304,256]{1,0:T(8,128)(2,1)S(1)} %constant_dynamic-update-slice_fusion.refs_0_.refs_4_), channel_id=1, source_target_pairs={{0,2},{1,3},{2,4},{3,5},{4,6},{5,7},{6,0},{7,1},{8,10},{9,11},{10,... | collective-permute-start | bytes 3538952 | tf_op jit(solution)/shard_map/ppermute | solution.py:700
  10.5 1.5 %collective-permute-start.3 = (bf16[2304,256]{1,0:T(8,128)(2,1)S(1)}, bf16[2304,256]{1,0:T(8,128)(2,1)S(1)}, u32[]{:S(2)}, u32[]{:S(2)}) collective-permute-start(bf16[2304,256]{1,0:T(8,128)(2,1)S(1)} %constant_dynamic-update-slice_fusion.refs_0_.refs_4_), channel_id=1, source_target_pairs={{0,6},{1,7},{2,0},{3,1},{4,2},{5,3},{6,4},{7,5},{8,14},{9,15},{10,... | collective-permute-start | bytes 3538952 | tf_op jit(solution)/shard_map/ppermute | solution.py:700
  12.0 0.0 collective-permute-done.1.halo_ref
  12.0 0.6 copy-done.7
  12.6 24.4 %local_part.1 = (f32[2048,128]{1,0:T(8,128)}, bf16[2048,256]{1,0:T(8,128)(2,1)}, bf16[2048,256]{1,0:T(8,128)(2,1)}, bf16[2048,256]{1,0:T(8,128)(2,1)}, bf16[2048...) custom-call(bf16[2048,2304]{1,0:T(8,128)(2,1)} %x_ref.3, ...), custom_call_target="tpu_custom_call" | custom-call | flops 14000000000 | bytes 24000000 | tf_op jit(solution)/shard_map/local_part/pallas_call | solution.py:268
  37.0 3.4 %collective-permute-start.5 = (bf16[128,512]{1,0:T(8,128)(2,1)}, bf16[128,512]{1,0:T(8,128)(2,1)S(1)}, u32[]{:S(2)}, u32[]{:S(2)}) collective-permute-start(bf16[128,512]{1,0:T(8,128)(2,1)} %get-tuple-element.46.own), channel_id=1, source_target_pairs={{0,16},{8,24},{16,0},{24,8},{32,48},{40,56},{48,32},{56,40},{64,80... | collective-permute-start | bytes 393224 | tf_op jit(solution)/shard_map/ppermute | solution.py:719
  40.4 0.0 collective-permute-start.4
  40.4 2.7 %collective-permute-start.6 = (bf16[128,512]{1,0:T(8,128)(2,1)}, bf16[128,512]{1,0:T(8,128)(2,1)S(1)}, u32[]{:S(2)}, u32[]{:S(2)}) collective-permute-start(bf16[128,512]{1,0:T(8,128)(2,1)} %get-tuple-element.46.own), channel_id=1, source_target_pairs={{0,24},{8,0},{16,8},{24,16},{32,56},{40,32},{48,40},{56,48},{64,88... | collective-permute-start | bytes 393224 | tf_op jit(solution)/shard_map/ppermute | solution.py:719
  43.1 0.0 collective-permute-done.2.refs_1_.refs_5_
  43.1 0.0 collective-permute-done.3.refs_2_.refs_6_
  43.2 1.7 %collective-permute-start.8 = (bf16[1152,256]{1,0:T(8,128)(2,1)S(1)}, bf16[1152,256]{1,0:T(8,128)(2,1)S(1)}, u32[]{:S(2)}, u32[]{:S(2)}) collective-permute-start(bf16[1152,256]{1,0:T(8,128)(2,1)S(1)} %slice.10), channel_id=1, source_target_pairs={{0,6},{1,7},{2,0},{3,1},{4,2},{5,3},{6,4},{7,5},{8,14},{9,15},{10,... | collective-permute-start | bytes 1769480 | tf_op jit(solution)/shard_map/ppermute | solution.py:700
  44.9 0.1 collective-permute-start.9
  45.0 11.4 %query_part.1 = (bf16[2048,128]{1,0:T(8,128)(2,1)}, bf16[2048,256]{1,0:T(8,128)(2,1)}, bf16[2048,256]{1,0:T(8,128)(2,1)}) custom-call(bf16[2048,2304]{1,0:T(8,128)(2,1)} %x_ref.3, bf16[16,2304]{1,0:T(8,128)(2,1)} %copy-done.7, f32[18,128]{1,0:T(8,128)} %bitcast.14, bf16[3,2304,256]{2,1,0:T(8,128)(2,1)} %w_ref.3, bf16[3,4,256]{2,1,0:T(4,128)(2,1)} %conv_ref.3, ...), custom_call_target="tpu_custom_call" | custom-call | flops 4000000000 | bytes 17000000 | tf_op jit(solution)/shard_map/query_part/pallas_call | solution.py:412
  56.3 0.0 collective-permute-done.5.two
  56.3 0.0 collective-permute-done.4.one
  56.3 0.0 collective-permute-done.6.three
  56.4 0.6 compose.1
  57.0 0.6 copy-done.2
  57.6 1.2 %collective-permute-start.7 = (bf16[128,512]{1,0:T(8,128)(2,1)S(1)}, bf16[128,512]{1,0:T(8,128)(2,1)S(1)}, u32[]{:S(2)}, u32[]{:S(2)}) collective-permute-start(bf16[128,512]{1,0:T(8,128)(2,1)S(1)} %get-tuple-element.53), channel_id=1, source_target_pairs={{0,32},{8,40},{16,48},{24,56},{32,64},{40,72},{48,80},{56,88},{64,... | collective-permute-start | bytes 393224 | tf_op jit(solution)/shard_map/ppermute | solution.py:723
  58.8 2.5 %collective-permute-start.10 = (bf16[128,512]{1,0:T(8,128)(2,1)S(1)}, bf16[128,512]{1,0:T(8,128)(2,1)S(1)}, u32[]{:S(2)}, u32[]{:S(2)}) collective-permute-start(bf16[128,512]{1,0:T(8,128)(2,1)S(1)} %get-tuple-element.53), channel_id=1, source_target_pairs={{0,64},{8,72},{16,80},{24,88},{32,96},{40,104},{48,112},{56,120},{... | collective-permute-start | bytes 393224 | tf_op jit(solution)/shard_map/ppermute | solution.py:723
  61.3 1.1 %collective-permute-start.11 = (bf16[128,512]{1,0:T(8,128)(2,1)S(1)}, bf16[128,512]{1,0:T(8,128)(2,1)S(1)}, u32[]{:S(2)}, u32[]{:S(2)}) collective-permute-start(bf16[128,512]{1,0:T(8,128)(2,1)S(1)} %get-tuple-element.53), channel_id=1, source_target_pairs={{0,96},{8,104},{16,112},{24,120},{32,0},{40,8},{48,16},{56,24},{64... | collective-permute-start | bytes 393224 | tf_op jit(solution)/shard_map/ppermute | solution.py:723
  62.4 5.3 %reading_part.1 = (bf16[2048,256]{1,0:T(8,128)(2,1)}, bf16[2048,256]{1,0:T(8,128)(2,1)}, bf16[2048,256]{1,0:T(8,128)(2,1)}) custom-call(bf16[2048,256]{1,0:T(8,128)(2,1)} %get-tuple-element.58.m_ref, bf16[2048,256]{1,0:T(8,128)(2,1)} %get-tuple-element.59.q_ref, bf16[2048,256]{1,0:T(8,128)(2,1)} %get-tuple-element.60.u_ref, ...), custom_call_target="tpu_custom_call" | custom-call | flops 3000000000 | bytes 12000000 | tf_op jit(solution)/shard_map/reading_part/pallas_call | solution.py:469
  67.7 0.0 collective-permute-done.7.one
  67.7 0.0 collective-permute-done.8.refs_3_
  67.7 0.0 collective-permute-done.9.refs_7_
  67.7 0.0 collective-permute-done.10.two
  67.8 0.0 collective-permute-done.11.three
  67.8 0.6 copy-done.4
  68.4 0.0 copy-done.5
  68.4 0.1 copy-done.6
  68.5 4.6 %gated_part.1 = (bf16[512,256]{1,0:T(8,128)(2,1)}, bf16[512,256]{1,0:T(8,128)(2,1)}, bf16[512,256]{1,0:T(8,128)(2,1)}, bf16[512,256]{1,0:T(8,128)(2,1)}) custom-call(s32[2]{0:T(128)} %pad_add_fusion.1.at_ref, bf16[128,512]{1,0:T(8,128)(2,1)} %copy-done.4, bf16[128,512]{1,0:T(8,128)(2,1)} %copy-done.5, bf16[128,512]{1,0:T(8,128)(2,1)} %copy-done.6, ...), custom_call_target="tpu_custom_call" | custom-call | flops 300000000 | bytes 4000000 | tf_op jit(solution)/shard_map/gated_part/pallas_call | solution.py:563
  73.0 0.1 collective-permute-start.12
  73.1 2.7 %collective-permute-start.13 = (bf16[512,256]{1,0:T(8,128)(2,1)}, bf16[512,256]{1,0:T(8,128)(2,1)S(1)}, u32[]{:S(2)}, u32[]{:S(2)}) collective-permute-start(bf16[512,256]{1,0:T(8,128)(2,1)} %get-tuple-element.69), channel_id=1, source_target_pairs={{0,6},{1,7},{2,0},{3,1},{4,2},{5,3},{6,4},{7,5},{8,14},{9,15},{10,... | collective-permute-start | bytes 786440 | tf_op jit(solution)/shard_map/ppermute | solution.py:700
  75.8 1.1 collective-permute-start.14
  76.9 3.6 %collective-permute-start.15 = (bf16[512,256]{1,0:T(8,128)(2,1)}, bf16[512,256]{1,0:T(8,128)(2,1)S(1)}, u32[]{:S(2)}, u32[]{:S(2)}) collective-permute-start(bf16[512,256]{1,0:T(8,128)(2,1)} %get-tuple-element.67.refs_8_), channel_id=1, source_target_pairs={{0,1},{1,0},{2,3},{3,2},{4,5},{5,4},{6,7},{7,6},{8,9},{9,8},{10,11... | collective-permute-start | bytes 786440 | tf_op jit(solution)/shard_map/ppermute | solution.py:703
  80.5 0.0 collective-permute-done.12.refs_9_
  80.5 6.0 %collective-permute-start.16 = (bf16[512,256]{1,0:T(8,128)(2,1)S(1)}, bf16[512,256]{1,0:T(8,128)(2,1)S(1)}, u32[]{:S(2)}, u32[]{:S(2)}) collective-permute-start(bf16[512,256]{1,0:T(8,128)(2,1)S(1)} %collective-permute-done.12.refs_9_), channel_id=1, source_target_pairs={{0,1},{1,0},{2,3},{3,2},{4,5},{5,4},{6,7},{7,6},{8,9},{9,8},{10,11... | collective-permute-start | bytes 786440 | tf_op jit(solution)/shard_map/ppermute | solution.py:703
  86.5 0.0 collective-permute-done.13.refs_10_
  86.5 1.8 %collective-permute-start.17 = (bf16[512,256]{1,0:T(8,128)(2,1)S(1)}, bf16[512,256]{1,0:T(8,128)(2,1)S(1)}, u32[]{:S(2)}, u32[]{:S(2)}) collective-permute-start(bf16[512,256]{1,0:T(8,128)(2,1)S(1)} %collective-permute-done.13.refs_10_), channel_id=1, source_target_pairs={{0,1},{1,0},{2,3},{3,2},{4,5},{5,4},{6,7},{7,6},{8,9},{9,8},{10,11... | collective-permute-start | bytes 786440 | tf_op jit(solution)/shard_map/ppermute | solution.py:703
  88.3 0.0 collective-permute-done.14.refs_11_
  88.3 1.7 %collective-permute-start.18 = (bf16[512,256]{1,0:T(8,128)(2,1)S(1)}, bf16[512,256]{1,0:T(8,128)(2,1)S(1)}, u32[]{:S(2)}, u32[]{:S(2)}) collective-permute-start(bf16[512,256]{1,0:T(8,128)(2,1)S(1)} %collective-permute-done.14.refs_11_), channel_id=1, source_target_pairs={{0,1},{1,0},{2,3},{3,2},{4,5},{5,4},{6,7},{7,6},{8,9},{9,8},{10,11... | collective-permute-start | bytes 786440 | tf_op jit(solution)/shard_map/ppermute | solution.py:703
  90.0 0.0 collective-permute-done.15.refs_12_
  90.0 0.0 collective-permute-done.16.refs_13_
  90.0 0.0 collective-permute-done.17.refs_14_
  90.0 1.1 %collective-permute-done.18.refs_15_ = bf16[512,256]{1,0:T(8,128)(2,1)S(1)} collective-permute-done((bf16[512,256]{1,0:T(8,128)(2,1)S(1)}, bf16[512,256]{1,0:T(8,128)(2,1)S(1)}, u32[]{:S(2)}, u32[]{:S(2)}) %collective-permute-start.18) | collective-permute-done | bytes 262176 | tf_op jit(solution)/shard_map/ppermute | solution.py:703
  91.2 0.9 copy-done
  92.1 1.3 %mixed_part.3 = bf16[288,512]{1,0:T(8,128)(2,1)S(1)} custom-call(s32[2]{0:T(128)S(1)} %pad_add_fusion.at_ref, bf16[2304,256]{1,0:T(8,128)(2,1)S(1)} %constant_dynamic-update-slice_fusion.refs_0_.refs_4_, bf16[2304,256]{1,0:T(8,128)(2,1)S(1)} %collective-permute-done.2.refs_1_.refs_5_, bf16[2304,256]{1,0:T(8,128)(2,1)S(1)} %collective-permute-done.3.refs_2_.refs_6_, ...), custom_call_target="tpu_custom_call" | custom-call | flops 600000000 | bytes 3500000 | tf_op jit(solution)/shard_map/mixed_part/pallas_call | solution.py:638
  93.5 0.8 collective-permute-start.19
  94.3 2.2 %mixed_part.5 = (bf16[288,512]{1,0:T(8,128)(2,1)S(1)}, bf16[288,512]{1,0:T(8,128)(2,1)S(1)}) custom-call(s32[2]{0:T(128)S(1)} %pad_add_fusion.at_ref, bf16[2304,256]{1,0:T(8,128)(2,1)S(1)} %constant_dynamic-update-slice_fusion.refs_0_.refs_4_, bf16[2304,256]{1,0:T(8,128)(2,1)S(1)} %collective-permute-done.2.refs_1_.refs_5_, ...), custom_call_target="tpu_custom_call" | custom-call | flops 1200000000 | bytes 5000000 | tf_op jit(solution)/shard_map/mixed_part/pallas_call | solution.py:638
  96.5 1.9 %collective-permute-start.20 = (bf16[288,512]{1,0:T(8,128)(2,1)S(1)}, bf16[288,512]{1,0:T(8,128)(2,1)S(1)}, u32[]{:S(2)}, u32[]{:S(2)}) collective-permute-start(bf16[288,512]{1,0:T(8,128)(2,1)S(1)} %get-tuple-element.74), channel_id=1, source_target_pairs={{0,2},{1,3},{2,4},{3,5},{4,6},{5,7},{6,0},{7,1},{8,10},{9,11},{10,... | collective-permute-start | bytes 884744 | tf_op jit(solution)/shard_map/ppermute | solution.py:700
  98.4 0.9 collective-permute-start.21
  99.3 4.1 %collective-permute-done.19.refs_2_ = bf16[288,512]{1,0:T(8,128)(2,1)S(1)} collective-permute-done((bf16[288,512]{1,0:T(8,128)(2,1)S(1)}, bf16[288,512]{1,0:T(8,128)(2,1)S(1)}, u32[]{:S(2)}, u32[]{:S(2)}) %collective-permute-start.19) | collective-permute-done | bytes 294944 | tf_op jit(solution)/shard_map/ppermute | solution.py:700
  103.3 1.3 %mixed_part.4.refs_0_ = bf16[288,512]{1,0:T(8,128)(2,1)S(1)} custom-call(s32[2]{0:T(128)S(1)} %pad_add_fusion.at_ref, bf16[2304,256]{1,0:T(8,128)(2,1)S(1)} %constant_dynamic-update-slice_fusion.refs_0_.refs_4_, bf16[2304,256]{1,0:T(8,128)(2,1)S(1)} %collective-permute-done.2.refs_1_.refs_5_, bf16[2304,256]{1,0:T(8,128)(2,1)S(1)} %collective-permute-done.3.refs_2_.refs_6_, ...), custom_call_target="tpu_custom_call" | custom-call | flops 600000000 | bytes 3500000 | tf_op jit(solution)/shard_map/mixed_part/pallas_call | solution.py:638
  104.7 5.6 %collective-permute-done.20.refs_1_ = bf16[288,512]{1,0:T(8,128)(2,1)S(1)} collective-permute-done((bf16[288,512]{1,0:T(8,128)(2,1)S(1)}, bf16[288,512]{1,0:T(8,128)(2,1)S(1)}, u32[]{:S(2)}, u32[]{:S(2)}) %collective-permute-start.20) | collective-permute-done | bytes 294944 | tf_op jit(solution)/shard_map/ppermute | solution.py:700
  110.3 0.0 collective-permute-done.21.refs_3_
  110.3 1.1 joined.1
  (13 shorter events, 0.2 us)
Async XLA Ops:
  0.1 1.3 %copy-start.1 = (bf16[256,2304]{1,0:T(8,128)(2,1)S(1)}, bf16[256,2304]{1,0:T(8,128)(2,1)}, u32[]{:S(2)}) copy-start(bf16[256,2304]{1,0:T(8,128)(2,1)} %w_ref.2) | copy-start | bytes 3538948
  2.3 6.7 %collective-permute-start = (bf16[1152,256]{1,0:T(8,128)(2,1)S(1)}, bf16[1152,256]{1,0:T(8,128)(2,1)S(1)}, u32[]{:S(2)}, u32[]{:S(2)}) collective-permute-start(bf16[1152,256]{1,0:T(8,128)(2,1)S(1)} %get-tuple-element.42), channel_id=1, source_target_pairs={{0,1},{1,0},{2,3},{3,2},{4,5},{5,4},{6,7},{7,6},{8,9},{9,8},{10,11... | collective-permute-start | bytes 1769480 | tf_op jit(solution)/shard_map/ppermute | solution.py:703
  4.7 7.3 %collective-permute-start.1 = (bf16[16,2304]{1,0:T(8,128)(2,1)S(1)}, bf16[16,2304]{1,0:T(8,128)(2,1)S(1)}, u32[]{:S(2)}, u32[]{:S(2)}) collective-permute-start(bf16[16,2304]{1,0:T(8,128)(2,1)S(1)} %slice.9), channel_id=1, source_target_pairs={{0,8},{8,16},{16,24},{24,32},{32,40},{40,48},{48,56},{56,64},{64,7... | collective-permute-start | bytes 221192 | tf_op jit(solution)/shard_map/ppermute | solution.py:707
  9.1 34.0 %collective-permute-start.2 = (bf16[2304,256]{1,0:T(8,128)(2,1)S(1)}, bf16[2304,256]{1,0:T(8,128)(2,1)S(1)}, u32[]{:S(2)}, u32[]{:S(2)}) collective-permute-start(bf16[2304,256]{1,0:T(8,128)(2,1)S(1)} %constant_dynamic-update-slice_fusion.refs_0_.refs_4_), channel_id=1, source_target_pairs={{0,2},{1,3},{2,4},{3,5},{4,6},{5,7},{6,0},{7,1},{8,10},{9,11},{10,... | collective-permute-start | bytes 3538952 | tf_op jit(solution)/shard_map/ppermute | solution.py:700
  10.5 32.6 %collective-permute-start.3 = (bf16[2304,256]{1,0:T(8,128)(2,1)S(1)}, bf16[2304,256]{1,0:T(8,128)(2,1)S(1)}, u32[]{:S(2)}, u32[]{:S(2)}) collective-permute-start(bf16[2304,256]{1,0:T(8,128)(2,1)S(1)} %constant_dynamic-update-slice_fusion.refs_0_.refs_4_), channel_id=1, source_target_pairs={{0,6},{1,7},{2,0},{3,1},{4,2},{5,3},{6,4},{7,5},{8,14},{9,15},{10,... | collective-permute-start | bytes 3538952 | tf_op jit(solution)/shard_map/ppermute | solution.py:700
  12.0 0.6 copy-start.7
  37.0 19.3 %collective-permute-start.5 = (bf16[128,512]{1,0:T(8,128)(2,1)}, bf16[128,512]{1,0:T(8,128)(2,1)S(1)}, u32[]{:S(2)}, u32[]{:S(2)}) collective-permute-start(bf16[128,512]{1,0:T(8,128)(2,1)} %get-tuple-element.46.own), channel_id=1, source_target_pairs={{0,16},{8,24},{16,0},{24,8},{32,48},{40,56},{48,32},{56,40},{64,80... | collective-permute-start | bytes 393224 | tf_op jit(solution)/shard_map/ppermute | solution.py:719
  40.4 15.9 %collective-permute-start.4 = (bf16[128,512]{1,0:T(8,128)(2,1)}, bf16[128,512]{1,0:T(8,128)(2,1)S(1)}, u32[]{:S(2)}, u32[]{:S(2)}) collective-permute-start(bf16[128,512]{1,0:T(8,128)(2,1)} %get-tuple-element.46.own), channel_id=1, source_target_pairs={{0,8},{8,16},{16,24},{24,0},{32,40},{40,48},{48,56},{56,32},{64,72... | collective-permute-start | bytes 393224 | tf_op jit(solution)/shard_map/ppermute | solution.py:719
  40.4 15.9 %collective-permute-start.6 = (bf16[128,512]{1,0:T(8,128)(2,1)}, bf16[128,512]{1,0:T(8,128)(2,1)S(1)}, u32[]{:S(2)}, u32[]{:S(2)}) collective-permute-start(bf16[128,512]{1,0:T(8,128)(2,1)} %get-tuple-element.46.own), channel_id=1, source_target_pairs={{0,24},{8,0},{16,8},{24,16},{32,56},{40,32},{48,40},{56,48},{64,88... | collective-permute-start | bytes 393224 | tf_op jit(solution)/shard_map/ppermute | solution.py:719
  43.2 24.6 %collective-permute-start.8 = (bf16[1152,256]{1,0:T(8,128)(2,1)S(1)}, bf16[1152,256]{1,0:T(8,128)(2,1)S(1)}, u32[]{:S(2)}, u32[]{:S(2)}) collective-permute-start(bf16[1152,256]{1,0:T(8,128)(2,1)S(1)} %slice.10), channel_id=1, source_target_pairs={{0,6},{1,7},{2,0},{3,1},{4,2},{5,3},{6,4},{7,5},{8,14},{9,15},{10,... | collective-permute-start | bytes 1769480 | tf_op jit(solution)/shard_map/ppermute | solution.py:700
  44.9 22.9 %collective-permute-start.9 = (bf16[1152,256]{1,0:T(8,128)(2,1)S(1)}, bf16[1152,256]{1,0:T(8,128)(2,1)S(1)}, u32[]{:S(2)}, u32[]{:S(2)}) collective-permute-start(bf16[1152,256]{1,0:T(8,128)(2,1)S(1)} %slice.11), channel_id=1, source_target_pairs={{0,2},{1,3},{2,4},{3,5},{4,6},{5,7},{6,0},{7,1},{8,10},{9,11},{10,... | collective-permute-start | bytes 1769480 | tf_op jit(solution)/shard_map/ppermute | solution.py:700
  45.0 11.4 %copy-start.3 = (bf16[128,512]{1,0:T(8,128)(2,1)S(1)}, bf16[128,512]{1,0:T(8,128)(2,1)}, u32[]{:S(2)}) copy-start(bf16[128,512]{1,0:T(8,128)(2,1)} %get-tuple-element.46.own) | copy-start | bytes 393220
  57.0 0.7 copy-start.2
  57.6 10.1 %collective-permute-start.7 = (bf16[128,512]{1,0:T(8,128)(2,1)S(1)}, bf16[128,512]{1,0:T(8,128)(2,1)S(1)}, u32[]{:S(2)}, u32[]{:S(2)}) collective-permute-start(bf16[128,512]{1,0:T(8,128)(2,1)S(1)} %get-tuple-element.53), channel_id=1, source_target_pairs={{0,32},{8,40},{16,48},{24,56},{32,64},{40,72},{48,80},{56,88},{64,... | collective-permute-start | bytes 393224 | tf_op jit(solution)/shard_map/ppermute | solution.py:723
  58.8 8.9 %collective-permute-start.10 = (bf16[128,512]{1,0:T(8,128)(2,1)S(1)}, bf16[128,512]{1,0:T(8,128)(2,1)S(1)}, u32[]{:S(2)}, u32[]{:S(2)}) collective-permute-start(bf16[128,512]{1,0:T(8,128)(2,1)S(1)} %get-tuple-element.53), channel_id=1, source_target_pairs={{0,64},{8,72},{16,80},{24,88},{32,96},{40,104},{48,112},{56,120},{... | collective-permute-start | bytes 393224 | tf_op jit(solution)/shard_map/ppermute | solution.py:723
  61.3 6.5 %collective-permute-start.11 = (bf16[128,512]{1,0:T(8,128)(2,1)S(1)}, bf16[128,512]{1,0:T(8,128)(2,1)S(1)}, u32[]{:S(2)}, u32[]{:S(2)}) collective-permute-start(bf16[128,512]{1,0:T(8,128)(2,1)S(1)} %get-tuple-element.53), channel_id=1, source_target_pairs={{0,96},{8,104},{16,112},{24,120},{32,0},{40,8},{48,16},{56,24},{64... | collective-permute-start | bytes 393224 | tf_op jit(solution)/shard_map/ppermute | solution.py:723
  67.7 0.7 copy-start.4
  67.7 0.7 copy-start.5
  67.8 0.7 copy-start.6
  73.0 7.5 %collective-permute-start.12 = (bf16[512,256]{1,0:T(8,128)(2,1)}, bf16[512,256]{1,0:T(8,128)(2,1)S(1)}, u32[]{:S(2)}, u32[]{:S(2)}) collective-permute-start(bf16[512,256]{1,0:T(8,128)(2,1)} %get-tuple-element.68), channel_id=1, source_target_pairs={{0,2},{1,3},{2,4},{3,5},{4,6},{5,7},{6,0},{7,1},{8,10},{9,11},{10,... | collective-permute-start | bytes 786440 | tf_op jit(solution)/shard_map/ppermute | solution.py:700
  73.1 13.4 %collective-permute-start.13 = (bf16[512,256]{1,0:T(8,128)(2,1)}, bf16[512,256]{1,0:T(8,128)(2,1)S(1)}, u32[]{:S(2)}, u32[]{:S(2)}) collective-permute-start(bf16[512,256]{1,0:T(8,128)(2,1)} %get-tuple-element.69), channel_id=1, source_target_pairs={{0,6},{1,7},{2,0},{3,1},{4,2},{5,3},{6,4},{7,5},{8,14},{9,15},{10,... | collective-permute-start | bytes 786440 | tf_op jit(solution)/shard_map/ppermute | solution.py:700
  75.8 12.5 %collective-permute-start.14 = (bf16[512,256]{1,0:T(8,128)(2,1)}, bf16[512,256]{1,0:T(8,128)(2,1)S(1)}, u32[]{:S(2)}, u32[]{:S(2)}) collective-permute-start(bf16[512,256]{1,0:T(8,128)(2,1)} %get-tuple-element.70), channel_id=1, source_target_pairs={{0,4},{1,5},{2,6},{3,7},{4,0},{5,1},{6,2},{7,3},{8,12},{9,13},{10,... | collective-permute-start | bytes 786440 | tf_op jit(solution)/shard_map/ppermute | solution.py:700
  76.9 13.1 %collective-permute-start.15 = (bf16[512,256]{1,0:T(8,128)(2,1)}, bf16[512,256]{1,0:T(8,128)(2,1)S(1)}, u32[]{:S(2)}, u32[]{:S(2)}) collective-permute-start(bf16[512,256]{1,0:T(8,128)(2,1)} %get-tuple-element.67.refs_8_), channel_id=1, source_target_pairs={{0,1},{1,0},{2,3},{3,2},{4,5},{5,4},{6,7},{7,6},{8,9},{9,8},{10,11... | collective-permute-start | bytes 786440 | tf_op jit(solution)/shard_map/ppermute | solution.py:703
  80.5 9.5 %collective-permute-start.16 = (bf16[512,256]{1,0:T(8,128)(2,1)S(1)}, bf16[512,256]{1,0:T(8,128)(2,1)S(1)}, u32[]{:S(2)}, u32[]{:S(2)}) collective-permute-start(bf16[512,256]{1,0:T(8,128)(2,1)S(1)} %collective-permute-done.12.refs_9_), channel_id=1, source_target_pairs={{0,1},{1,0},{2,3},{3,2},{4,5},{5,4},{6,7},{7,6},{8,9},{9,8},{10,11... | collective-permute-start | bytes 786440 | tf_op jit(solution)/shard_map/ppermute | solution.py:703
  86.5 3.5 %collective-permute-start.17 = (bf16[512,256]{1,0:T(8,128)(2,1)S(1)}, bf16[512,256]{1,0:T(8,128)(2,1)S(1)}, u32[]{:S(2)}, u32[]{:S(2)}) collective-permute-start(bf16[512,256]{1,0:T(8,128)(2,1)S(1)} %collective-permute-done.13.refs_10_), channel_id=1, source_target_pairs={{0,1},{1,0},{2,3},{3,2},{4,5},{5,4},{6,7},{7,6},{8,9},{9,8},{10,11... | collective-permute-start | bytes 786440 | tf_op jit(solution)/shard_map/ppermute | solution.py:703
  88.3 2.9 %collective-permute-start.18 = (bf16[512,256]{1,0:T(8,128)(2,1)S(1)}, bf16[512,256]{1,0:T(8,128)(2,1)S(1)}, u32[]{:S(2)}, u32[]{:S(2)}) collective-permute-start(bf16[512,256]{1,0:T(8,128)(2,1)S(1)} %collective-permute-done.14.refs_11_), channel_id=1, source_target_pairs={{0,1},{1,0},{2,3},{3,2},{4,5},{5,4},{6,7},{7,6},{8,9},{9,8},{10,11... | collective-permute-start | bytes 786440 | tf_op jit(solution)/shard_map/ppermute | solution.py:703
  91.2 0.9 copy-start
  93.5 9.8 %collective-permute-start.19 = (bf16[288,512]{1,0:T(8,128)(2,1)S(1)}, bf16[288,512]{1,0:T(8,128)(2,1)S(1)}, u32[]{:S(2)}, u32[]{:S(2)}) collective-permute-start(bf16[288,512]{1,0:T(8,128)(2,1)S(1)} %mixed_part.3), channel_id=1, source_target_pairs={{0,4},{1,5},{2,6},{3,7},{4,0},{5,1},{6,2},{7,3},{8,12},{9,13},{10,... | collective-permute-start | bytes 884744 | tf_op jit(solution)/shard_map/ppermute | solution.py:700
  96.5 13.8 %collective-permute-start.20 = (bf16[288,512]{1,0:T(8,128)(2,1)S(1)}, bf16[288,512]{1,0:T(8,128)(2,1)S(1)}, u32[]{:S(2)}, u32[]{:S(2)}) collective-permute-start(bf16[288,512]{1,0:T(8,128)(2,1)S(1)} %get-tuple-element.74), channel_id=1, source_target_pairs={{0,2},{1,3},{2,4},{3,5},{4,6},{5,7},{6,0},{7,1},{8,10},{9,11},{10,... | collective-permute-start | bytes 884744 | tf_op jit(solution)/shard_map/ppermute | solution.py:700
  98.4 11.9 %collective-permute-start.21 = (bf16[288,512]{1,0:T(8,128)(2,1)S(1)}, bf16[288,512]{1,0:T(8,128)(2,1)S(1)}, u32[]{:S(2)}, u32[]{:S(2)}) collective-permute-start(bf16[288,512]{1,0:T(8,128)(2,1)S(1)} %get-tuple-element.76), channel_id=1, source_target_pairs={{0,6},{1,7},{2,0},{3,1},{4,2},{5,3},{6,4},{7,5},{8,14},{9,15},{10,... | collective-permute-start | bytes 884744 | tf_op jit(solution)/shard_map/ppermute | solution.py:700

commit v5 on v4

--- a/solution.py
+++ b/solution.py
@@ -748,7 +748,8 @@
     x1, far = lax.optimization_barrier((x1, far))
     at = jnp.stack([xi, yi])
     q0, q1, q2, q3 = gated_part(at, x1, x2, x3, before, o, r, s)
-    own = [q0, along_y(q1, 1), along_y(q3, 3), along_y(q2, 2)]
+    opposite = along_y(q2, 2)
+    own = [q0, along_y(q1, 1), along_y(q3, 3), opposite]
     weights = [(both, 0, 8), (below, 0, 8), (above, 0, 8), (far[0], 0, 4)]
     weights += [(both, 4, 8), (below, 4, 8), (above, 4, 8), (far[1], 0, 4)]
     blocks = own, [across(a) for a in own]

time: 112 us -> 112 us (level)
  no operation moved by 1% of the time
where the time goes in v5:
time: 112 us; the launch traced here: 111 us
  Pallas kernels  53.2 us (48%)
  starting transfers between devices  41.1 us (37%)
  waiting for transfers between devices  10.9 us (10%)
  local copies, waits for them, and re-layouts  5.23 us (5%)
    pallas_call x1, Pallas kernels, local_part(): pl.pallas_call(local_kernel, grid=(grid + 1,), in_specs=[early(d), whole(...  24.4 us
    ppermute x5, starting transfers between devices, across(): return lax.ppermute(a, 'head', [(i, i ^ 1) for i in range(8)])  14.6 us
    ppermute x10, starting transfers between devices, along_y(): return lax.ppermute(a, 'head', [(i, (i + 2 * by) % 8) for i in range(8)])  12.1 us
    pallas_call x1, Pallas kernels, query_part(): pl.pallas_call(query_kernel, grid=(grid + 1,), in_specs=[early(d), whole(...  11.4 us
    ppermute x10, waiting for transfers between devices, along_y(): return lax.ppermute(a, 'head', [(i, (i + 2 * by) % 8) for i in range(8)])  9.71 us
    ppermute x3, starting transfers between devices, along_z(): return lax.ppermute(a, 'ctx', pairs)  6.05 us
    pallas_call x1, Pallas kernels, reading_part(): pl.pallas_call(reading_kernel, grid=(tokens // (2 * TILE),), in_specs=[ro...  5.29 us
    pallas_call x3, Pallas kernels, mixed_part(): pl.pallas_call(mixed_kernel, grid_spec=pltpu.PrefetchScalarGridSpec(num_s...  4.93 us
  transfers between devices with their start and end apart: 22, of which 3 were waited for; matrix products, arithmetic and copies ran while one was open for 2% of the time, Pallas kernels for 41%

profile of v5, /device:TPU:1, one launch (start us, length us, event | category | flops | bytes accessed | tf_op | source)
XLA Modules:
  0.0 111.4 jit_solution(14135543724545465081)
XLA Ops:
  0.0 0.1 pad_add_fusion.at_ref
  0.1 1.3 %copy-done.1 = bf16[256,2304]{1,0:T(8,128)(2,1)S(1)} copy-done((bf16[256,2304]{1,0:T(8,128)(2,1)S(1)}, bf16[256,2304]{1,0:T(8,128)(2,1)}, u32[]{:S(2)}) %copy-start.1) | copy-done | bytes 1179672
  1.3 1.0 turned.1
  2.3 1.5 %collective-permute-start = (bf16[1152,256]{1,0:T(8,128)(2,1)S(1)}, bf16[1152,256]{1,0:T(8,128)(2,1)S(1)}, u32[]{:S(2)}, u32[]{:S(2)}) collective-permute-start(bf16[1152,256]{1,0:T(8,128)(2,1)S(1)} %get-tuple-element.42), channel_id=1, source_target_pairs={{0,1},{1,0},{2,3},{3,2},{4,5},{5,4},{6,7},{7,6},{8,9},{9,8},{10,11... | collective-permute-start | bytes 1769480 | tf_op jit(solution)/shard_map/ppermute | solution.py:703
  3.8 0.9 slice.9
  4.7 3.6 %collective-permute-start.1 = (bf16[16,2304]{1,0:T(8,128)(2,1)S(1)}, bf16[16,2304]{1,0:T(8,128)(2,1)S(1)}, u32[]{:S(2)}, u32[]{:S(2)}) collective-permute-start(bf16[16,2304]{1,0:T(8,128)(2,1)S(1)} %slice.9), channel_id=1, source_target_pairs={{0,8},{8,16},{16,24},{24,32},{32,40},{40,48},{48,56},{56,64},{64,7... | collective-permute-start | bytes 221192 | tf_op jit(solution)/shard_map/ppermute | solution.py:707
  8.4 0.6 pad_add_fusion.1.at_ref
  9.0 0.0 collective-permute-done
  9.1 1.4 %collective-permute-start.2 = (bf16[2304,256]{1,0:T(8,128)(2,1)S(1)}, bf16[2304,256]{1,0:T(8,128)(2,1)S(1)}, u32[]{:S(2)}, u32[]{:S(2)}) collective-permute-start(bf16[2304,256]{1,0:T(8,128)(2,1)S(1)} %constant_dynamic-update-slice_fusion.refs_0_.refs_4_), channel_id=1, source_target_pairs={{0,2},{1,3},{2,4},{3,5},{4,6},{5,7},{6,0},{7,1},{8,10},{9,11},{10,... | collective-permute-start | bytes 3538952 | tf_op jit(solution)/shard_map/ppermute | solution.py:700
  10.5 1.5 %collective-permute-start.3 = (bf16[2304,256]{1,0:T(8,128)(2,1)S(1)}, bf16[2304,256]{1,0:T(8,128)(2,1)S(1)}, u32[]{:S(2)}, u32[]{:S(2)}) collective-permute-start(bf16[2304,256]{1,0:T(8,128)(2,1)S(1)} %constant_dynamic-update-slice_fusion.refs_0_.refs_4_), channel_id=1, source_target_pairs={{0,6},{1,7},{2,0},{3,1},{4,2},{5,3},{6,4},{7,5},{8,14},{9,15},{10,... | collective-permute-start | bytes 3538952 | tf_op jit(solution)/shard_map/ppermute | solution.py:700
  12.0 0.0 collective-permute-done.1.halo_ref
  12.0 0.6 copy-done.7
  12.6 24.4 %local_part.1 = (f32[2048,128]{1,0:T(8,128)}, bf16[2048,256]{1,0:T(8,128)(2,1)}, bf16[2048,256]{1,0:T(8,128)(2,1)}, bf16[2048,256]{1,0:T(8,128)(2,1)}, bf16[2048...) custom-call(bf16[2048,2304]{1,0:T(8,128)(2,1)} %x_ref.3, ...), custom_call_target="tpu_custom_call" | custom-call | flops 14000000000 | bytes 24000000 | tf_op jit(solution)/shard_map/local_part/pallas_call | solution.py:268
  37.0 3.4 %collective-permute-start.5 = (bf16[128,512]{1,0:T(8,128)(2,1)}, bf16[128,512]{1,0:T(8,128)(2,1)S(1)}, u32[]{:S(2)}, u32[]{:S(2)}) collective-permute-start(bf16[128,512]{1,0:T(8,128)(2,1)} %get-tuple-element.46.own), channel_id=1, source_target_pairs={{0,16},{8,24},{16,0},{24,8},{32,48},{40,56},{48,32},{56,40},{64,80... | collective-permute-start | bytes 393224 | tf_op jit(solution)/shard_map/ppermute | solution.py:719
  40.4 0.0 collective-permute-start.4
  40.4 2.7 %collective-permute-start.6 = (bf16[128,512]{1,0:T(8,128)(2,1)}, bf16[128,512]{1,0:T(8,128)(2,1)S(1)}, u32[]{:S(2)}, u32[]{:S(2)}) collective-permute-start(bf16[128,512]{1,0:T(8,128)(2,1)} %get-tuple-element.46.own), channel_id=1, source_target_pairs={{0,24},{8,0},{16,8},{24,16},{32,56},{40,32},{48,40},{56,48},{64,88... | collective-permute-start | bytes 393224 | tf_op jit(solution)/shard_map/ppermute | solution.py:719
  43.1 0.0 collective-permute-done.2.refs_1_.refs_5_
  43.1 0.0 collective-permute-done.3.refs_2_.refs_6_
  43.2 1.7 %collective-permute-start.8 = (bf16[1152,256]{1,0:T(8,128)(2,1)S(1)}, bf16[1152,256]{1,0:T(8,128)(2,1)S(1)}, u32[]{:S(2)}, u32[]{:S(2)}) collective-permute-start(bf16[1152,256]{1,0:T(8,128)(2,1)S(1)} %slice.10), channel_id=1, source_target_pairs={{0,6},{1,7},{2,0},{3,1},{4,2},{5,3},{6,4},{7,5},{8,14},{9,15},{10,... | collective-permute-start | bytes 1769480 | tf_op jit(solution)/shard_map/ppermute | solution.py:700
  44.9 0.1 collective-permute-start.9
  45.0 11.4 %query_part.1 = (bf16[2048,128]{1,0:T(8,128)(2,1)}, bf16[2048,256]{1,0:T(8,128)(2,1)}, bf16[2048,256]{1,0:T(8,128)(2,1)}) custom-call(bf16[2048,2304]{1,0:T(8,128)(2,1)} %x_ref.3, bf16[16,2304]{1,0:T(8,128)(2,1)} %copy-done.7, f32[18,128]{1,0:T(8,128)} %bitcast.14, bf16[3,2304,256]{2,1,0:T(8,128)(2,1)} %w_ref.3, bf16[3,4,256]{2,1,0:T(4,128)(2,1)} %conv_ref.3, ...), custom_call_target="tpu_custom_call" | custom-call | flops 4000000000 | bytes 17000000 | tf_op jit(solution)/shard_map/query_part/pallas_call | solution.py:412
  56.3 0.0 collective-permute-done.5.two
  56.3 0.0 collective-permute-done.4.one
  56.3 0.0 collective-permute-done.6.three
  56.4 0.6 compose.1
  57.0 0.6 copy-done.2
  57.6 1.2 %collective-permute-start.7 = (bf16[128,512]{1,0:T(8,128)(2,1)S(1)}, bf16[128,512]{1,0:T(8,128)(2,1)S(1)}, u32[]{:S(2)}, u32[]{:S(2)}) collective-permute-start(bf16[128,512]{1,0:T(8,128)(2,1)S(1)} %get-tuple-element.53), channel_id=1, source_target_pairs={{0,32},{8,40},{16,48},{24,56},{32,64},{40,72},{48,80},{56,88},{64,... | collective-permute-start | bytes 393224 | tf_op jit(solution)/shard_map/ppermute | solution.py:723
  58.8 2.5 %collective-permute-start.10 = (bf16[128,512]{1,0:T(8,128)(2,1)S(1)}, bf16[128,512]{1,0:T(8,128)(2,1)S(1)}, u32[]{:S(2)}, u32[]{:S(2)}) collective-permute-start(bf16[128,512]{1,0:T(8,128)(2,1)S(1)} %get-tuple-element.53), channel_id=1, source_target_pairs={{0,64},{8,72},{16,80},{24,88},{32,96},{40,104},{48,112},{56,120},{... | collective-permute-start | bytes 393224 | tf_op jit(solution)/shard_map/ppermute | solution.py:723
  61.3 1.1 %collective-permute-start.11 = (bf16[128,512]{1,0:T(8,128)(2,1)S(1)}, bf16[128,512]{1,0:T(8,128)(2,1)S(1)}, u32[]{:S(2)}, u32[]{:S(2)}) collective-permute-start(bf16[128,512]{1,0:T(8,128)(2,1)S(1)} %get-tuple-element.53), channel_id=1, source_target_pairs={{0,96},{8,104},{16,112},{24,120},{32,0},{40,8},{48,16},{56,24},{64... | collective-permute-start | bytes 393224 | tf_op jit(solution)/shard_map/ppermute | solution.py:723
  62.4 5.3 %reading_part.1 = (bf16[2048,256]{1,0:T(8,128)(2,1)}, bf16[2048,256]{1,0:T(8,128)(2,1)}, bf16[2048,256]{1,0:T(8,128)(2,1)}) custom-call(bf16[2048,256]{1,0:T(8,128)(2,1)} %get-tuple-element.58.m_ref, bf16[2048,256]{1,0:T(8,128)(2,1)} %get-tuple-element.59.q_ref, bf16[2048,256]{1,0:T(8,128)(2,1)} %get-tuple-element.60.u_ref, ...), custom_call_target="tpu_custom_call" | custom-call | flops 3000000000 | bytes 12000000 | tf_op jit(solution)/shard_map/reading_part/pallas_call | solution.py:469
  67.7 0.0 collective-permute-done.7.one
  67.7 0.0 collective-permute-done.8.refs_3_
  67.7 0.0 collective-permute-done.9.refs_7_
  67.7 0.0 collective-permute-done.10.two
  67.8 0.0 collective-permute-done.11.three
  67.8 0.6 copy-done.4
  68.4 0.0 copy-done.5
  68.4 0.1 copy-done.6
  68.5 4.6 %gated_part.1 = (bf16[512,256]{1,0:T(8,128)(2,1)}, bf16[512,256]{1,0:T(8,128)(2,1)}, bf16[512,256]{1,0:T(8,128)(2,1)}, bf16[512,256]{1,0:T(8,128)(2,1)}) custom-call(s32[2]{0:T(128)} %pad_add_fusion.1.at_ref, bf16[128,512]{1,0:T(8,128)(2,1)} %copy-done.4, bf16[128,512]{1,0:T(8,128)(2,1)} %copy-done.5, bf16[128,512]{1,0:T(8,128)(2,1)} %copy-done.6, ...), custom_call_target="tpu_custom_call" | custom-call | flops 300000000 | bytes 4000000 | tf_op jit(solution)/shard_map/gated_part/pallas_call | solution.py:563
  73.0 0.1 collective-permute-start.12
  73.1 2.7 %collective-permute-start.13 = (bf16[512,256]{1,0:T(8,128)(2,1)}, bf16[512,256]{1,0:T(8,128)(2,1)S(1)}, u32[]{:S(2)}, u32[]{:S(2)}) collective-permute-start(bf16[512,256]{1,0:T(8,128)(2,1)} %get-tuple-element.69), channel_id=1, source_target_pairs={{0,6},{1,7},{2,0},{3,1},{4,2},{5,3},{6,4},{7,5},{8,14},{9,15},{10,... | collective-permute-start | bytes 786440 | tf_op jit(solution)/shard_map/ppermute | solution.py:700
  75.8 1.1 collective-permute-start.14
  76.9 3.6 %collective-permute-start.15 = (bf16[512,256]{1,0:T(8,128)(2,1)}, bf16[512,256]{1,0:T(8,128)(2,1)S(1)}, u32[]{:S(2)}, u32[]{:S(2)}) collective-permute-start(bf16[512,256]{1,0:T(8,128)(2,1)} %get-tuple-element.67.refs_8_), channel_id=1, source_target_pairs={{0,1},{1,0},{2,3},{3,2},{4,5},{5,4},{6,7},{7,6},{8,9},{9,8},{10,11... | collective-permute-start | bytes 786440 | tf_op jit(solution)/shard_map/ppermute | solution.py:703
  80.5 0.0 collective-permute-done.12.refs_9_
  80.5 6.0 %collective-permute-start.16 = (bf16[512,256]{1,0:T(8,128)(2,1)S(1)}, bf16[512,256]{1,0:T(8,128)(2,1)S(1)}, u32[]{:S(2)}, u32[]{:S(2)}) collective-permute-start(bf16[512,256]{1,0:T(8,128)(2,1)S(1)} %collective-permute-done.12.refs_9_), channel_id=1, source_target_pairs={{0,1},{1,0},{2,3},{3,2},{4,5},{5,4},{6,7},{7,6},{8,9},{9,8},{10,11... | collective-permute-start | bytes 786440 | tf_op jit(solution)/shard_map/ppermute | solution.py:703
  86.5 0.0 collective-permute-done.13.refs_10_
  86.5 1.8 %collective-permute-start.17 = (bf16[512,256]{1,0:T(8,128)(2,1)S(1)}, bf16[512,256]{1,0:T(8,128)(2,1)S(1)}, u32[]{:S(2)}, u32[]{:S(2)}) collective-permute-start(bf16[512,256]{1,0:T(8,128)(2,1)S(1)} %collective-permute-done.13.refs_10_), channel_id=1, source_target_pairs={{0,1},{1,0},{2,3},{3,2},{4,5},{5,4},{6,7},{7,6},{8,9},{9,8},{10,11... | collective-permute-start | bytes 786440 | tf_op jit(solution)/shard_map/ppermute | solution.py:703
  88.3 0.0 collective-permute-done.14.refs_11_
  88.3 1.7 %collective-permute-start.18 = (bf16[512,256]{1,0:T(8,128)(2,1)S(1)}, bf16[512,256]{1,0:T(8,128)(2,1)S(1)}, u32[]{:S(2)}, u32[]{:S(2)}) collective-permute-start(bf16[512,256]{1,0:T(8,128)(2,1)S(1)} %collective-permute-done.14.refs_11_), channel_id=1, source_target_pairs={{0,1},{1,0},{2,3},{3,2},{4,5},{5,4},{6,7},{7,6},{8,9},{9,8},{10,11... | collective-permute-start | bytes 786440 | tf_op jit(solution)/shard_map/ppermute | solution.py:703
  90.0 0.0 collective-permute-done.15.refs_12_
  90.0 0.0 collective-permute-done.16.refs_13_
  90.0 0.0 collective-permute-done.17.refs_14_
  90.0 1.1 %collective-permute-done.18.refs_15_ = bf16[512,256]{1,0:T(8,128)(2,1)S(1)} collective-permute-done((bf16[512,256]{1,0:T(8,128)(2,1)S(1)}, bf16[512,256]{1,0:T(8,128)(2,1)S(1)}, u32[]{:S(2)}, u32[]{:S(2)}) %collective-permute-start.18) | collective-permute-done | bytes 262176 | tf_op jit(solution)/shard_map/ppermute | solution.py:703
  91.2 0.9 copy-done
  92.1 1.3 %mixed_part.3 = bf16[288,512]{1,0:T(8,128)(2,1)S(1)} custom-call(s32[2]{0:T(128)S(1)} %pad_add_fusion.at_ref, bf16[2304,256]{1,0:T(8,128)(2,1)S(1)} %constant_dynamic-update-slice_fusion.refs_0_.refs_4_, bf16[2304,256]{1,0:T(8,128)(2,1)S(1)} %collective-permute-done.2.refs_1_.refs_5_, bf16[2304,256]{1,0:T(8,128)(2,1)S(1)} %collective-permute-done.3.refs_2_.refs_6_, ...), custom_call_target="tpu_custom_call" | custom-call | flops 600000000 | bytes 3500000 | tf_op jit(solution)/shard_map/mixed_part/pallas_call | solution.py:638
  93.5 0.8 collective-permute-start.19
  94.3 2.2 %mixed_part.5 = (bf16[288,512]{1,0:T(8,128)(2,1)S(1)}, bf16[288,512]{1,0:T(8,128)(2,1)S(1)}) custom-call(s32[2]{0:T(128)S(1)} %pad_add_fusion.at_ref, bf16[2304,256]{1,0:T(8,128)(2,1)S(1)} %constant_dynamic-update-slice_fusion.refs_0_.refs_4_, bf16[2304,256]{1,0:T(8,128)(2,1)S(1)} %collective-permute-done.2.refs_1_.refs_5_, ...), custom_call_target="tpu_custom_call" | custom-call | flops 1200000000 | bytes 5000000 | tf_op jit(solution)/shard_map/mixed_part/pallas_call | solution.py:638
  96.5 1.9 %collective-permute-start.20 = (bf16[288,512]{1,0:T(8,128)(2,1)S(1)}, bf16[288,512]{1,0:T(8,128)(2,1)S(1)}, u32[]{:S(2)}, u32[]{:S(2)}) collective-permute-start(bf16[288,512]{1,0:T(8,128)(2,1)S(1)} %get-tuple-element.74), channel_id=1, source_target_pairs={{0,2},{1,3},{2,4},{3,5},{4,6},{5,7},{6,0},{7,1},{8,10},{9,11},{10,... | collective-permute-start | bytes 884744 | tf_op jit(solution)/shard_map/ppermute | solution.py:700
  98.4 0.9 collective-permute-start.21
  99.3 4.1 %collective-permute-done.19.refs_2_ = bf16[288,512]{1,0:T(8,128)(2,1)S(1)} collective-permute-done((bf16[288,512]{1,0:T(8,128)(2,1)S(1)}, bf16[288,512]{1,0:T(8,128)(2,1)S(1)}, u32[]{:S(2)}, u32[]{:S(2)}) %collective-permute-start.19) | collective-permute-done | bytes 294944 | tf_op jit(solution)/shard_map/ppermute | solution.py:700
  103.3 1.3 %mixed_part.4.refs_0_ = bf16[288,512]{1,0:T(8,128)(2,1)S(1)} custom-call(s32[2]{0:T(128)S(1)} %pad_add_fusion.at_ref, bf16[2304,256]{1,0:T(8,128)(2,1)S(1)} %constant_dynamic-update-slice_fusion.refs_0_.refs_4_, bf16[2304,256]{1,0:T(8,128)(2,1)S(1)} %collective-permute-done.2.refs_1_.refs_5_, bf16[2304,256]{1,0:T(8,128)(2,1)S(1)} %collective-permute-done.3.refs_2_.refs_6_, ...), custom_call_target="tpu_custom_call" | custom-call | flops 600000000 | bytes 3500000 | tf_op jit(solution)/shard_map/mixed_part/pallas_call | solution.py:638
  104.7 5.6 %collective-permute-done.20.refs_1_ = bf16[288,512]{1,0:T(8,128)(2,1)S(1)} collective-permute-done((bf16[288,512]{1,0:T(8,128)(2,1)S(1)}, bf16[288,512]{1,0:T(8,128)(2,1)S(1)}, u32[]{:S(2)}, u32[]{:S(2)}) %collective-permute-start.20) | collective-permute-done | bytes 294944 | tf_op jit(solution)/shard_map/ppermute | solution.py:700
  110.3 0.0 collective-permute-done.21.refs_3_
  110.3 1.1 joined.1
  (13 shorter events, 0.2 us)
Async XLA Ops:
  0.1 1.3 %copy-start.1 = (bf16[256,2304]{1,0:T(8,128)(2,1)S(1)}, bf16[256,2304]{1,0:T(8,128)(2,1)}, u32[]{:S(2)}) copy-start(bf16[256,2304]{1,0:T(8,128)(2,1)} %w_ref.2) | copy-start | bytes 3538948
  2.3 6.7 %collective-permute-start = (bf16[1152,256]{1,0:T(8,128)(2,1)S(1)}, bf16[1152,256]{1,0:T(8,128)(2,1)S(1)}, u32[]{:S(2)}, u32[]{:S(2)}) collective-permute-start(bf16[1152,256]{1,0:T(8,128)(2,1)S(1)} %get-tuple-element.42), channel_id=1, source_target_pairs={{0,1},{1,0},{2,3},{3,2},{4,5},{5,4},{6,7},{7,6},{8,9},{9,8},{10,11... | collective-permute-start | bytes 1769480 | tf_op jit(solution)/shard_map/ppermute | solution.py:703
  4.7 7.3 %collective-permute-start.1 = (bf16[16,2304]{1,0:T(8,128)(2,1)S(1)}, bf16[16,2304]{1,0:T(8,128)(2,1)S(1)}, u32[]{:S(2)}, u32[]{:S(2)}) collective-permute-start(bf16[16,2304]{1,0:T(8,128)(2,1)S(1)} %slice.9), channel_id=1, source_target_pairs={{0,8},{8,16},{16,24},{24,32},{32,40},{40,48},{48,56},{56,64},{64,7... | collective-permute-start | bytes 221192 | tf_op jit(solution)/shard_map/ppermute | solution.py:707
  9.1 34.0 %collective-permute-start.2 = (bf16[2304,256]{1,0:T(8,128)(2,1)S(1)}, bf16[2304,256]{1,0:T(8,128)(2,1)S(1)}, u32[]{:S(2)}, u32[]{:S(2)}) collective-permute-start(bf16[2304,256]{1,0:T(8,128)(2,1)S(1)} %constant_dynamic-update-slice_fusion.refs_0_.refs_4_), channel_id=1, source_target_pairs={{0,2},{1,3},{2,4},{3,5},{4,6},{5,7},{6,0},{7,1},{8,10},{9,11},{10,... | collective-permute-start | bytes 3538952 | tf_op jit(solution)/shard_map/ppermute | solution.py:700
  10.5 32.6 %collective-permute-start.3 = (bf16[2304,256]{1,0:T(8,128)(2,1)S(1)}, bf16[2304,256]{1,0:T(8,128)(2,1)S(1)}, u32[]{:S(2)}, u32[]{:S(2)}) collective-permute-start(bf16[2304,256]{1,0:T(8,128)(2,1)S(1)} %constant_dynamic-update-slice_fusion.refs_0_.refs_4_), channel_id=1, source_target_pairs={{0,6},{1,7},{2,0},{3,1},{4,2},{5,3},{6,4},{7,5},{8,14},{9,15},{10,... | collective-permute-start | bytes 3538952 | tf_op jit(solution)/shard_map/ppermute | solution.py:700
  12.0 0.6 copy-start.7
  37.0 19.3 %collective-permute-start.5 = (bf16[128,512]{1,0:T(8,128)(2,1)}, bf16[128,512]{1,0:T(8,128)(2,1)S(1)}, u32[]{:S(2)}, u32[]{:S(2)}) collective-permute-start(bf16[128,512]{1,0:T(8,128)(2,1)} %get-tuple-element.46.own), channel_id=1, source_target_pairs={{0,16},{8,24},{16,0},{24,8},{32,48},{40,56},{48,32},{56,40},{64,80... | collective-permute-start | bytes 393224 | tf_op jit(solution)/shard_map/ppermute | solution.py:719
  40.4 15.9 %collective-permute-start.4 = (bf16[128,512]{1,0:T(8,128)(2,1)}, bf16[128,512]{1,0:T(8,128)(2,1)S(1)}, u32[]{:S(2)}, u32[]{:S(2)}) collective-permute-start(bf16[128,512]{1,0:T(8,128)(2,1)} %get-tuple-element.46.own), channel_id=1, source_target_pairs={{0,8},{8,16},{16,24},{24,0},{32,40},{40,48},{48,56},{56,32},{64,72... | collective-permute-start | bytes 393224 | tf_op jit(solution)/shard_map/ppermute | solution.py:719
  40.4 15.9 %collective-permute-start.6 = (bf16[128,512]{1,0:T(8,128)(2,1)}, bf16[128,512]{1,0:T(8,128)(2,1)S(1)}, u32[]{:S(2)}, u32[]{:S(2)}) collective-permute-start(bf16[128,512]{1,0:T(8,128)(2,1)} %get-tuple-element.46.own), channel_id=1, source_target_pairs={{0,24},{8,0},{16,8},{24,16},{32,56},{40,32},{48,40},{56,48},{64,88... | collective-permute-start | bytes 393224 | tf_op jit(solution)/shard_map/ppermute | solution.py:719
  43.2 24.6 %collective-permute-start.8 = (bf16[1152,256]{1,0:T(8,128)(2,1)S(1)}, bf16[1152,256]{1,0:T(8,128)(2,1)S(1)}, u32[]{:S(2)}, u32[]{:S(2)}) collective-permute-start(bf16[1152,256]{1,0:T(8,128)(2,1)S(1)} %slice.10), channel_id=1, source_target_pairs={{0,6},{1,7},{2,0},{3,1},{4,2},{5,3},{6,4},{7,5},{8,14},{9,15},{10,... | collective-permute-start | bytes 1769480 | tf_op jit(solution)/shard_map/ppermute | solution.py:700
  44.9 22.9 %collective-permute-start.9 = (bf16[1152,256]{1,0:T(8,128)(2,1)S(1)}, bf16[1152,256]{1,0:T(8,128)(2,1)S(1)}, u32[]{:S(2)}, u32[]{:S(2)}) collective-permute-start(bf16[1152,256]{1,0:T(8,128)(2,1)S(1)} %slice.11), channel_id=1, source_target_pairs={{0,2},{1,3},{2,4},{3,5},{4,6},{5,7},{6,0},{7,1},{8,10},{9,11},{10,... | collective-permute-start | bytes 1769480 | tf_op jit(solution)/shard_map/ppermute | solution.py:700
  45.0 11.4 %copy-start.3 = (bf16[128,512]{1,0:T(8,128)(2,1)S(1)}, bf16[128,512]{1,0:T(8,128)(2,1)}, u32[]{:S(2)}) copy-start(bf16[128,512]{1,0:T(8,128)(2,1)} %get-tuple-element.46.own) | copy-start | bytes 393220
  57.0 0.7 copy-start.2
  57.6 10.1 %collective-permute-start.7 = (bf16[128,512]{1,0:T(8,128)(2,1)S(1)}, bf16[128,512]{1,0:T(8,128)(2,1)S(1)}, u32[]{:S(2)}, u32[]{:S(2)}) collective-permute-start(bf16[128,512]{1,0:T(8,128)(2,1)S(1)} %get-tuple-element.53), channel_id=1, source_target_pairs={{0,32},{8,40},{16,48},{24,56},{32,64},{40,72},{48,80},{56,88},{64,... | collective-permute-start | bytes 393224 | tf_op jit(solution)/shard_map/ppermute | solution.py:723
  58.8 8.9 %collective-permute-start.10 = (bf16[128,512]{1,0:T(8,128)(2,1)S(1)}, bf16[128,512]{1,0:T(8,128)(2,1)S(1)}, u32[]{:S(2)}, u32[]{:S(2)}) collective-permute-start(bf16[128,512]{1,0:T(8,128)(2,1)S(1)} %get-tuple-element.53), channel_id=1, source_target_pairs={{0,64},{8,72},{16,80},{24,88},{32,96},{40,104},{48,112},{56,120},{... | collective-permute-start | bytes 393224 | tf_op jit(solution)/shard_map/ppermute | solution.py:723
  61.3 6.5 %collective-permute-start.11 = (bf16[128,512]{1,0:T(8,128)(2,1)S(1)}, bf16[128,512]{1,0:T(8,128)(2,1)S(1)}, u32[]{:S(2)}, u32[]{:S(2)}) collective-permute-start(bf16[128,512]{1,0:T(8,128)(2,1)S(1)} %get-tuple-element.53), channel_id=1, source_target_pairs={{0,96},{8,104},{16,112},{24,120},{32,0},{40,8},{48,16},{56,24},{64... | collective-permute-start | bytes 393224 | tf_op jit(solution)/shard_map/ppermute | solution.py:723
  67.7 0.7 copy-start.4
  67.7 0.7 copy-start.5
  67.8 0.7 copy-start.6
  73.0 7.5 %collective-permute-start.12 = (bf16[512,256]{1,0:T(8,128)(2,1)}, bf16[512,256]{1,0:T(8,128)(2,1)S(1)}, u32[]{:S(2)}, u32[]{:S(2)}) collective-permute-start(bf16[512,256]{1,0:T(8,128)(2,1)} %get-tuple-element.68), channel_id=1, source_target_pairs={{0,2},{1,3},{2,4},{3,5},{4,6},{5,7},{6,0},{7,1},{8,10},{9,11},{10,... | collective-permute-start | bytes 786440 | tf_op jit(solution)/shard_map/ppermute | solution.py:700
  73.1 13.4 %collective-permute-start.13 = (bf16[512,256]{1,0:T(8,128)(2,1)}, bf16[512,256]{1,0:T(8,128)(2,1)S(1)}, u32[]{:S(2)}, u32[]{:S(2)}) collective-permute-start(bf16[512,256]{1,0:T(8,128)(2,1)} %get-tuple-element.69), channel_id=1, source_target_pairs={{0,6},{1,7},{2,0},{3,1},{4,2},{5,3},{6,4},{7,5},{8,14},{9,15},{10,... | collective-permute-start | bytes 786440 | tf_op jit(solution)/shard_map/ppermute | solution.py:700
  75.8 12.5 %collective-permute-start.14 = (bf16[512,256]{1,0:T(8,128)(2,1)}, bf16[512,256]{1,0:T(8,128)(2,1)S(1)}, u32[]{:S(2)}, u32[]{:S(2)}) collective-permute-start(bf16[512,256]{1,0:T(8,128)(2,1)} %get-tuple-element.70), channel_id=1, source_target_pairs={{0,4},{1,5},{2,6},{3,7},{4,0},{5,1},{6,2},{7,3},{8,12},{9,13},{10,... | collective-permute-start | bytes 786440 | tf_op jit(solution)/shard_map/ppermute | solution.py:700
  76.9 13.1 %collective-permute-start.15 = (bf16[512,256]{1,0:T(8,128)(2,1)}, bf16[512,256]{1,0:T(8,128)(2,1)S(1)}, u32[]{:S(2)}, u32[]{:S(2)}) collective-permute-start(bf16[512,256]{1,0:T(8,128)(2,1)} %get-tuple-element.67.refs_8_), channel_id=1, source_target_pairs={{0,1},{1,0},{2,3},{3,2},{4,5},{5,4},{6,7},{7,6},{8,9},{9,8},{10,11... | collective-permute-start | bytes 786440 | tf_op jit(solution)/shard_map/ppermute | solution.py:703
  80.5 9.5 %collective-permute-start.16 = (bf16[512,256]{1,0:T(8,128)(2,1)S(1)}, bf16[512,256]{1,0:T(8,128)(2,1)S(1)}, u32[]{:S(2)}, u32[]{:S(2)}) collective-permute-start(bf16[512,256]{1,0:T(8,128)(2,1)S(1)} %collective-permute-done.12.refs_9_), channel_id=1, source_target_pairs={{0,1},{1,0},{2,3},{3,2},{4,5},{5,4},{6,7},{7,6},{8,9},{9,8},{10,11... | collective-permute-start | bytes 786440 | tf_op jit(solution)/shard_map/ppermute | solution.py:703
  86.5 3.5 %collective-permute-start.17 = (bf16[512,256]{1,0:T(8,128)(2,1)S(1)}, bf16[512,256]{1,0:T(8,128)(2,1)S(1)}, u32[]{:S(2)}, u32[]{:S(2)}) collective-permute-start(bf16[512,256]{1,0:T(8,128)(2,1)S(1)} %collective-permute-done.13.refs_10_), channel_id=1, source_target_pairs={{0,1},{1,0},{2,3},{3,2},{4,5},{5,4},{6,7},{7,6},{8,9},{9,8},{10,11... | collective-permute-start | bytes 786440 | tf_op jit(solution)/shard_map/ppermute | solution.py:703
  88.3 2.9 %collective-permute-start.18 = (bf16[512,256]{1,0:T(8,128)(2,1)S(1)}, bf16[512,256]{1,0:T(8,128)(2,1)S(1)}, u32[]{:S(2)}, u32[]{:S(2)}) collective-permute-start(bf16[512,256]{1,0:T(8,128)(2,1)S(1)} %collective-permute-done.14.refs_11_), channel_id=1, source_target_pairs={{0,1},{1,0},{2,3},{3,2},{4,5},{5,4},{6,7},{7,6},{8,9},{9,8},{10,11... | collective-permute-start | bytes 786440 | tf_op jit(solution)/shard_map/ppermute | solution.py:703
  91.2 0.9 copy-start
  93.5 9.8 %collective-permute-start.19 = (bf16[288,512]{1,0:T(8,128)(2,1)S(1)}, bf16[288,512]{1,0:T(8,128)(2,1)S(1)}, u32[]{:S(2)}, u32[]{:S(2)}) collective-permute-start(bf16[288,512]{1,0:T(8,128)(2,1)S(1)} %mixed_part.3), channel_id=1, source_target_pairs={{0,4},{1,5},{2,6},{3,7},{4,0},{5,1},{6,2},{7,3},{8,12},{9,13},{10,... | collective-permute-start | bytes 884744 | tf_op jit(solution)/shard_map/ppermute | solution.py:700
  96.5 13.8 %collective-permute-start.20 = (bf16[288,512]{1,0:T(8,128)(2,1)S(1)}, bf16[288,512]{1,0:T(8,128)(2,1)S(1)}, u32[]{:S(2)}, u32[]{:S(2)}) collective-permute-start(bf16[288,512]{1,0:T(8,128)(2,1)S(1)} %get-tuple-element.74), channel_id=1, source_target_pairs={{0,2},{1,3},{2,4},{3,5},{4,6},{5,7},{6,0},{7,1},{8,10},{9,11},{10,... | collective-permute-start | bytes 884744 | tf_op jit(solution)/shard_map/ppermute | solution.py:700
  98.4 11.9 %collective-permute-start.21 = (bf16[288,512]{1,0:T(8,128)(2,1)S(1)}, bf16[288,512]{1,0:T(8,128)(2,1)S(1)}, u32[]{:S(2)}, u32[]{:S(2)}) collective-permute-start(bf16[288,512]{1,0:T(8,128)(2,1)S(1)} %get-tuple-element.76), channel_id=1, source_target_pairs={{0,6},{1,7},{2,0},{3,1},{4,2},{5,3},{6,4},{7,5},{8,14},{9,15},{10,... | collective-permute-start | bytes 884744 | tf_op jit(solution)/shard_map/ppermute | solution.py:700
